TPU v7x, 32 devices: a whole 2x2x4 slice. The times are simulated.
32 devices in a mesh: grp: 2 (over core), fsdp: 16 (over z, y, x).
Axes of the slice: x: 2, y: 2, z: 4, core: 2. Of those that a mesh axis runs over, the one named last changes fastest.
Arguments:
- features: bfloat16 [12288, 128], P(('grp', 'fsdp')), may hold values from -6 to 6
- adjacency: int32 [96, 128, 128], P(('grp', 'fsdp')), may hold values from 0 to 1, as said below
- counts: int32 [96], P(('grp', 'fsdp')), may hold values from 64 to 128, as said below
- input_weight: bfloat16 [128, 512], P('fsdp'), may hold values from -0.5 to 0.5
- first_gain: bfloat16 [512], P('fsdp'), may hold values from 0.5 to 1.5
- first_shift: bfloat16 [512], P('fsdp'), may hold values from -1.75 to 1.75
- attend_weight: bfloat16 [512, 1536], P('fsdp'), may hold values from -0.25 to 0.25
- merge_weight: bfloat16 [512, 512], P('fsdp'), may hold values from -0.75 to 0.75
- second_gain: bfloat16 [512], P('fsdp'), may hold values from 0.5 to 1.5
- second_shift: bfloat16 [512], P('fsdp'), may hold values from -1.75 to 1.75
- expand_weight: bfloat16 [512, 1024], P('fsdp'), may hold values from -0.25 to 0.25
- reduce_weight: bfloat16 [1024, 512], P('fsdp'), may hold values from -0.1875 to 0.1875
- readout_weight: bfloat16 [1024], P('fsdp'), may hold values from -0.25 to 0.25
- cotangent: float32 [12288, 512], P(('grp', 'fsdp')), may hold values from -6 to 6
Outputs:
- node_output: float32 [12288, 512], P(('grp', 'fsdp'))
- grad_features: float32 [12288, 128], P(('grp', 'fsdp'))
- grad_input_weight: float32 [128, 512], P('fsdp')
- grad_first_gain: float32 [512], P('fsdp')
- grad_first_shift: float32 [512], P('fsdp')
- grad_attend: float32 [512, 1536], P('fsdp')
- grad_merge: float32 [512, 512], P('fsdp')
- grad_second_gain: float32 [512], P('fsdp')
- grad_second_shift: float32 [512], P('fsdp')
- grad_expand: float32 [512, 1024], P('fsdp')
- grad_reduce: float32 [1024, 512], P('fsdp')
- grad_readout: float32 [1024], P('fsdp')
Inputs may be any that keep to these rules, and one draw needn't show every extreme that they name: `counts`: the live nodes of a cluster fill its first slots; the other slots of its 128 are empty. `adjacency`: symmetric within each cluster, with a zero diagonal; links of empty slots are ignored.
All inputs are finite; a program needn't handle non-finite values.
Results may differ from a plain program's by a relative error of at most 0.012.
The roundings to bfloat16 on the way count: a program that leaves them out, or rounds other values in their place, can miss the bound.
Values may be sent and summed in bfloat16 or wider, within the bound.
A program may use at most 192 MiB of HBM per device.

v0:
```python
import jax
import jax.numpy as jnp
from jax import lax
from jax.sharding import PartitionSpec as P

HEADS = 8
HEAD = 64
HOPS = 7


highest = lax.Precision.HIGHEST


def norm_rows(values_in, gain_row, shift_row):
    row_mean = jnp.mean(values_in, axis=-1, keepdims=True)
    centred = values_in - row_mean
    row_var = jnp.mean(centred * centred, axis=-1, keepdims=True)
    return centred * lax.rsqrt(row_var + 1e-05) * gain_row + shift_row


def contract_lead(left, right):
    return lax.dot_general(
        left, right, (((0,), (0,)), ((), ())), preferred_element_type=jnp.float32
    )


def contract_last(left, right):
    return lax.dot_general(
        left, right, (((1,), (1,)), ((), ())), preferred_element_type=jnp.float32
    )


def attention_parts(hidden, gain_row, shift_row, attend_full, node_count):
    model_width = hidden.shape[1]
    normed = norm_rows(hidden, gain_row.astype(jnp.float32), shift_row.astype(jnp.float32)).astype(
        jnp.bfloat16
    )
    triple = jnp.dot(normed, attend_full, preferred_element_type=jnp.float32).astype(jnp.bfloat16)
    shaped = triple.reshape(node_count, HOPS + 1, 3, HEADS, model_width // HEADS)
    query_heads = shaped[:, :, 0]
    key_heads = shaped[:, :, 1]
    value_heads = shaped[:, :, 2]
    scores = jnp.einsum(
        "nihd,njhd->nhij", query_heads, key_heads, preferred_element_type=jnp.float32
    ) * HEAD ** (-0.5)
    prob_rows = jax.nn.softmax(scores, axis=-1)
    rounded = prob_rows.astype(jnp.bfloat16)
    mixed_heads = jnp.einsum(
        "nhij,njhd->nihd", rounded, value_heads, preferred_element_type=jnp.float32
    )
    mixed_heads = mixed_heads.reshape(node_count * (HOPS + 1), model_width).astype(jnp.bfloat16)
    return (normed, query_heads, key_heads, value_heads, prob_rows, rounded, mixed_heads)


def expand_parts(second, gain_row, shift_row, expand_full):
    inner = norm_rows(second, gain_row.astype(jnp.float32), shift_row.astype(jnp.float32)).astype(
        jnp.bfloat16
    )
    before = jnp.dot(inner, expand_full, preferred_element_type=jnp.float32)
    after = jax.nn.gelu(before).astype(jnp.bfloat16)
    return (inner, before, after)


def body(
    features,
    adjacency,
    counts,
    input_weight,
    first_gain,
    first_shift,
    attend_weight,
    merge_weight,
    second_gain,
    second_shift,
    expand_weight,
    reduce_weight,
    readout_weight,
    cotangent,
):
    clusters = adjacency.shape[0]
    slot_count = adjacency.shape[1]
    node_count = features.shape[0]
    feat_width = features.shape[1]
    token_count = HOPS + 1
    slot_index = jnp.arange(slot_count, dtype=jnp.int32)
    valid_mask = (slot_index[None, :] < counts[:, None]).astype(jnp.float32)
    link_matrix = adjacency.astype(jnp.float32) * valid_mask[:, :, None] * valid_mask[:, None, :]
    link_matrix = link_matrix + jnp.eye(slot_count, dtype=jnp.float32)
    root_scale = lax.rsqrt(jnp.sum(link_matrix, axis=-1))
    operator = link_matrix * root_scale[:, :, None] * root_scale[:, None, :]
    keep_mask = valid_mask.reshape(node_count, 1)
    hop_state = (
        features.astype(jnp.float32).reshape(clusters, slot_count, feat_width)
        * valid_mask[:, :, None]
    )
    hop_list = [hop_state]
    for hop_step in range(HOPS):
        hop_state = jnp.einsum("cij,cjf->cif", operator, hop_state, precision=highest)
        hop_list.append(hop_state)
    stacked = (
        jnp.stack(hop_list, axis=2)
        .reshape(node_count * token_count, feat_width)
        .astype(jnp.bfloat16)
    )
    first_set = (
        lax.all_gather(input_weight, "fsdp", axis=0, tiled=True),
        lax.all_gather(first_gain, "fsdp", axis=0, tiled=True),
        lax.all_gather(first_shift, "fsdp", axis=0, tiled=True),
        lax.all_gather(attend_weight, "fsdp", axis=0, tiled=True),
        lax.all_gather(merge_weight, "fsdp", axis=0, tiled=True),
    )
    embed_full, gain_one, shift_one, attend_full, merge_full = first_set
    hidden = jnp.dot(stacked, embed_full, preferred_element_type=jnp.float32)
    model_width = hidden.shape[1]
    mixed_heads = attention_parts(hidden, gain_one, shift_one, attend_full, node_count)[6]
    second = hidden + jnp.dot(mixed_heads, merge_full, preferred_element_type=jnp.float32)
    second_set = (
        lax.all_gather(second_gain, "fsdp", axis=0, tiled=True),
        lax.all_gather(second_shift, "fsdp", axis=0, tiled=True),
        lax.all_gather(expand_weight, "fsdp", axis=0, tiled=True),
        lax.all_gather(reduce_weight, "fsdp", axis=0, tiled=True),
        lax.all_gather(readout_weight, "fsdp", axis=0, tiled=True),
    )
    gain_two, shift_two, expand_full, reduce_full, readout_full = second_set
    after = expand_parts(second, gain_two, shift_two, expand_full)[2]
    third_sum = second + jnp.dot(after, reduce_full, preferred_element_type=jnp.float32)

    def read_nodes(third_in, readout):
        shaped = third_in.reshape(node_count, token_count, model_width)
        centre = shaped[:, 0]
        others = shaped[:, 1:]
        logits = jnp.dot(centre, readout[:model_width], precision=highest)[:, None]
        logits = logits + jnp.einsum("nkd,d->nk", others, readout[model_width:], precision=highest)
        hop_weights = jax.nn.softmax(logits, axis=-1)
        return (
            centre + jnp.einsum("nk,nkd->nd", hop_weights, others, precision=highest)
        ) * keep_mask

    node_output, read_pull = jax.vjp(read_nodes, third_sum, readout_full.astype(jnp.float32))
    grad_third, grad_readout = read_pull(cotangent)
    late_set = (
        lax.all_gather(second_gain, "fsdp", axis=0, tiled=True),
        lax.all_gather(second_shift, "fsdp", axis=0, tiled=True),
        lax.all_gather(expand_weight, "fsdp", axis=0, tiled=True),
        lax.all_gather(reduce_weight, "fsdp", axis=0, tiled=True),
    )
    gain_late, shift_late, expand_late, reduce_late = late_set
    inner, before, after = expand_parts(second, gain_late, shift_late, expand_late)
    grad_branch = grad_third.astype(jnp.bfloat16)
    grad_reduce = contract_lead(after, grad_branch)
    grad_after = contract_last(grad_branch, reduce_late)
    grad_before = jax.vjp(jax.nn.gelu, before)[1](grad_after)[0].astype(jnp.bfloat16)
    grad_expand = contract_lead(inner, grad_before)
    grad_inner = contract_last(grad_before, expand_late)
    norm_pull = jax.vjp(
        norm_rows, second, gain_late.astype(jnp.float32), shift_late.astype(jnp.float32)
    )[1]
    grad_second_ln, grad_second_gain, grad_second_shift = norm_pull(grad_inner)
    grad_second = grad_third + grad_second_ln
    early_set = (
        lax.all_gather(input_weight, "fsdp", axis=0, tiled=True),
        lax.all_gather(first_gain, "fsdp", axis=0, tiled=True),
        lax.all_gather(first_shift, "fsdp", axis=0, tiled=True),
        lax.all_gather(attend_weight, "fsdp", axis=0, tiled=True),
        lax.all_gather(merge_weight, "fsdp", axis=0, tiled=True),
    )
    embed_late, gain_early, shift_early, attend_late, merge_late = early_set
    normed, query_heads, key_heads, value_heads, prob_rows, rounded, mixed_heads = attention_parts(
        hidden, gain_early, shift_early, attend_late, node_count
    )
    grad_attn = grad_second.astype(jnp.bfloat16)
    grad_merge = contract_lead(mixed_heads, grad_attn)
    grad_mixed = contract_last(grad_attn, merge_late).astype(jnp.bfloat16)
    grad_mixed = grad_mixed.reshape(node_count, token_count, HEADS, model_width // HEADS)
    grad_probs = jnp.einsum(
        "nihd,njhd->nhij", grad_mixed, value_heads, preferred_element_type=jnp.float32
    )
    grad_scores = (
        prob_rows * (grad_probs - jnp.sum(prob_rows * grad_probs, axis=-1, keepdims=True))
    ).astype(jnp.bfloat16)
    grad_values = jnp.einsum(
        "nhij,nihd->njhd", rounded, grad_mixed, preferred_element_type=jnp.float32
    )
    grad_query = jnp.einsum(
        "nhij,njhd->nihd", grad_scores, key_heads, preferred_element_type=jnp.float32
    ) * HEAD ** (-0.5)
    grad_keys = jnp.einsum(
        "nhij,nihd->njhd", grad_scores, query_heads, preferred_element_type=jnp.float32
    ) * HEAD ** (-0.5)
    grad_triple = jnp.stack((grad_query, grad_keys, grad_values), axis=2)
    grad_triple = grad_triple.reshape(node_count * token_count, 3 * model_width).astype(
        jnp.bfloat16
    )
    grad_attend = contract_lead(normed, grad_triple)
    grad_normed = contract_last(grad_triple, attend_late)
    first_pull = jax.vjp(
        norm_rows, hidden, gain_early.astype(jnp.float32), shift_early.astype(jnp.float32)
    )[1]
    grad_hidden_ln, grad_first_gain, grad_first_shift = first_pull(grad_normed)
    grad_hidden = (grad_second + grad_hidden_ln).astype(jnp.bfloat16)
    grad_input_weight = contract_lead(stacked, grad_hidden)
    grad_stacked = contract_last(grad_hidden, embed_late).reshape(
        clusters, slot_count, token_count, feat_width
    )
    back_carry = grad_stacked[:, :, HOPS]
    for hop_step in range(HOPS - 1, -1, -1):
        back_carry = grad_stacked[:, :, hop_step] + jnp.einsum(
            "cji,cjf->cif", operator, back_carry, precision=highest
        )
    grad_features = (back_carry * valid_mask[:, :, None]).reshape(node_count, feat_width)
    grad_terms = (
        grad_input_weight,
        grad_first_gain,
        grad_first_shift,
        grad_attend,
        grad_merge,
        grad_second_gain,
        grad_second_shift,
        grad_expand,
        grad_reduce,
        grad_readout,
    )
    summed = (
        lax.psum(grad_terms[0].astype(jnp.bfloat16), "grp").astype(jnp.float32),
        lax.psum(grad_terms[1].astype(jnp.bfloat16), "grp").astype(jnp.float32),
        lax.psum(grad_terms[2].astype(jnp.bfloat16), "grp").astype(jnp.float32),
        lax.psum(grad_terms[3].astype(jnp.bfloat16), "grp").astype(jnp.float32),
        lax.psum(grad_terms[4].astype(jnp.bfloat16), "grp").astype(jnp.float32),
        lax.psum(grad_terms[5].astype(jnp.bfloat16), "grp").astype(jnp.float32),
        lax.psum(grad_terms[6].astype(jnp.bfloat16), "grp").astype(jnp.float32),
        lax.psum(grad_terms[7].astype(jnp.bfloat16), "grp").astype(jnp.float32),
        lax.psum(grad_terms[8].astype(jnp.bfloat16), "grp").astype(jnp.float32),
        lax.psum(grad_terms[9].astype(jnp.bfloat16), "grp").astype(jnp.float32),
    )
    shares = (
        lax.psum_scatter(summed[0], "fsdp", scatter_dimension=0, tiled=True),
        lax.psum_scatter(summed[1], "fsdp", scatter_dimension=0, tiled=True),
        lax.psum_scatter(summed[2], "fsdp", scatter_dimension=0, tiled=True),
        lax.psum_scatter(summed[3], "fsdp", scatter_dimension=0, tiled=True),
        lax.psum_scatter(summed[4], "fsdp", scatter_dimension=0, tiled=True),
        lax.psum_scatter(summed[5], "fsdp", scatter_dimension=0, tiled=True),
        lax.psum_scatter(summed[6], "fsdp", scatter_dimension=0, tiled=True),
        lax.psum_scatter(summed[7], "fsdp", scatter_dimension=0, tiled=True),
        lax.psum_scatter(summed[8], "fsdp", scatter_dimension=0, tiled=True),
        lax.psum_scatter(summed[9], "fsdp", scatter_dimension=0, tiled=True),
    )
    return (
        node_output,
        grad_features,
        shares[0],
        shares[1],
        shares[2],
        shares[3],
        shares[4],
        shares[5],
        shares[6],
        shares[7],
        shares[8],
        shares[9],
    )


def solution(mesh):
    in_specs = (
        P(("grp", "fsdp"), None),
        P(("grp", "fsdp"), None, None),
        P(("grp", "fsdp")),
        P("fsdp", None),
        P("fsdp"),
        P("fsdp"),
        P("fsdp", None),
        P("fsdp", None),
        P("fsdp"),
        P("fsdp"),
        P("fsdp", None),
        P("fsdp", None),
        P("fsdp"),
        P(("grp", "fsdp"), None),
    )
    out_specs = (
        P(("grp", "fsdp"), None),
        P(("grp", "fsdp"), None),
        P("fsdp", None),
        P("fsdp"),
        P("fsdp"),
        P("fsdp", None),
        P("fsdp", None),
        P("fsdp"),
        P("fsdp"),
        P("fsdp", None),
        P("fsdp", None),
        P("fsdp"),
    )
    return jax.shard_map(body, mesh=mesh, in_specs=in_specs, out_specs=out_specs, check_vma=False)
```

profile of v0, /device:TPU:0, one launch (start us, length us, event | category | flops | bytes accessed | tf_op | source)
XLA Modules:
  0.0 1001.2 jit_solution(9576038091035832798)
XLA Ops:
  21.4 44.4 %all-reduce.15 = (bf16[1024]{0:T(1024)(128)(2,1)S(1)}, bf16[512]{0:T(512)(128)(2,1)S(1)}, bf16[512]{0:T(512)(128)(2,1)S(1)}, bf16[512]{0:T(512)(128)(2,1)S(1)}, bf16[512]{0:T(512)(128)(2,1)S(1)}) all-reduce(bf16[1024]{0:T(1024)(128)(2,1)S(1)} %dynamic-update-slice.4, ...), channel_id=1, replica_groups=mesh['grp'=2,'fsdp'=16] {'fsdp'}, use_global_device_ids=true, to_apply=%add.8 | all-reduce | flops 3072 | bytes 12288
  68.2 36.6 %all_gather.39 = bf16[128,512]{1,0:T(8,128)(2,1)S(1)} all-gather(bf16[8,512]{1,0:T(8,128)(2,1)} %param.17), channel_id=1, replica_groups=mesh['grp'=2,'fsdp'=16] {'fsdp'}, dimensions={0}, use_global_device_ids=true | all-gather | bytes 139264 | tf_op jit(solution)/shard_map/all_gather | solution.py:106
  105.8 43.9 %all_gather.43 = bf16[512,512]{1,0:T(8,128)(2,1)} all-gather(bf16[32,512]{1,0:T(8,128)(2,1)} %param.21), channel_id=1, replica_groups=mesh['grp'=2,'fsdp'=16] {'fsdp'}, dimensions={0}, use_global_device_ids=true | all-gather | bytes 557056 | tf_op jit(solution)/shard_map/all_gather | solution.py:110
  159.7 10.6 %convolution_convert_fusion = bf16[3072,1536]{1,0:T(8,128)(2,1)} fusion(bf16[512,1536]{1,0:T(8,128)(2,1)} %all-gather.4.cloned.1.call-done, f32[3072,512]{1,0:T(8,128)} %copy-done, f32[512]{0:T(512)S(1)} %convert_element_type.174, f32[512]{0:T(512)S(1)} %convert_element_type.173, f32[3072]{0:T(1024)S(1)} %fusion.54, f32[3072]{0:T(1024)S(1)} %broadcast_multiply_fusion.2), kind=kOutput, calls=%fused_computation.17 | convolution fusion | flops 4844421120 | bytes 17330176 | tf_op jit(solution)/shard_map/dot_general | solution.py:38
  170.3 23.5 %reshape.220 = bf16[384,8,3,8,64]{4,3,2,1,0:T(8,128)(2,1)} reshape(bf16[3072,1536]{1,0:T(8,128)(2,1)} %convolution_convert_fusion) | data formatting | bytes 18874368 | tf_op jit(solution)/shard_map/reshape | solution.py:39
  193.9 14.0 %fusion.69 = (bf16[384,8,1,8,64]{4,3,2,1,0:T(8,128)(2,1)}, bf16[384,8,1,8,64]{4,3,2,1,0:T(8,128)(2,1)}, bf16[384,8,1,8,64]{4,3,2,1,0:T(8,128)(2,1)}) fusion(bf16[384,8,3,8,64]{4,3,2,1,0:T(8,128)(2,1)} %reshape.220), kind=kLoop, calls=%fused_computation.142 | loop fusion | bytes 18874368 | tf_op jit(solution)/shard_map/slice | solution.py:41
  207.9 12.7 %fusion.17 = f32[384,8,8,8]{2,3,1,0:T(8,128)} fusion(bf16[384,8,1,8,64]{4,3,2,1,0:T(8,128)(2,1)} %get-tuple-element.45, bf16[384,8,1,8,64]{4,3,2,1,0:T(8,128)(2,1)} %get-tuple-element.44), kind=kOutput, calls=%fused_computation.47 | convolution fusion | flops 25165824 | bytes 7077888 | tf_op jit(solution)/shard_map/nihd,njhd->nhij/dot_general | solution.py:43
  220.6 17.9 %fusion.73 = (f32[384,8,8]{2,1,0:T(8,128)S(1)}, f32[384,8,8,8]{2,3,1,0:T(8,128)}) fusion(f32[384,8,8,8]{2,3,1,0:T(8,128)} %fusion.17), kind=kOutput, calls=%fused_computation.146 | output fusion | flops 786439 | bytes 1671168 | tf_op jit(solution)/shard_map/sub | solution.py:46
  292.3 12.3 %fusion.40 = f32[384,1,7]{2,1,0:T(1,128)S(1)} fusion(f32[384,512,1]{1,0,2:T(8,128)S(1)} %copy-done.12, f32[384,8,512]{2,1,0:T(8,128)S(1)} %add_bitcast_fusion), kind=kOutput, calls=%fused_computation.84 | convolution fusion | flops 16515072 | bytes 7088640 | tf_op jit(solution)/shard_map/transpose(jvp(nk,nkd->nd))/dot_general | solution.py:136
  304.7 9.6 fusion.24
  322.0 15.1 %convolution_convert_fusion.3 = bf16[1024,512]{1,0:T(8,128)(2,1)} fusion(f32[384,8,512]{2,0,1:T(8,128)S(1)} %pad_add_fusion, f32[3072,1024]{1,0:T(8,128)} %fusion.64), kind=kOutput, calls=%fused_computation.65 | convolution fusion | flops 3250061312 | bytes 19922944 | tf_op jit(solution)/shard_map/dot_general | solution.py:22
  337.1 17.3 %fusion.7 = bf16[3072,1024]{1,0:T(8,128)(2,1)} fusion(f32[3072,1024]{1,0:T(8,128)} %fusion.64, bf16[1024,512]{1,0:T(8,128)(2,1)S(1)} %copy-done.40, f32[384,8,512]{2,0,1:T(8,128)S(1)} %pad_add_fusion), kind=kOutput, calls=%fused_computation.10 | convolution fusion | flops 3284140032 | bytes 26214400 | tf_op jit(solution)/shard_map/dot_general | solution.py:28
  389.3 12.0 %convert_bitcast_fusion = bf16[384,8,1,8,64]{4,1,3,0,2:T(8,128)(2,1)} fusion(bf16[384,8,8,64]{3,2,1,0:T(8,128)(2,1)} %reshape.223, f32[384,8,8,8]{2,3,1,0:T(8,128)} %get-tuple-element.79, f32[384,8,8]{2,1,0:T(8,128)} %copy-done.13), kind=kOutput, calls=%fused_computation.33 | convolution fusion | flops 27131904 | bytes 7176192 | tf_op jit(solution)/shard_map/nhij,nihd->njhd/dot_general | solution.py:181
  401.2 16.0 %multiply_reduce_fusion = (f32[384,8,8]{2,1,0:T(8,128)S(1)}, f32[384,8,8,8]{2,3,1,0:T(8,128)}) fusion(f32[384,8,8,8]{2,3,1,0:T(8,128)} %get-tuple-element.79, f32[384,8,8]{2,1,0:T(8,128)S(1)} %copy-done.14, bf16[384,8,1,8,64]{4,3,2,1,0:T(8,128)(2,1)} %get-tuple-element.46, bf16[384,8,8,64]{3,2,1,0:T(8,128)(2,1)} %reshape.223), kind=kOutput, calls=%fused_computation.14 | convolution fusion | flops 25731072 | bytes 8060928 | tf_op jit(solution)/shard_map/nihd,njhd->nhij/dot_general | solution.py:175
  417.2 13.2 %multiply_convert_fusion.2 = bf16[384,8,8,8]{2,3,1,0:T(8,128)(2,1)} fusion(f32[384,8,8,8]{2,3,1,0:T(8,128)} %get-tuple-element.84, f32[384,8,8]{2,1,0:T(8,128)S(1)} %get-tuple-element.83, f32[384,8,8,8]{2,3,1,0:T(8,128)} %get-tuple-element.79, f32[384,8,8]{2,1,0:T(8,128)S(1)} %copy-done.14), kind=kLoop, calls=%fused_computation.13 | loop fusion | flops 786432 | bytes 2162688 | tf_op jit(solution)/shard_map/convert_element_type | solution.py:180
  430.4 10.7 %fusion.12 = bf16[384,8,1,8,64]{4,1,3,0,2:T(8,128)(2,1)} fusion(bf16[384,8,8,8]{2,3,1,0:T(8,128)(2,1)} %multiply_convert_fusion.2, bf16[384,8,1,8,64]{4,3,2,1,0:T(8,128)(2,1)} %get-tuple-element.45), kind=kOutput, calls=%fused_computation.23 | convolution fusion | flops 28311552 | bytes 6684672 | tf_op jit(solution)/shard_map/nhij,nihd->njhd/dot_general | solution.py:187
  463.7 24.7 %convert_element_type.192 = bf16[3072,1536]{1,0:T(8,128)(2,1)} reshape(bf16[384,8,3,8,64]{4,3,2,1,0:T(8,128)(2,1)} %copy.64) | data formatting | bytes 18874368 | tf_op jit(solution)/shard_map/convert_element_type | solution.py:191
  488.5 12.1 %convolution_convert_fusion.2 = bf16[512,1536]{1,0:T(8,128)(2,1)} fusion(bf16[3072,1536]{1,0:T(8,128)(2,1)} %convert_element_type.192, f32[3072,512]{1,0:T(8,128)} %copy-done, f32[512]{0:T(512)S(1)} %copy-done.37, f32[512]{0:T(512)S(1)} %copy-done.35, f32[3072]{0:T(1024)S(1)} %copy-done.31, f32[3072]{0:T(1024)S(1)} %copy-done.21), kind=kOutput, calls=%fused_computation.61 | convolution fusion | flops 4840488960 | bytes 17330176 | tf_op jit(solution)/shard_map/dot_general | solution.py:22
  517.4 25.2 %all-reduce.20.cloned.1.call-done = (bf16[128,512]{1,0:T(8,128)(2,1)}, bf16[512,1536]{1,0:T(8,128)(2,1)}, bf16[512,512]{1,0:T(8,128)(2,1)}, bf16[512,1024]{1,0:T(8,128)(2,1)}, bf16[1024,512]{1,0:T(8,128)(2,1)}) async-done(((bf16[128,512]{1,0:T(8,128)(2,1)}, bf16[512,1536]{1,0:T(8,128)(2,1)}, bf16[512,512]{1,0:T(8,128)(2,1)}, bf16[512,1024]{1,0:T(8,128)(2,1)}, bf16[1024,512]{1,0:T(8,128)(2,1)}), ...) | async-done | bytes 4325392 | tf_op jit(solution)/shard_map/psum | solution.py:224
  570.7 77.5 %all-reduce.14 = (f32[512]{0:T(512)S(1)}, f32[512]{0:T(512)S(1)}, f32[512]{0:T(512)S(1)}, f32[512]{0:T(512)S(1)}, f32[1024]{0:T(1024)S(1)}) all-reduce(bf16[512]{0:T(512)(128)(2,1)S(1)} %get-tuple-element.28, bf16[512]{0:T(512)(128)(2,1)S(1)} %get-tuple-element.29, ...), channel_id=3, replica_groups=mesh['grp'=2,'fsdp'=16] {'fsdp'}, use_global_device_ids=true, to_apply=%region_20.0.clone | all-reduce | flops 3072 | bytes 18432
  664.7 34.6 %reduce-scatter.10.cloned.1.call-done = f32[32,512]{1,0:T(8,128)} async-done(((f32[512,512]{1,0:T(8,128)}), f32[32,512]{1,0:T(8,128)}) %reduce-scatter.10.cloned.1.call-update) | async-done | bytes 65552 | tf_op jit(solution)/shard_map/reduce_scatter | solution.py:240
  699.4 80.2 %reduce-scatter.12.cloned.1.call-done = f32[32,1024]{1,0:T(8,128)} async-done(((f32[512,1024]{1,0:T(8,128)}), f32[32,1024]{1,0:T(8,128)}) %reduce-scatter.12.cloned.1.call-update) | async-done | bytes 131088 | tf_op jit(solution)/shard_map/reduce_scatter | solution.py:243
  779.6 80.6 %reduce-scatter.14.cloned.1.call-done = f32[64,512]{1,0:T(8,128)} async-done(((f32[1024,512]{1,0:T(8,128)}), f32[64,512]{1,0:T(8,128)}) %reduce-scatter.14.cloned.1.call-update) | async-done | bytes 131088 | tf_op jit(solution)/shard_map/reduce_scatter | solution.py:244
  860.2 134.3 %reduce-scatter.8.cloned.1.call-done = f32[32,1536]{1,0:T(8,128)} async-done(((f32[512,1536]{1,0:T(8,128)}), f32[32,1536]{1,0:T(8,128)}) %reduce-scatter.8.cloned.1.call-update) | async-done | bytes 196624 | tf_op jit(solution)/shard_map/reduce_scatter | solution.py:239
  (243 shorter events, 204.5 us)
Async XLA Ops:
  7.2 152.5 %all-gather.4.cloned.1.call-start = ((), (), s32[]{:S(2)}) async-start(), calls=%async_computation.5 | async-start | bytes 1671168 | tf_op jit(solution)/shard_map/all_gather | solution.py:109
  7.9 260.4 %all-gather.6.cloned.1.call-start = ((), (), s32[]{:S(2)}) async-start(), calls=%async_computation.6 | async-start | bytes 1114112 | tf_op jit(solution)/shard_map/all_gather | solution.py:120
  8.7 268.9 %all-gather.8.cloned.1.call-start = ((), (), s32[]{:S(2)}) async-start(), calls=%async_computation.7 | async-start | bytes 1114112 | tf_op jit(solution)/shard_map/all_gather | solution.py:121
  9.4 533.2 %all-reduce.20.cloned.1.call-start = ((), (), s32[]{:S(2)}) async-start(), calls=%async_computation.13 | async-start | bytes 8650752 | tf_op jit(solution)/shard_map/psum | solution.py:224
  10.2 143.9 %copy-start.18 = (f32[3,128]{1,0:T(4,128)}, f32[3,128]{1,0:T(4,128)S(1)}, u32[]{:S(2)}) copy-start(f32[3,128]{1,0:T(4,128)S(1)} %get-tuple-element.63) | copy-start | bytes 4612
  10.2 307.7 %copy-start.28 = (f32[384]{0:T(512)}, f32[384]{0:T(512)S(1)}, u32[]{:S(2)}) copy-start(f32[384]{0:T(512)S(1)} %get-tuple-element.62) | copy-start | bytes 4612
  65.9 93.9 %copy-start.34 = (f32[512]{0:T(512)}, f32[512]{0:T(512)S(1)}, u32[]{:S(2)}) copy-start(f32[512]{0:T(512)S(1)} %convert_element_type.173) | copy-start | bytes 6148
  65.9 93.8 %copy-start.36 = (f32[512]{0:T(512)}, f32[512]{0:T(512)S(1)}, u32[]{:S(2)}) copy-start(f32[512]{0:T(512)S(1)} %convert_element_type.174) | copy-start | bytes 6148
  68.2 83.9 %copy-start.4 = (f32[3,128,128]{2,1,0:T(8,128)}, f32[3,128,128]{2,1,0:T(8,128)S(1)}, u32[]{:S(2)}) copy-start(f32[3,128,128]{2,1,0:T(8,128)S(1)} %multiply_multiply_fusion.2) | copy-start | bytes 589828
  104.9 49.3 %copy-start.15 = (bf16[128,512]{1,0:T(8,128)(2,1)}, bf16[128,512]{1,0:T(8,128)(2,1)S(1)}, u32[]{:S(2)}) copy-start(bf16[128,512]{1,0:T(8,128)(2,1)S(1)} %all_gather.39) | copy-start | bytes 393220
  207.9 30.6 %slice-start.8 = ((s8[6291456]{0:T(1024)(128)(4,1)}), s8[2097152]{0:T(1024)(128)(4,1)S(1)}, s32[]{:S(2)}) async-start(s8[6291456]{0:T(1024)(128)(4,1)} %bitcast.204), calls=%async_computation.22 | async-start | bytes 4194304
  322.0 32.5 %slice-start.4 = ((s8[6291456]{0:T(1024)(128)(4,1)}), s8[4194304]{0:T(1024)(128)(4,1)S(1)}, s32[]{:S(2)}) async-start(s8[6291456]{0:T(1024)(128)(4,1)} %bitcast.197), calls=%async_computation.18 | async-start | bytes 8388608
  463.7 24.7 %copy-start.31 = (f32[3072]{0:T(1024)S(1)}, f32[3072]{0:T(1024)}, u32[]{:S(2)}) copy-start(f32[3072]{0:T(1024)} %copy-done.30) | copy-start | bytes 36868
  463.7 24.7 %copy-start.35 = (f32[512]{0:T(512)S(1)}, f32[512]{0:T(512)}, u32[]{:S(2)}) copy-start(f32[512]{0:T(512)} %copy-done.34) | copy-start | bytes 6148
  463.7 24.8 %copy-start.37 = (f32[512]{0:T(512)S(1)}, f32[512]{0:T(512)}, u32[]{:S(2)}) copy-start(f32[512]{0:T(512)} %copy-done.36) | copy-start | bytes 6148
  463.7 36.9 %slice-start = ((s8[6291456]{0:T(1024)(128)(4,1)}), s8[2097152]{0:T(1024)(128)(4,1)S(1)}, s32[]{:S(2)}) async-start(s8[6291456]{0:T(1024)(128)(4,1)} %bitcast.193), calls=%async_computation.14 | async-start | bytes 4194304
  488.5 25.8 %slice-start.2 = ((s8[6291456]{0:T(1024)(128)(4,1)}), s8[4194304]{0:T(1024)(128)(4,1)S(1)}, s32[]{:S(2)}) async-start(s8[6291456]{0:T(1024)(128)(4,1)} %bitcast.195), calls=%async_computation.16 | async-start | bytes 8388608
  517.3 147.4 %reduce-scatter.6.cloned.1.call-start = ((), (), s32[]{:S(2)}) async-start(), calls=%async_computation.8 | async-start | bytes 278528 | tf_op jit(solution)/shard_map/reduce_scatter | solution.py:236
  544.3 155.1 %reduce-scatter.10.cloned.1.call-start = ((), (), s32[]{:S(2)}) async-start(), calls=%async_computation.10 | async-start | bytes 1114112 | tf_op jit(solution)/shard_map/reduce_scatter | solution.py:240
  546.5 233.1 %reduce-scatter.12.cloned.1.call-start = ((), (), s32[]{:S(2)}) async-start(), calls=%async_computation.11 | async-start | bytes 2228224 | tf_op jit(solution)/shard_map/reduce_scatter | solution.py:243
  549.3 310.8 %reduce-scatter.14.cloned.1.call-start = ((), (), s32[]{:S(2)}) async-start(), calls=%async_computation.12 | async-start | bytes 2228224 | tf_op jit(solution)/shard_map/reduce_scatter | solution.py:244
  552.3 442.1 %reduce-scatter.8.cloned.1.call-start = ((), (), s32[]{:S(2)}) async-start(), calls=%async_computation.9 | async-start | bytes 3342336 | tf_op jit(solution)/shard_map/reduce_scatter | solution.py:239
  552.4 98.7 %copy-start.16 = (bf16[128,512]{1,0:T(8,128)(2,1)S(1)}, bf16[128,512]{1,0:T(8,128)(2,1)}, u32[]{:S(2)}) copy-start(bf16[128,512]{1,0:T(8,128)(2,1)} %copy-done.15) | copy-start | bytes 393220
  568.1 85.5 %copy-start.5 = (f32[3,128,128]{2,1,0:T(8,128)S(1)}, f32[3,128,128]{2,1,0:T(8,128)}, u32[]{:S(2)}) copy-start(f32[3,128,128]{2,1,0:T(8,128)} %copy-done.4) | copy-start | bytes 589828
  (39 other events, 339.6 us)
Sparse Core Ops, SparseCore 0:
  10.8 61.1 all-gather.3
  74.7 55.8 all-gather.5
  133.4 54.4 all-gather.7
  517.4 25.1 all-reduce.19
  545.3 77.3 reduce-scatter.5
  625.4 73.8 reduce-scatter.9
  702.3 77.2 reduce-scatter.11
  782.5 77.5 reduce-scatter.13
  866.5 127.9 reduce-scatter.7
where the time goes:
time: 1010 us; the launch traced here: 1000 us
  waiting for transfers between devices  357 us (35%)
  matrix products  223 us (22%)
  blocking collectives  205 us (20%)
  local copies, waits for them, and re-layouts  113 us (11%)
  other arithmetic  84.1 us (8%)
  between operations  17.6 us (2%)
    reduce_scatter x1, waiting for transfers between devices, body(): lax.psum_scatter(summed[3], 'fsdp', scatter_dimension=0, tiled=True)  134 us
    unnamed x2, blocking collectives  122 us
    reduce_scatter x1, waiting for transfers between devices, body(): lax.psum_scatter(summed[8], 'fsdp', scatter_dimension=0, tiled=True)  80.6 us
    reduce_scatter x1, waiting for transfers between devices, body(): lax.psum_scatter(summed[7], 'fsdp', scatter_dimension=0, tiled=True)  80.2 us
    all_gather x1, blocking collectives, body(): lax.all_gather(merge_weight, 'fsdp', axis=0, tiled=True)  43.9 us
    dot_general x5, matrix products, contract_lead(): lax.dot_general(left, right, (((0,), (0,)), ((), ())), preferred_element_...  39.1 us
    all_gather x1, blocking collectives, body(): lax.all_gather(input_weight, 'fsdp', axis=0, tiled=True)  36.6 us
    dot_general x5, matrix products, contract_last(): lax.dot_general(left, right, (((1,), (1,)), ((), ())), preferred_element_...  35.1 us
  transfers between devices with their start and end apart: 9, of which 5 were waited for; matrix products, arithmetic and copies ran while one was open for 17% of the time, Pallas kernels for 0%

commit v1 on v0

v1 whole, which is shorter than its diff:
```python
import functools

import jax
import jax.numpy as jnp
from jax import lax
from jax.experimental import pallas as pl
from jax.experimental.pallas import tpu as pltpu
from jax.sharding import PartitionSpec as P

HEADS = 8
HEAD = 64
HOPS = 7
HOP_TOKENS = HOPS + 1
NODES_PER_TILE = 64
TOKENS = NODES_PER_TILE * HOP_TOKENS
GROUP = 16
MIB = 1 << 20
F32 = jnp.float32
BF16 = jnp.bfloat16
GELU_A = 0.7978845608028654
GELU_B = 0.044715


def dot(left, right):
    return jnp.dot(left, right, preferred_element_type=F32)


def dot_lead(left, right):
    return lax.dot_general(left, right, (((0,), (0,)), ((), ())), preferred_element_type=F32)


def dot_last(left, right):
    return lax.dot_general(left, right, (((1,), (1,)), ((), ())), preferred_element_type=F32)


def link_of(adjacency, count):
    slots = adjacency.shape[0]
    rows = lax.broadcasted_iota(jnp.int32, (slots, slots), 0)
    cols = lax.broadcasted_iota(jnp.int32, (slots, slots), 1)
    live = jnp.logical_and(rows < count, cols < count)
    link = jnp.where(live, adjacency, 0) + jnp.where(rows == cols, 1, 0)
    link = link.astype(F32)
    root = lax.rsqrt(jnp.sum(link, axis=-1, keepdims=True))
    return link.astype(BF16), root


def hop(link, root, state):
    width = state.shape[1]
    scaled = state * root
    high = scaled.astype(BF16)
    rest = scaled - high.astype(F32)
    middle = rest.astype(BF16)
    low = (rest - middle.astype(F32)).astype(BF16)
    spread = dot(link, jnp.concatenate([high, middle, low], axis=1))
    return (spread[:, :width] + (spread[:, width : 2 * width] + spread[:, 2 * width :])) * root


def live_rows(count, first, rows):
    index = lax.broadcasted_iota(jnp.int32, (rows, 1), 0) + first
    return jnp.where(index < count, 1.0, 0.0).astype(F32)


def norm_stats(values):
    mean = jnp.mean(values, axis=-1, keepdims=True)
    centred = values - mean
    var = jnp.mean(centred * centred, axis=-1, keepdims=True)
    inv = lax.rsqrt(var + 1e-05)
    return centred * inv, inv


def head_masks():
    lane = lax.broadcasted_iota(jnp.int32, (GROUP * HOP_TOKENS, 2 * HEAD), 1)
    return lane < HEAD


def pair_stack(block, first_half):
    zero = jnp.zeros_like(block)
    return jnp.concatenate(
        [jnp.where(first_half, block, zero), jnp.where(first_half, zero, block)], axis=0
    )


def same_node():
    span = GROUP * HOP_TOKENS
    row = lax.broadcasted_iota(jnp.int32, (span, span), 0) % GROUP
    col = lax.broadcasted_iota(jnp.int32, (span, span), 1) % GROUP
    return row == col


def pair_probs(queries, key_stack, keep):
    span = GROUP * HOP_TOKENS
    scores = dot_last(queries, key_stack)
    halves = []
    for half in range(2):
        part = jnp.where(keep, scores[:, half * span : (half + 1) * span], -jnp.inf)
        top = jnp.max(part, axis=-1, keepdims=True)
        power = jnp.exp((part - top) * HEAD ** (-0.5))
        halves.append(power * (1.0 / jnp.sum(power, axis=-1, keepdims=True)))
    return halves


def read_block(ref, group, first):
    rows = pl.ds(pl.multiple_of(group * GROUP, GROUP), GROUP)
    return ref[:, rows, first : first + 2 * HEAD].reshape(GROUP * HOP_TOKENS, 2 * HEAD)


def write_block(ref, group, first, block):
    rows = pl.ds(pl.multiple_of(group * GROUP, GROUP), GROUP)
    ref[:, rows, first : first + 2 * HEAD] = block.reshape(HOP_TOKENS, GROUP, 2 * HEAD)


def forward_kernel(
    counts_ref,
    adjacency_ref,
    features_ref,
    embed_ref,
    gain_ref,
    shift_ref,
    attend_ref,
    merge_ref,
    stacked_ref,
    hidden_ref,
    normed_ref,
    triple_ref,
    mixed_ref,
    second_ref,
):
    step = pl.program_id(0)
    clusters, slots = adjacency_ref.shape[:2]
    width = hidden_ref.shape[-1]
    per_cluster = slots // NODES_PER_TILE

    @pl.when(step == 0)
    def _():
        links = []
        states = []
        for cluster in range(clusters):
            count = counts_ref[cluster]
            links.append(link_of(adjacency_ref[cluster], count))
            states.append(
                features_ref[cluster * slots : (cluster + 1) * slots].astype(F32)
                * live_rows(count, 0, slots)
            )
        for index in range(HOP_TOKENS):
            for cluster in range(clusters):
                if index > 0:
                    states[cluster] = hop(*links[cluster], states[cluster])
                rounded = states[cluster].astype(BF16)
                for part in range(per_cluster):
                    stacked_ref[cluster * per_cluster + part, index] = rounded[
                        part * NODES_PER_TILE : (part + 1) * NODES_PER_TILE
                    ]

    stacked = stacked_ref[step].reshape(TOKENS, stacked_ref.shape[-1])
    hidden = dot(stacked, embed_ref[...])
    hidden_ref[...] = hidden
    normal, _ = norm_stats(hidden)
    normed = (normal * gain_ref[...] + shift_ref[...]).astype(BF16)
    normed_ref[...] = normed
    triple = dot(normed, attend_ref[...]).astype(BF16)
    triple_ref[...] = triple.reshape(triple_ref.shape)
    first_half = head_masks()
    keep = same_node()

    def group_step(group, carry):
        for first in range(0, width, 2 * HEAD):
            queries = read_block(triple_ref, group, first)
            keys = pair_stack(read_block(triple_ref, group, width + first), first_half)
            values = pair_stack(read_block(triple_ref, group, 2 * width + first), first_half)
            probs = pair_probs(queries, keys, keep)
            rounded = jnp.concatenate([half.astype(BF16) for half in probs], axis=1)
            write_block(mixed_ref, group, first, dot(rounded, values).astype(BF16))
        return carry

    lax.fori_loop(0, NODES_PER_TILE // GROUP, group_step, 0)
    mixed = mixed_ref[...].reshape(TOKENS, width)
    second_ref[...] = hidden_ref[...] + dot(mixed, merge_ref[...])


def middle_kernel(
    counts_ref,
    second_ref,
    mixed_ref,
    cotangent_ref,
    gain_ref,
    shift_ref,
    expand_ref,
    reduce_ref,
    readout_ref,
    output_ref,
    grad_second_ref,
    grad_merge_ref,
    grad_gain_ref,
    grad_shift_ref,
    grad_expand_ref,
    grad_reduce_ref,
    grad_readout_ref,
):
    step = pl.program_id(0)
    width = second_ref.shape[-1]
    per_cluster = 128 // NODES_PER_TILE

    @pl.when(step == 0)
    def _():
        for ref in (
            grad_merge_ref,
            grad_gain_ref,
            grad_shift_ref,
            grad_expand_ref,
            grad_reduce_ref,
            grad_readout_ref,
        ):
            ref[...] = jnp.zeros_like(ref)

    second = second_ref[...]
    normal, inv = norm_stats(second)
    inner = (normal * gain_ref[...] + shift_ref[...]).astype(BF16)
    before = dot(inner, expand_ref[...])
    square = before * before
    curve = jnp.tanh(GELU_A * before * (1.0 + GELU_B * square))
    after = (0.5 * before * (1.0 + curve)).astype(BF16)
    slope = 0.5 * (1.0 + curve) + (0.5 * GELU_A) * before * (1.0 - curve * curve) * (
        1.0 + (3.0 * GELU_B) * square
    )
    third = second + dot(after, reduce_ref[...])
    shaped = third.reshape(HOP_TOKENS, NODES_PER_TILE, width)
    keep = live_rows(
        counts_ref[step // per_cluster], (step % per_cluster) * NODES_PER_TILE, NODES_PER_TILE
    )
    centre = shaped[0]
    row_node = readout_ref[0:1]
    row_hop = readout_ref[1:2]
    base = jnp.sum(centre * row_node, axis=-1, keepdims=True)
    logits = [
        base + jnp.sum(shaped[k] * row_hop, axis=-1, keepdims=True) for k in range(1, HOP_TOKENS)
    ]
    top = functools.reduce(jnp.maximum, logits)
    powers = [jnp.exp(logit - top) for logit in logits]
    scale = 1.0 / functools.reduce(jnp.add, powers)
    shares = [power * scale for power in powers]
    total = centre
    for k in range(1, HOP_TOKENS):
        total = total + shares[k - 1] * shaped[k]
    output_ref[...] = total * keep
    cotangent = cotangent_ref[...] * keep
    grad_shares = [
        jnp.sum(cotangent * shaped[k], axis=-1, keepdims=True) for k in range(1, HOP_TOKENS)
    ]
    mean_share = functools.reduce(jnp.add, [s * g for s, g in zip(shares, grad_shares)])
    grad_logits = [s * (g - mean_share) for s, g in zip(shares, grad_shares)]
    grad_base = functools.reduce(jnp.add, grad_logits)
    parts = [cotangent + grad_base * row_node]
    read_hop = jnp.zeros((NODES_PER_TILE, width), F32)
    for k in range(1, HOP_TOKENS):
        parts.append(shares[k - 1] * cotangent + grad_logits[k - 1] * row_hop)
        read_hop = read_hop + grad_logits[k - 1] * shaped[k]
    grad_readout_ref[0:1] += jnp.sum(grad_base * centre, axis=0, keepdims=True)
    grad_readout_ref[1:2] += jnp.sum(read_hop, axis=0, keepdims=True)
    grad_third = jnp.concatenate(parts, axis=0)
    grad_branch = grad_third.astype(BF16)
    grad_reduce_ref[...] += dot_lead(after, grad_branch)
    grad_before = (slope * dot_last(grad_branch, reduce_ref[...])).astype(BF16)
    grad_expand_ref[...] += dot_lead(inner, grad_before)
    grad_inner = dot_last(grad_before, expand_ref[...])
    grad_gain_ref[...] += jnp.sum(grad_inner * normal, axis=0, keepdims=True)
    grad_shift_ref[...] += jnp.sum(grad_inner, axis=0, keepdims=True)
    grad_normal = grad_inner * gain_ref[...]
    grad_second = grad_third + inv * (
        grad_normal
        - jnp.mean(grad_normal, axis=-1, keepdims=True)
        - normal * jnp.mean(grad_normal * normal, axis=-1, keepdims=True)
    )
    grad_second_ref[...] = grad_second
    grad_merge_ref[...] += dot_lead(mixed_ref[...].reshape(TOKENS, width), grad_second.astype(BF16))


def backward_kernel(
    counts_ref,
    adjacency_ref,
    stacked_ref,
    hidden_ref,
    normed_ref,
    triple_ref,
    grad_second_ref,
    embed_ref,
    gain_ref,
    attend_ref,
    merge_ref,
    grad_features_ref,
    grad_embed_ref,
    grad_gain_ref,
    grad_shift_ref,
    grad_attend_ref,
    grad_mixed_ref,
    grad_triple_ref,
    grad_stacked_ref,
):
    step = pl.program_id(0)
    steps = pl.num_programs(0)
    clusters, slots = adjacency_ref.shape[:2]
    width = hidden_ref.shape[-1]
    per_cluster = slots // NODES_PER_TILE

    @pl.when(step == 0)
    def _():
        for ref in (grad_embed_ref, grad_gain_ref, grad_shift_ref, grad_attend_ref):
            ref[...] = jnp.zeros_like(ref)

    grad_second = grad_second_ref[...]
    grad_mixed = dot_last(grad_second.astype(BF16), merge_ref[...]).astype(BF16)
    grad_mixed_ref[...] = grad_mixed.reshape(grad_mixed_ref.shape)
    first_half = head_masks()
    keep = same_node()
    span = GROUP * HOP_TOKENS

    def group_step(group, carry):
        for first in range(0, width, 2 * HEAD):
            queries = read_block(triple_ref, group, first)
            keys = pair_stack(read_block(triple_ref, group, width + first), first_half)
            values = pair_stack(read_block(triple_ref, group, 2 * width + first), first_half)
            out_grad = read_block(grad_mixed_ref, group, first)
            probs = pair_probs(queries, keys, keep)
            grad_probs = dot_last(out_grad, values)
            grad_halves = []
            for half in range(2):
                part = grad_probs[:, half * span : (half + 1) * span]
                weighted = probs[half] * part
                grad_halves.append(
                    (weighted - probs[half] * jnp.sum(weighted, axis=-1, keepdims=True)).astype(
                        BF16
                    )
                )
            grad_scores = jnp.concatenate(grad_halves, axis=1)
            grad_query = dot(grad_scores, keys) * HEAD ** (-0.5)
            grad_key = dot_lead(
                jnp.concatenate(grad_halves, axis=0), pair_stack(queries, first_half)
            ) * HEAD ** (-0.5)
            grad_value = dot_lead(
                jnp.concatenate([half.astype(BF16) for half in probs], axis=0),
                pair_stack(out_grad, first_half),
            )
            write_block(grad_triple_ref, group, first, grad_query.astype(BF16))
            write_block(grad_triple_ref, group, width + first, grad_key.astype(BF16))
            write_block(grad_triple_ref, group, 2 * width + first, grad_value.astype(BF16))
        return carry

    lax.fori_loop(0, NODES_PER_TILE // GROUP, group_step, 0)
    grad_triple = grad_triple_ref[...].reshape(TOKENS, 3 * width)
    grad_attend_ref[...] += dot_lead(normed_ref[...], grad_triple)
    grad_normed = dot_last(grad_triple, attend_ref[...])
    normal, inv = norm_stats(hidden_ref[...])
    grad_gain_ref[...] += jnp.sum(grad_normed * normal, axis=0, keepdims=True)
    grad_shift_ref[...] += jnp.sum(grad_normed, axis=0, keepdims=True)
    grad_normal = grad_normed * gain_ref[...]
    grad_hidden = grad_second_ref[...] + inv * (
        grad_normal
        - jnp.mean(grad_normal, axis=-1, keepdims=True)
        - normal * jnp.mean(grad_normal * normal, axis=-1, keepdims=True)
    )
    grad_hidden = grad_hidden.astype(BF16)
    stacked = stacked_ref[...].reshape(TOKENS, stacked_ref.shape[-1])
    grad_embed_ref[...] += dot_lead(stacked, grad_hidden)
    grad_stacked_ref[step] = dot_last(grad_hidden, embed_ref[...]).reshape(
        grad_stacked_ref.shape[1:]
    )

    @pl.when(step == steps - 1)
    def _():
        links = []
        states = []

        def hop_grad(cluster, index):
            return jnp.concatenate(
                [grad_stacked_ref[cluster * per_cluster + p, index] for p in range(per_cluster)],
                axis=0,
            )

        for cluster in range(clusters):
            links.append(link_of(adjacency_ref[cluster], counts_ref[cluster]))
            states.append(hop_grad(cluster, HOPS))
        for index in range(HOPS - 1, -1, -1):
            for cluster in range(clusters):
                states[cluster] = hop_grad(cluster, index) + hop(*links[cluster], states[cluster])
        for cluster in range(clusters):
            grad_features_ref[cluster * slots : (cluster + 1) * slots] = states[
                cluster
            ] * live_rows(counts_ref[cluster], 0, slots)


def whole(shape):
    return pl.BlockSpec(shape, lambda t: (0,) * len(shape), pipeline_mode=pl.Buffered(1))


def kept(shape):
    return pl.BlockSpec(shape, lambda t: (0,) * len(shape))


def tiled(*shape):
    return pl.BlockSpec((None,) + shape, lambda t: (t,) + (0,) * len(shape))


def rows_of(*shape):
    return pl.BlockSpec(shape, lambda t: (t,) + (0,) * (len(shape) - 1))


def sds(shape, dtype):
    return jax.ShapeDtypeStruct(shape, dtype)


SMEM_SPEC = pl.BlockSpec(memory_space=pltpu.SMEM)


def params():
    return pltpu.CompilerParams(
        vmem_limit_bytes=56 * MIB, dimension_semantics=("arbitrary",)
    )


def forward_part(counts, adjacency, features, embed, gain, shift, attend, merge):
    nodes, feat = features.shape
    width = merge.shape[0]
    tiles = nodes // NODES_PER_TILE
    hops, per = HOP_TOKENS, NODES_PER_TILE
    return pl.pallas_call(
        forward_kernel,
        grid=(tiles,),
        in_specs=[
            SMEM_SPEC,
            whole(adjacency.shape),
            whole(features.shape),
            whole(embed.shape),
            whole(gain.shape),
            whole(shift.shape),
            whole(attend.shape),
            whole(merge.shape),
        ],
        out_specs=[
            kept((tiles, hops, per, feat)),
            tiled(TOKENS, width),
            tiled(TOKENS, width),
            rows_of(hops, per, 3 * width),
            rows_of(hops, per, width),
            tiled(TOKENS, width),
        ],
        out_shape=[
            sds((tiles, hops, per, feat), BF16),
            sds((tiles, TOKENS, width), F32),
            sds((tiles, TOKENS, width), BF16),
            sds((tiles * hops, per, 3 * width), BF16),
            sds((tiles * hops, per, width), BF16),
            sds((tiles, TOKENS, width), F32),
        ],
        compiler_params=params(),
        name="hops_attention",
    )(counts, adjacency, features, embed, gain, shift, attend, merge)


def middle_part(counts, second, mixed, cotangent, gain, shift, expand, reducer, readout):
    tiles, _, width = second.shape
    hops, per = HOP_TOKENS, NODES_PER_TILE
    grads = [
        (width, width),
        (1, width),
        (1, width),
        expand.shape,
        reducer.shape,
        readout.shape,
    ]
    return pl.pallas_call(
        middle_kernel,
        grid=(tiles,),
        in_specs=[
            SMEM_SPEC,
            tiled(TOKENS, width),
            rows_of(hops, per, width),
            rows_of(per, width),
            whole(gain.shape),
            whole(shift.shape),
            whole(expand.shape),
            whole(reducer.shape),
            whole(readout.shape),
        ],
        out_specs=[rows_of(per, width), tiled(TOKENS, width)] + [kept(shape) for shape in grads],
        out_shape=[sds(cotangent.shape, F32), sds(second.shape, F32)]
        + [sds(shape, F32) for shape in grads],
        compiler_params=params(),
        name="feed_forward",
    )(counts, second, mixed, cotangent, gain, shift, expand, reducer, readout)


def backward_part(
    counts, adjacency, stacked, hidden, normed, triple, grad_second, embed, gain, attend, merge
):
    tiles, _, width = hidden.shape
    hops, per = HOP_TOKENS, NODES_PER_TILE
    feat = stacked.shape[-1]
    grads = [(tiles * per, feat), embed.shape, (1, width), (1, width), attend.shape]
    return pl.pallas_call(
        backward_kernel,
        grid=(tiles,),
        in_specs=[
            SMEM_SPEC,
            whole(adjacency.shape),
            tiled(hops, per, feat),
            tiled(TOKENS, width),
            tiled(TOKENS, width),
            rows_of(hops, per, 3 * width),
            tiled(TOKENS, width),
            whole(embed.shape),
            whole(gain.shape),
            whole(attend.shape),
            whole(merge.shape),
        ],
        out_specs=[kept(shape) for shape in grads],
        out_shape=[sds(shape, F32) for shape in grads],
        scratch_shapes=[
            pltpu.VMEM((hops, per, width), BF16),
            pltpu.VMEM((hops, per, 3 * width), BF16),
            pltpu.VMEM((tiles, hops, per, feat), F32),
        ],
        compiler_params=params(),
        name="attention_backward",
    )(counts, adjacency, stacked, hidden, normed, triple, grad_second, embed, gain, attend, merge)


def local_layer(
    features,
    adjacency,
    counts,
    embed,
    gain_one,
    shift_one,
    attend,
    merge,
    gain_two,
    shift_two,
    expand,
    reducer,
    readout,
    cotangent,
):
    row = lambda v: v.astype(F32).reshape(1, -1)
    gain_one, shift_one, gain_two, shift_two = map(row, (gain_one, shift_one, gain_two, shift_two))
    readout = readout.astype(F32).reshape(2, -1)
    stacked, hidden, normed, triple, mixed, second = forward_part(
        counts, adjacency, features, embed, gain_one, shift_one, attend, merge
    )
    (
        output,
        grad_second,
        grad_merge,
        grad_gain_two,
        grad_shift_two,
        grad_expand,
        grad_reduce,
        grad_readout,
    ) = middle_part(
        counts, second, mixed, cotangent, gain_two, shift_two, expand, reducer, readout
    )
    grad_features, grad_embed, grad_gain_one, grad_shift_one, grad_attend = backward_part(
        counts, adjacency, stacked, hidden, normed, triple, grad_second, embed, gain_one, attend, merge
    )
    return (
        output,
        grad_features,
        grad_embed,
        grad_gain_one.reshape(-1),
        grad_shift_one.reshape(-1),
        grad_attend,
        grad_merge,
        grad_gain_two.reshape(-1),
        grad_shift_two.reshape(-1),
        grad_expand,
        grad_reduce,
        grad_readout.reshape(-1),
    )


def gather(block):
    return lax.all_gather(block, "fsdp", axis=0, tiled=True)


def share(term):
    part = lax.psum_scatter(term.astype(BF16), "fsdp", scatter_dimension=0, tiled=True)
    return lax.psum(part.astype(F32), "grp")


def body(
    features,
    adjacency,
    counts,
    input_weight,
    first_gain,
    first_shift,
    attend_weight,
    merge_weight,
    second_gain,
    second_shift,
    expand_weight,
    reduce_weight,
    readout_weight,
    cotangent,
):
    vectors = (first_gain, first_shift, second_gain, second_shift, readout_weight)
    lengths = [v.shape[0] for v in vectors]
    places = [sum(lengths[:i]) for i in range(len(lengths) + 1)]
    packed = lax.all_gather(jnp.concatenate(vectors), "fsdp", axis=0, tiled=False)
    full = [
        packed[:, places[i] : places[i + 1]].reshape(-1) for i in range(len(lengths))
    ]
    terms = local_layer(
        features,
        adjacency,
        counts,
        gather(input_weight),
        full[0],
        full[1],
        gather(attend_weight),
        gather(merge_weight),
        full[2],
        full[3],
        gather(expand_weight),
        gather(reduce_weight),
        full[4],
        cotangent,
    )
    output, grad_features, *grads = terms
    small = [1, 2, 5, 6, 9]
    parts = packed.shape[0]
    packed_grad = jnp.concatenate([grads[i].reshape(parts, -1) for i in small], axis=1)
    packed_grad = lax.psum(
        lax.psum_scatter(packed_grad, "fsdp", scatter_dimension=0, tiled=True), "grp"
    ).reshape(-1)
    shares = [None if i in small else share(grad) for i, grad in enumerate(grads)]
    for place, i in enumerate(small):
        shares[i] = packed_grad[places[place] : places[place + 1]]
    return (output, grad_features, *shares)


def solution(mesh):
    nodes = ("grp", "fsdp")
    rows = P("fsdp", None)
    vector = P("fsdp")
    in_specs = (
        P(nodes, None),
        P(nodes, None, None),
        P(nodes),
        rows,
        vector,
        vector,
        rows,
        rows,
        vector,
        vector,
        rows,
        rows,
        vector,
        P(nodes, None),
    )
    out_specs = (
        P(nodes, None),
        P(nodes, None),
        rows,
        vector,
        vector,
        rows,
        rows,
        vector,
        vector,
        rows,
        rows,
        vector,
    )
    return jax.shard_map(body, mesh=mesh, in_specs=in_specs, out_specs=out_specs, check_vma=False)
```

time: 1010 us -> 744 us (0.74)
  matrix products: 223 us -> 0 us
  Pallas kernels: 0 us -> 149 us
  local copies, waits for them, and re-layouts: 113 us -> 11.1 us
  other arithmetic: 84.1 us -> 10.8 us
    dot_general x41 -> x0, matrix products: 223 us -> none  [the longest x5 39.1 us: contract_lead(): lax.dot_general(left, right, (((0,), (0,)), ((), ())), preferred_element_...]
    pallas_call x0 -> x3, Pallas kernels: none -> 149 us  [the longest x1 76.2 us: backward_part(): pl.pallas_call(backward_kernel, grid=(tiles,), in_specs=[SMEM_SPEC, whole...]
    convert_element_type x3 -> x5, local copies, waits for them, and re-layouts: 37 us -> 3.29 us  [the longest x4 2.62 us: local_layer(): row = lambda v: v.astype(F32).reshape(1, -1)]
    reshape x2 -> x0, local copies, waits for them, and re-layouts: 29.2 us -> none  [the longest x1 23.5 us: attention_parts(): triple.reshape(node_count, HOPS + 1, 3, HEADS, model_width // HEADS)]
    psum x1 -> x0, waiting for transfers between devices: 25.2 us -> none  [body(): lax.psum(grad_terms[0].astype(jnp.bfloat16), 'grp').astype(jnp.float32)]
    convert_element_type x15 -> x7, other arithmetic: 29.5 us -> 8.11 us  [the longest x5 8.03 us: share(): term.astype(BF16)]
    slice x6 -> x2, local copies, waits for them, and re-layouts: 21 us -> 1.1 us  [body(): shares[i] = packed_grad[places[place]:places[place + 1]]]
    sub x1 -> x0, other arithmetic: 17.9 us -> none  [attention_parts(): prob_rows = jax.nn.softmax(scores, axis=-1)]
  transfers between devices with their start and end apart: 9 -> 8, of which waited for: 5 -> 5; matrix products, arithmetic and copies ran while one was open for 17% -> 3% of each run, Pallas kernels for 0% -> 5%
where the time goes in v1:
time: 744 us; the launch traced here: 743 us
  waiting for transfers between devices  348 us (47%)
  blocking collectives  208 us (28%)
  Pallas kernels  149 us (20%)
  between operations  14.9 us (2%)
  local copies, waits for them, and re-layouts  11.1 us (1%)
  other arithmetic  10.8 us (1%)
    reduce_scatter x5, waiting for transfers between devices, share(): lax.psum_scatter(term.astype(BF16), 'fsdp', scatter_dimension=0, tiled=True)  343 us
    unnamed x2, blocking collectives  119 us
    all_gather x2, blocking collectives, gather(): return lax.all_gather(block, 'fsdp', axis=0, tiled=True)  82.9 us
    pallas_call x1, Pallas kernels, backward_part(): pl.pallas_call(backward_kernel, grid=(tiles,), in_specs=[SMEM_SPEC, whole...  76.2 us
    pallas_call x1, Pallas kernels, forward_part(): pl.pallas_call(forward_kernel, grid=(tiles,), in_specs=[SMEM_SPEC, whole(...  37.7 us
    pallas_call x1, Pallas kernels, middle_part(): pl.pallas_call(middle_kernel, grid=(tiles,), in_specs=[SMEM_SPEC, tiled(T...  35.6 us
  transfers between devices with their start and end apart: 8, of which 5 were waited for; matrix products, arithmetic and copies ran while one was open for 3% of the time, Pallas kernels for 5%

profile of v1, /device:TPU:0, one launch (start us, length us, event | category | flops | bytes accessed | tf_op | source)
XLA Modules:
  0.0 743.2 jit_solution(6385472334573406253)
XLA Ops:
  7.2 0.7 all-gather.5.cloned.1.call-update
  8.0 0.7 all-gather.7.cloned.1.call-update
  8.7 0.7 all-gather.9.cloned.1.call-update
  9.4 1.3 fusion
  11.4 3.4 concatenate.6
  15.1 44.3 %all-reduce = bf16[3072]{0:T(1024)(128)(2,1)S(1)} all-reduce(bf16[3072]{0:T(1024)(128)(2,1)S(1)} %dynamic-update-slice), channel_id=2, replica_groups=mesh['grp'=2,'fsdp'=16] {'fsdp'}, use_global_device_ids=true, to_apply=%add | all-reduce | flops 3072 | bytes 12288
  62.2 0.7 reshape.95.readout_ref
  62.9 39.1 %all_gather.21.embed_ref = bf16[128,512]{1,0:T(8,128)(2,1)} all-gather(bf16[8,512]{1,0:T(8,128)(2,1)} %param.17), channel_id=1, replica_groups=mesh['grp'=2,'fsdp'=16] {'fsdp'}, dimensions={0}, use_global_device_ids=true | all-gather | bytes 139264 | tf_op jit(solution)/shard_map/all_gather | solution.py:580
  102.0 43.8 %all_gather.25.merge_ref = bf16[512,512]{1,0:T(8,128)(2,1)} all-gather(bf16[32,512]{1,0:T(8,128)(2,1)} %param.21), channel_id=1, replica_groups=mesh['grp'=2,'fsdp'=16] {'fsdp'}, dimensions={0}, use_global_device_ids=true | all-gather | bytes 557056 | tf_op jit(solution)/shard_map/all_gather | solution.py:580
  145.8 37.7 %hops_attention.1 = (bf16[6,8,64,128]{3,2,1,0:T(8,128)(2,1)}, f32[6,512,512]{2,1,0:T(8,128)}, bf16[6,512,512]{2,1,0:T(8,128)(2,1)}, bf16[48,64,1536]{2,1,0:T(8,1...) custom-call(s32[3]{0:T(128)} %counts_ref.5, s32[3,128,128]{2,1,0:T(8,128)} %adjacency_ref.3, ...), custom_call_target="tpu_custom_call" | custom-call | tf_op jit(solution)/shard_map/hops_attention/pallas_call | solution.py:424
  183.5 3.2 all-gather.9.cloned.1.call-done.reduce_ref
  186.7 35.6 %feed_forward.1 = (f32[384,512]{1,0:T(8,128)}, f32[6,512,512]{2,1,0:T(8,128)}, f32[512,512]{1,0:T(8,128)}, f32[1,512]{1,0:T(1,128)}, f32[1,512]{1,0:T(1,128)}, /...) custom-call(s32[3]{0:T(128)} %counts_ref.5, f32[6,512,512]{2,1,0:T(8,128)} %get-tuple-element.31.second_ref, ...), custom_call_target="tpu_custom_call" | custom-call | tf_op jit(solution)/shard_map/feed_forward/pallas_call | solution.py:469
  222.3 76.2 %attention_backward.1 = (f32[384,128]{1,0:T(8,128)}, f32[128,512]{1,0:T(8,128)}, f32[1,512]{1,0:T(1,128)}, f32[1,512]{1,0:T(1,128)}, f32[512,1536]{1,0:T(8,128)}) custom-call(s32[3]{0:T(128)} %counts_ref.5, s32[3,128,128]{2,1,0:T(8,128)} %adjacency_ref.3, bf16[6,8,64,128]{3,2,1,0:T(8,128)(2,1)} %get-tuple-element.34.stacked_ref, ...), custom_call_target="tpu_custom_call" | custom-call | tf_op jit(solution)/shard_map/attention_backward/pallas_call | solution.py:498
  298.5 1.8 convert_element_type.99
  300.3 0.9 convert_element_type.103
  301.3 1.2 convert_element_type.105
  302.6 2.8 convert_element_type.107
  305.6 1.3 convert_element_type.101
  310.6 74.7 %all-reduce.1 = f32[16,192]{1,0:T(8,128)S(1)} all-reduce(f32[16,192]{1,0:T(8,128)S(1)} %concatenate.7), channel_id=4, replica_groups=mesh['grp'=2,'fsdp'=16] {'fsdp'}, use_global_device_ids=true, to_apply=%region_2.0.clone | all-reduce | flops 3072 | bytes 24576
  385.9 64.3 %reduce-scatter.10.cloned.1.call-done = bf16[32,512]{1,0:T(8,128)(2,1)} async-done(((bf16[512,512]{1,0:T(8,128)(2,1)}), bf16[32,512]{1,0:T(8,128)(2,1)}) %reduce-scatter.10.cloned.1.call-update) | async-done | bytes 32784 | tf_op jit(solution)/shard_map/reduce_scatter | solution.py:584
  450.3 76.1 %reduce-scatter.12.cloned.1.call-done = bf16[32,1024]{1,0:T(8,128)(2,1)} async-done(((bf16[512,1024]{1,0:T(8,128)(2,1)}), bf16[32,1024]{1,0:T(8,128)(2,1)}) %reduce-scatter.12.cloned.1.call-update) | async-done | bytes 65552 | tf_op jit(solution)/shard_map/reduce_scatter | solution.py:584
  526.4 76.7 %reduce-scatter.14.cloned.1.call-done = bf16[64,512]{1,0:T(8,128)(2,1)} async-done(((bf16[1024,512]{1,0:T(8,128)(2,1)}), bf16[64,512]{1,0:T(8,128)(2,1)}) %reduce-scatter.14.cloned.1.call-update) | async-done | bytes 65552 | tf_op jit(solution)/shard_map/reduce_scatter | solution.py:584
  603.1 125.9 %reduce-scatter.8.cloned.1.call-done = bf16[32,1536]{1,0:T(8,128)(2,1)} async-done(((bf16[512,1536]{1,0:T(8,128)(2,1)}), bf16[32,1536]{1,0:T(8,128)(2,1)}) %reduce-scatter.8.cloned.1.call-update) | async-done | bytes 98320 | tf_op jit(solution)/shard_map/reduce_scatter | solution.py:584
  729.0 6.3 all-reduce.4
  (55 shorter events, 8.9 us)
Async XLA Ops:
  7.2 138.6 %all-gather.5.cloned.1.call-start = ((), (), s32[]{:S(2)}) async-start(), calls=%async_computation.5 | async-start | bytes 1671168 | tf_op jit(solution)/shard_map/all_gather | solution.py:580
  7.9 175.6 %all-gather.7.cloned.1.call-start = ((), (), s32[]{:S(2)}) async-start(), calls=%async_computation.6 | async-start | bytes 1114112 | tf_op jit(solution)/shard_map/all_gather | solution.py:580
  8.7 178.0 %all-gather.9.cloned.1.call-start = ((), (), s32[]{:S(2)}) async-start(), calls=%async_computation.7 | async-start | bytes 1114112 | tf_op jit(solution)/shard_map/all_gather | solution.py:580
  9.4 376.5 %reduce-scatter.6.cloned.1.call-start = ((), (), s32[]{:S(2)}) async-start(), calls=%async_computation.8 | async-start | bytes 139264 | tf_op jit(solution)/shard_map/reduce_scatter | solution.py:584
  222.3 78.1 %copy-start.2 = (f32[512,512]{1,0:T(8,128)S(1)}, f32[512,512]{1,0:T(8,128)}, u32[]{:S(2)}) copy-start(f32[512,512]{1,0:T(8,128)} %get-tuple-element.47) | copy-start | bytes 3145732
  298.5 2.8 copy-start.1
  300.3 150.0 %reduce-scatter.10.cloned.1.call-start = ((), (), s32[]{:S(2)}) async-start(), calls=%async_computation.10 | async-start | bytes 557056 | tf_op jit(solution)/shard_map/reduce_scatter | solution.py:584
  301.2 225.2 %reduce-scatter.12.cloned.1.call-start = ((), (), s32[]{:S(2)}) async-start(), calls=%async_computation.11 | async-start | bytes 1114112 | tf_op jit(solution)/shard_map/reduce_scatter | solution.py:584
  302.5 3.0 copy-start
  302.5 300.6 %reduce-scatter.14.cloned.1.call-start = ((), (), s32[]{:S(2)}) async-start(), calls=%async_computation.12 | async-start | bytes 1114112 | tf_op jit(solution)/shard_map/reduce_scatter | solution.py:584
  305.4 423.6 %reduce-scatter.8.cloned.1.call-start = ((), (), s32[]{:S(2)}) async-start(), calls=%async_computation.9 | async-start | bytes 1671168 | tf_op jit(solution)/shard_map/reduce_scatter | solution.py:584
  305.5 1.9 copy-start.7
  305.5 2.7 copy-start.6
  305.5 3.4 copy-start.5
  305.5 4.1 copy-start.4
  305.5 4.9 copy-start.3
Sparse Core Ops, SparseCore 0:
  10.8 60.9 all-gather.4
  74.5 55.4 all-gather.6
  132.8 53.8 all-gather.8
  300.4 74.6 reduce-scatter.5
  377.3 72.9 reduce-scatter.9
  452.4 73.9 reduce-scatter.11
  528.8 74.2 reduce-scatter.13
  607.9 121.0 reduce-scatter.7

commit v2 on v1

v2 whole, which is shorter than its diff:
```python
import functools

import jax
import jax.numpy as jnp
from jax import lax
from jax.experimental import pallas as pl
from jax.experimental.pallas import tpu as pltpu
from jax.sharding import PartitionSpec as P

HEADS = 8
HEAD = 64
HOPS = 7
HOP_TOKENS = HOPS + 1
NODES_PER_TILE = 64
TOKENS = NODES_PER_TILE * HOP_TOKENS
GROUP = 16
MIB = 1 << 20
F32 = jnp.float32
BF16 = jnp.bfloat16
GELU_A = 0.7978845608028654
GELU_B = 0.044715
PLANE = 4
PACK = 16
MESH = pl.DeviceIdType.MESH


def dot(left, right):
    return jnp.dot(left, right, preferred_element_type=F32)


def dot_lead(left, right):
    return lax.dot_general(left, right, (((0,), (0,)), ((), ())), preferred_element_type=F32)


def dot_last(left, right):
    return lax.dot_general(left, right, (((1,), (1,)), ((), ())), preferred_element_type=F32)


def link_of(adjacency, count):
    slots = adjacency.shape[0]
    rows = lax.broadcasted_iota(jnp.int32, (slots, slots), 0)
    cols = lax.broadcasted_iota(jnp.int32, (slots, slots), 1)
    live = jnp.logical_and(rows < count, cols < count)
    link = jnp.where(live, adjacency, 0) + jnp.where(rows == cols, 1, 0)
    link = link.astype(F32)
    root = lax.rsqrt(jnp.sum(link, axis=-1, keepdims=True))
    return link.astype(BF16), root


def hop(link, root, state):
    width = state.shape[1]
    scaled = state * root
    high = scaled.astype(BF16)
    rest = scaled - high.astype(F32)
    middle = rest.astype(BF16)
    low = (rest - middle.astype(F32)).astype(BF16)
    spread = dot(link, jnp.concatenate([high, middle, low], axis=1))
    return (spread[:, :width] + (spread[:, width : 2 * width] + spread[:, 2 * width :])) * root


def live_rows(count, first, rows):
    index = lax.broadcasted_iota(jnp.int32, (rows, 1), 0) + first
    return jnp.where(index < count, 1.0, 0.0).astype(F32)


def norm_stats(values):
    mean = jnp.mean(values, axis=-1, keepdims=True)
    centred = values - mean
    var = jnp.mean(centred * centred, axis=-1, keepdims=True)
    inv = lax.rsqrt(var + 1e-05)
    return centred * inv, inv


def head_masks():
    lane = lax.broadcasted_iota(jnp.int32, (GROUP * HOP_TOKENS, 2 * HEAD), 1)
    return lane < HEAD


def pair_stack(block, first_half):
    zero = jnp.zeros_like(block)
    return jnp.concatenate(
        [jnp.where(first_half, block, zero), jnp.where(first_half, zero, block)], axis=0
    )


def same_node():
    span = GROUP * HOP_TOKENS
    row = lax.broadcasted_iota(jnp.int32, (span, span), 0) % GROUP
    col = lax.broadcasted_iota(jnp.int32, (span, span), 1) % GROUP
    return row == col


def pair_probs(queries, key_stack, keep):
    span = GROUP * HOP_TOKENS
    scores = dot_last(queries, key_stack)
    halves = []
    for half in range(2):
        part = jnp.where(keep, scores[:, half * span : (half + 1) * span], -jnp.inf)
        top = jnp.max(part, axis=-1, keepdims=True)
        power = jnp.exp((part - top) * HEAD ** (-0.5))
        halves.append(power * (1.0 / jnp.sum(power, axis=-1, keepdims=True)))
    return halves


def read_block(ref, group, first):
    rows = pl.ds(pl.multiple_of(group * GROUP, GROUP), GROUP)
    return ref[:, rows, first : first + 2 * HEAD].reshape(GROUP * HOP_TOKENS, 2 * HEAD)


def write_block(ref, group, first, block):
    rows = pl.ds(pl.multiple_of(group * GROUP, GROUP), GROUP)
    ref[:, rows, first : first + 2 * HEAD] = block.reshape(HOP_TOKENS, GROUP, 2 * HEAD)


class Place:
    def __init__(self, lines):
        self.lines = lines
        self.core = lax.axis_index("grp")
        self.owner = lax.axis_index("fsdp")
        self.line = lax.div(self.owner, PLANE)
        self.spot = lax.rem(self.owner, PLANE)

    def line_turn(self, ahead):
        return lax.rem(self.line + ahead + self.lines, self.lines)

    def spot_turn(self, ahead):
        return lax.rem(self.spot + ahead + PLANE, PLANE)

    def line_peer(self, ahead):
        return (self.core, self.line_turn(ahead) * PLANE + self.spot)

    def plane_peer(self, ahead):
        return (self.core, self.line * PLANE + self.spot_turn(ahead))

    def sibling(self):
        return (1 - self.core, self.owner)

    def peers(self):
        return (
            [self.line_peer(d) for d in range(1, self.lines)]
            + [self.plane_peer(e) for e in range(1, PLANE)]
            + [self.sibling()]
        )

    def greet(self):
        barrier = pltpu.get_barrier_semaphore()
        for peer in self.peers():
            pl.semaphore_signal(barrier, inc=1, device_id=peer, device_id_type=MESH)

    def greeted(self):
        pl.semaphore_wait(pltpu.get_barrier_semaphore(), self.lines + PLANE - 1)


def remote(source, target, send, recv, device):
    return pltpu.make_async_remote_copy(
        src_ref=source,
        dst_ref=target,
        send_sem=send,
        recv_sem=recv,
        device_id=device,
        device_id_type=MESH,
    )


class Gather:
    def __init__(self, place, slots, source, send, recv, pair, halves=True):
        self.place, self.slots, self.source = place, slots, source
        self.send, self.recv, self.pair_sems, self.halves = send, recv, pair, halves

    def slot(self, owner):
        return self.slots.at[owner, self.place.core] if self.halves else self.slots.at[owner]

    def own_copies(self):
        place = self.place
        peers = [place.line_peer(d) for d in range(1, place.lines)]
        peers += [place.plane_peer(e) for e in range(1, PLANE)]
        return [
            remote(
                self.source, self.slot(place.owner), self.send.at[i], self.recv.at[place.owner], peer
            )
            for i, peer in enumerate(peers)
        ]

    def onward(self, d):
        place = self.place
        owner = place.line_turn(-d) * PLANE + place.spot
        first = place.lines + PLANE - 2 + (d - 1) * (PLANE - 1)
        return [
            remote(
                self.slot(owner),
                self.slot(owner),
                self.send.at[first + e - 1],
                self.recv.at[owner],
                place.plane_peer(e),
            )
            for e in range(1, PLANE)
        ]

    def start(self):
        for copy in self.own_copies():
            copy.start()

    def forward(self):
        for d in range(1, self.place.lines):
            copies = self.onward(d)
            copies[0].wait_recv()
            for copy in copies:
                copy.start()

    def finish(self):
        place = self.place
        for d in range(place.lines):
            for e in range(1, PLANE):
                owner = place.line_turn(d) * PLANE + place.spot_turn(-e)
                remote(
                    self.slot(owner),
                    self.slot(owner),
                    self.send.at[0],
                    self.recv.at[owner],
                    place.plane_peer(e),
                ).wait_recv()
        for copy in self.own_copies():
            copy.wait_send()
        for d in range(1, place.lines):
            for copy in self.onward(d):
                copy.wait_send()

    def pair(self):
        half = self.slots.at[:, self.place.core]
        return remote(half, half, self.pair_sems.at[0], self.pair_sems.at[1], self.place.sibling())


class Scatter:
    def __init__(self, place, terms, got, chip, plane_got, line_out, line_got, result, sems):
        self.place, self.terms, self.got, self.chip = place, terms, got, chip
        self.plane_got, self.line_out, self.line_got = plane_got, line_out, line_got
        self.result, self.sems = result, sems

    def pair(self):
        place = self.place
        return remote(
            self.terms.at[:, 1 - place.core],
            self.got,
            self.sems.at[0, 0],
            self.sems.at[1, 0],
            place.sibling(),
        )

    def plane(self):
        place = self.place
        return [
            remote(
                self.chip.at[:, place.spot_turn(e)],
                self.plane_got.at[e - 1],
                self.sems.at[0, e],
                self.sems.at[1, e],
                place.plane_peer(e),
            )
            for e in range(1, PLANE)
        ]

    def line(self):
        place = self.place
        return [
            remote(
                self.line_out.at[place.line_turn(d)],
                self.line_got.at[d - 1],
                self.sems.at[0, PLANE + d - 1],
                self.sems.at[1, PLANE + d - 1],
                place.line_peer(d),
            )
            for d in range(1, place.lines)
        ]

    def last(self):
        place = self.place
        half = self.result.at[place.core]
        k = PLANE + place.lines - 1
        return remote(half, half, self.sems.at[0, k], self.sems.at[1, k], place.sibling())

    def begin(self):
        self.pair().start()

    def to_plane(self):
        place = self.place
        self.pair().wait()

        def add(line, carry):
            for spot in range(PLANE):
                owner = line * PLANE + spot
                both = self.terms[owner, place.core].astype(F32) + self.got[owner].astype(F32)
                self.chip[line, spot] = both.astype(BF16)
            return carry

        lax.fori_loop(0, place.lines, add, 0)
        for copy in self.plane():
            copy.start()

    def to_line(self):
        place = self.place
        for copy in self.plane():
            copy.wait()

        def add(line, carry):
            total = self.chip[line, place.spot].astype(F32)
            for e in range(PLANE - 1):
                total = total + self.plane_got[e, line].astype(F32)
            self.line_out[line] = total.astype(BF16)
            return carry

        lax.fori_loop(0, place.lines, add, 0)
        for copy in self.line():
            copy.start()

    def to_sibling(self):
        place = self.place
        for copy in self.line():
            copy.wait()
        total = self.line_out[place.line].astype(F32)
        for d in range(place.lines - 1):
            total = total + self.line_got[d].astype(F32)
        self.result[place.core] = total
        self.last().start()

    def end(self):
        self.last().wait()


class TailScatter:
    def __init__(self, place, own, plane_got, line_out, line_got, mine, other, sems):
        self.place, self.own, self.plane_got, self.line_out = place, own, plane_got, line_out
        self.line_got, self.mine, self.other, self.sems = line_got, mine, other, sems

    def plane(self):
        place = self.place
        return [
            remote(
                self.own.at[place.spot_turn(e)],
                self.plane_got.at[e - 1],
                self.sems.at[0, e],
                self.sems.at[1, e],
                place.plane_peer(e),
            )
            for e in range(1, PLANE)
        ]

    def line(self):
        place = self.place
        return [
            remote(
                self.line_out.at[place.line_turn(d)],
                self.line_got.at[d - 1],
                self.sems.at[0, PLANE + d - 1],
                self.sems.at[1, PLANE + d - 1],
                place.line_peer(d),
            )
            for d in range(1, place.lines)
        ]

    def last(self):
        return remote(
            self.mine, self.other, self.sems.at[0, 0], self.sems.at[1, 0], self.place.sibling()
        )

    def begin(self):
        for copy in self.plane():
            copy.start()

    def to_line(self):
        place = self.place
        for copy in self.plane():
            copy.wait()
        total = self.own[place.spot]
        for e in range(PLANE - 1):
            total = total + self.plane_got[e]
        for line in range(place.lines):
            self.line_out[line, 0] = total[line]
            self.line_out[line, 1] = total[place.lines]
        for copy in self.line():
            copy.start()

    def to_sibling(self):
        place = self.place
        for copy in self.line():
            copy.wait()
        total = self.line_out[place.line]
        for d in range(place.lines - 1):
            total = total + self.line_got[d]
        self.mine[...] = total
        self.last().start()

    def end(self):
        self.last().wait()
        return self.mine[...] + self.other[...]


def hop_states(counts_ref, adjacency_ref, features_ref, stacked_ref):
    clusters, slots = adjacency_ref.shape[:2]
    per_cluster = slots // NODES_PER_TILE
    links = []
    states = []
    for cluster in range(clusters):
        count = counts_ref[cluster]
        links.append(link_of(adjacency_ref[cluster], count))
        states.append(
            features_ref[cluster * slots : (cluster + 1) * slots].astype(F32)
            * live_rows(count, 0, slots)
        )
    for index in range(HOP_TOKENS):
        for cluster in range(clusters):
            if index > 0:
                states[cluster] = hop(*links[cluster], states[cluster])
            rounded = states[cluster].astype(BF16)
            for part in range(per_cluster):
                stacked_ref[cluster * per_cluster + part, index] = rounded[
                    part * NODES_PER_TILE : (part + 1) * NODES_PER_TILE
                ]


def embed_tile(step, stacked_ref, embed, gain, shift, hidden_keep, normed_keep, hidden_ref, normed_ref):
    stacked = stacked_ref[step].reshape(TOKENS, stacked_ref.shape[-1])
    hidden = dot(stacked, embed)
    hidden_keep[step] = hidden
    hidden_ref[...] = hidden
    normal, _ = norm_stats(hidden)
    normed = (normal * gain + shift).astype(BF16)
    normed_keep[step] = normed
    normed_ref[...] = normed


def attend_tile(tile, hidden_keep, normed_keep, attend, merge_of, triple_ref, mixed_ref, second_ref):
    width = hidden_keep.shape[-1]
    triple_ref[...] = dot(normed_keep[tile], attend).astype(BF16).reshape(triple_ref.shape)
    first_half = head_masks()
    keep = same_node()

    def group_step(group, carry):
        for first in range(0, width, 2 * HEAD):
            queries = read_block(triple_ref, group, first)
            keys = pair_stack(read_block(triple_ref, group, width + first), first_half)
            values = pair_stack(read_block(triple_ref, group, 2 * width + first), first_half)
            probs = pair_probs(queries, keys, keep)
            rounded = jnp.concatenate([half.astype(BF16) for half in probs], axis=1)
            write_block(mixed_ref, group, first, dot(rounded, values).astype(BF16))
        return carry

    lax.fori_loop(0, NODES_PER_TILE // GROUP, group_step, 0)
    mixed = mixed_ref[...].reshape(TOKENS, width)
    second_ref[...] = hidden_keep[tile] + dot(mixed, merge_of())


def spread_vectors(small, owners, width):
    rows = small.shape[0]
    lane = lax.broadcasted_iota(jnp.int32, (128, width), 0)
    column = lax.broadcasted_iota(jnp.int32, (128, width), 1)
    row = lax.broadcasted_iota(jnp.int32, (rows, width), 0)
    place = lax.broadcasted_iota(jnp.int32, (rows, width), 1)
    piece = width // owners
    pieces = dot(small, jnp.where(lane == column % piece, 1.0, 0.0).astype(BF16))
    out = []
    for vector in range(4):
        mine = jnp.logical_and(row % 8 == vector, lax.div(row, 8) == lax.div(place, piece))
        out.append(jnp.sum(jnp.where(mine, pieces, 0.0), axis=0, keepdims=True))
    pieces = dot(small, jnp.where(lane == column % (2 * piece), 1.0, 0.0).astype(BF16))
    for first in (0, owners // 2):
        owner = lax.div(place, 2 * piece) + first
        mine = jnp.logical_and(row % 8 == 4, lax.div(row, 8) == owner)
        out.append(jnp.sum(jnp.where(mine, pieces, 0.0), axis=0, keepdims=True))
    return jnp.concatenate(out + [jnp.zeros((2, width), F32)], axis=0)


def forward_kernel(
    lines,
    counts_ref,
    adjacency_ref,
    features_ref,
    embed_shard,
    vector_a,
    vector_b,
    vector_c,
    vector_d,
    vector_e,
    attend_shard,
    merge_shard,
    expand_shard,
    reduce_shard,
    stacked_ref,
    hidden_ref,
    normed_ref,
    triple_ref,
    mixed_ref,
    second_ref,
    rows_ref,
    embed_ref,
    attend_out,
    merge_out,
    expand_slots,
    reduce_slots,
    small_keep,
    head_slots,
    attend_slots,
    merge_slots,
    hidden_keep,
    normed_keep,
    send,
    recv,
    pair,
    local,
):
    step = pl.program_id(0)
    tiles = hidden_keep.shape[0]
    owners = head_slots.shape[0]
    width = hidden_keep.shape[-1]
    place = Place(lines)
    core, owner = place.core, place.owner

    def half_of(shard):
        rows = shard.shape[0] // 2
        return shard.at[pl.ds(pl.multiple_of(core * rows, rows), rows)]

    def gather(index, slots, source, halves=True):
        return Gather(
            place, slots, source, send.at[index], recv.at[index], pair.at[index], halves
        )

    head = gather(0, head_slots, head_slots.at[owner], False)
    attend = gather(1, attend_slots, half_of(attend_shard))
    merge = gather(2, merge_slots, half_of(merge_shard))
    expand = gather(3, expand_slots, half_of(expand_shard))
    reducer = gather(4, reduce_slots, half_of(reduce_shard))
    own_copies = [
        pltpu.make_async_copy(half_of(shard), slots.at[owner, core], local.at[index])
        for index, (shard, slots) in enumerate(
            ((expand_shard, expand_slots), (reduce_shard, reduce_slots))
        )
    ]
    out_copies = [
        pltpu.make_async_copy(attend_slots, attend_out, local.at[2]),
        pltpu.make_async_copy(merge_slots, merge_out, local.at[3]),
    ]

    @pl.when(step == 0)
    def _():
        place.greet()
        small_keep[...] = jnp.zeros_like(small_keep)
        for index, vector in enumerate((vector_a, vector_b, vector_c, vector_d, vector_e)):
            length = vector.shape[0]
            small_keep[index : index + 1, 0:length] = vector[...].astype(F32).reshape(1, length)
        mine = embed_shard[...].astype(F32)
        half_width = width // 2
        packed = jnp.concatenate(
            [
                jnp.concatenate([mine[:, :half_width], small_keep[...]], axis=1),
                jnp.concatenate([mine[:, half_width:], jnp.zeros((8, 128), F32)], axis=1),
            ],
            axis=0,
        )
        head_slots[owner] = packed.astype(BF16)
        attend_slots[owner, core] = half_of(attend_shard)[...]
        merge_slots[owner, core] = half_of(merge_shard)[...]
        hop_states(counts_ref, adjacency_ref, features_ref, stacked_ref)
        place.greeted()
        head.start()
        attend.start()
        merge.start()
        for copy in own_copies:
            copy.start()
        head.forward()
        head.finish()
        whole_head = head_slots[...].astype(F32)
        top = whole_head[:, 0:8].reshape(owners * 8, half_width + 128)
        bottom = whole_head[:, 8:16].reshape(owners * 8, half_width + 128)
        embed_ref[:, :half_width] = top[:, :half_width].astype(BF16)
        embed_ref[:, half_width:] = bottom[:, :half_width].astype(BF16)
        rows_ref[...] = spread_vectors(top[:, half_width:].astype(BF16), owners, width)
        attend.forward()
        merge.forward()

    @pl.when(step < tiles)
    def _():
        embed_tile(
            step,
            stacked_ref,
            embed_ref[...],
            rows_ref[0:1],
            rows_ref[1:2],
            hidden_keep,
            normed_keep,
            hidden_ref,
            normed_ref,
        )

    @pl.when(step == tiles - 1)
    def _():
        attend.finish()
        attend.pair().start()
        merge.finish()
        merge.pair().start()
        for copy in own_copies:
            copy.wait()
        expand.start()
        reducer.start()
        attend.pair().wait()
        merge.pair().wait()
        for copy in out_copies:
            copy.start()

    @pl.when(step == tiles + 1)
    def _():
        expand.forward()
        reducer.forward()

    @pl.when(step == 2 * tiles - 2)
    def _():
        expand.finish()
        expand.pair().start()
        reducer.finish()
        reducer.pair().start()

    @pl.when(step >= tiles)
    def _():
        attend_tile(
            step - tiles,
            hidden_keep,
            normed_keep,
            attend_slots[...].reshape(width, 3 * width),
            lambda: merge_slots[...].reshape(width, width),
            triple_ref,
            mixed_ref,
            second_ref,
        )

    @pl.when(step == 2 * tiles - 1)
    def _():
        expand.pair().wait()
        reducer.pair().wait()
        for copy in out_copies:
            copy.wait()


def forward_alone_kernel(
    counts_ref,
    adjacency_ref,
    features_ref,
    rows_ref,
    embed_ref,
    attend_ref,
    merge_ref,
    stacked_ref,
    hidden_ref,
    normed_ref,
    triple_ref,
    mixed_ref,
    second_ref,
    hidden_keep,
    normed_keep,
):
    step = pl.program_id(0)
    tiles = hidden_keep.shape[0]
    width = hidden_keep.shape[-1]

    @pl.when(step == 0)
    def _():
        hop_states(counts_ref, adjacency_ref, features_ref, stacked_ref)

    @pl.when(step < tiles)
    def _():
        embed_tile(
            step,
            stacked_ref,
            embed_ref[...],
            rows_ref[0:1],
            rows_ref[1:2],
            hidden_keep,
            normed_keep,
            hidden_ref,
            normed_ref,
        )

    @pl.when(step >= tiles)
    def _():
        attend_tile(
            step - tiles,
            hidden_keep,
            normed_keep,
            attend_ref[...].reshape(width, 3 * width),
            lambda: merge_ref[...].reshape(width, width),
            triple_ref,
            mixed_ref,
            second_ref,
        )


def middle_kernel(
    counts_ref,
    second_ref,
    mixed_ref,
    cotangent_ref,
    rows_ref,
    expand_ref,
    reduce_ref,
    output_ref,
    grad_second_ref,
    terms_ref,
    rows_grad_ref,
    grad_merge_ref,
    grad_expand_ref,
    grad_reduce_ref,
):
    step = pl.program_id(0)
    width = second_ref.shape[-1]
    per_cluster = 128 // NODES_PER_TILE
    gain, shift = rows_ref[2:3], rows_ref[3:4]
    expand = expand_ref[...].reshape(width, expand_ref.shape[-1])
    reducer = reduce_ref[...].reshape(expand_ref.shape[-1], width)

    @pl.when(step == 0)
    def _():
        for ref in (rows_grad_ref, grad_merge_ref, grad_expand_ref, grad_reduce_ref):
            ref[...] = jnp.zeros_like(ref)

    second = second_ref[...]
    normal, inv = norm_stats(second)
    inner = (normal * gain + shift).astype(BF16)
    before = dot(inner, expand)
    square = before * before
    curve = jnp.tanh(GELU_A * before * (1.0 + GELU_B * square))
    after = (0.5 * before * (1.0 + curve)).astype(BF16)
    slope = 0.5 * (1.0 + curve) + (0.5 * GELU_A) * before * (1.0 - curve * curve) * (
        1.0 + (3.0 * GELU_B) * square
    )
    third = second + dot(after, reducer)
    shaped = third.reshape(HOP_TOKENS, NODES_PER_TILE, width)
    keep = live_rows(
        counts_ref[step // per_cluster], (step % per_cluster) * NODES_PER_TILE, NODES_PER_TILE
    )
    centre = shaped[0]
    row_node = rows_ref[4:5]
    row_hop = rows_ref[5:6]
    base = jnp.sum(centre * row_node, axis=-1, keepdims=True)
    logits = [
        base + jnp.sum(shaped[k] * row_hop, axis=-1, keepdims=True) for k in range(1, HOP_TOKENS)
    ]
    top = functools.reduce(jnp.maximum, logits)
    powers = [jnp.exp(logit - top) for logit in logits]
    scale = 1.0 / functools.reduce(jnp.add, powers)
    shares = [power * scale for power in powers]
    total = centre
    for k in range(1, HOP_TOKENS):
        total = total + shares[k - 1] * shaped[k]
    output_ref[...] = total * keep
    cotangent = cotangent_ref[...] * keep
    grad_shares = [
        jnp.sum(cotangent * shaped[k], axis=-1, keepdims=True) for k in range(1, HOP_TOKENS)
    ]
    mean_share = functools.reduce(jnp.add, [s * g for s, g in zip(shares, grad_shares)])
    grad_logits = [s * (g - mean_share) for s, g in zip(shares, grad_shares)]
    grad_base = functools.reduce(jnp.add, grad_logits)
    parts = [cotangent + grad_base * row_node]
    read_hop = jnp.zeros((NODES_PER_TILE, width), F32)
    for k in range(1, HOP_TOKENS):
        parts.append(shares[k - 1] * cotangent + grad_logits[k - 1] * row_hop)
        read_hop = read_hop + grad_logits[k - 1] * shaped[k]
    rows_grad_ref[4:5] += jnp.sum(grad_base * centre, axis=0, keepdims=True)
    rows_grad_ref[5:6] += jnp.sum(read_hop, axis=0, keepdims=True)
    grad_third = jnp.concatenate(parts, axis=0)
    grad_branch = grad_third.astype(BF16)
    grad_reduce_ref[...] += dot_lead(after, grad_branch)
    grad_before = (slope * dot_last(grad_branch, reducer)).astype(BF16)
    grad_expand_ref[...] += dot_lead(inner, grad_before)
    grad_inner = dot_last(grad_before, expand)
    rows_grad_ref[2:3] += jnp.sum(grad_inner * normal, axis=0, keepdims=True)
    rows_grad_ref[3:4] += jnp.sum(grad_inner, axis=0, keepdims=True)
    grad_normal = grad_inner * gain
    grad_second = grad_third + inv * (
        grad_normal
        - jnp.mean(grad_normal, axis=-1, keepdims=True)
        - normal * jnp.mean(grad_normal * normal, axis=-1, keepdims=True)
    )
    grad_second_ref[...] = grad_second
    grad_merge_ref[...] += dot_lead(mixed_ref[...].reshape(TOKENS, width), grad_second.astype(BF16))

    @pl.when(step == pl.num_programs(0) - 1)
    def _():
        spread = expand_ref.shape[-1]
        wide = grad_expand_ref[...].astype(BF16).reshape(PACK, 2, width // PACK // 2, spread)
        deep = grad_reduce_ref[...].astype(BF16).reshape(PACK, 2, spread // PACK // 2, width)
        square = grad_merge_ref[...].astype(BF16).reshape(PACK, 2, width // PACK // 2, width)
        terms_ref[:, :, 0:16] = wide[..., :width]
        terms_ref[:, :, 16:32] = wide[..., width:]
        terms_ref[:, :, 32:64] = deep
        terms_ref[:, :, 64:80] = square


def attend_back_tile(
    tile, triple_ref, normed_ref, grad_second_ref, merge, grad_mixed_ref, grad_triple_ref, grad_attend_ref
):
    width = normed_ref.shape[-1]
    grad_mixed = dot_last(grad_second_ref[...].astype(BF16), merge).astype(BF16)
    grad_mixed_ref[...] = grad_mixed.reshape(grad_mixed_ref.shape)
    first_half = head_masks()
    keep = same_node()
    span = GROUP * HOP_TOKENS
    out_ref = grad_triple_ref.at[tile]

    def group_step(group, carry):
        for first in range(0, width, 2 * HEAD):
            queries = read_block(triple_ref, group, first)
            keys = pair_stack(read_block(triple_ref, group, width + first), first_half)
            values = pair_stack(read_block(triple_ref, group, 2 * width + first), first_half)
            out_grad = read_block(grad_mixed_ref, group, first)
            probs = pair_probs(queries, keys, keep)
            grad_probs = dot_last(out_grad, values)
            grad_halves = []
            for half in range(2):
                part = grad_probs[:, half * span : (half + 1) * span]
                weighted = probs[half] * part
                grad_halves.append(
                    (weighted - probs[half] * jnp.sum(weighted, axis=-1, keepdims=True)).astype(
                        BF16
                    )
                )
            grad_scores = jnp.concatenate(grad_halves, axis=1)
            grad_query = dot(grad_scores, keys) * HEAD ** (-0.5)
            grad_key = dot_lead(
                jnp.concatenate(grad_halves, axis=0), pair_stack(queries, first_half)
            ) * HEAD ** (-0.5)
            grad_value = dot_lead(
                jnp.concatenate([half.astype(BF16) for half in probs], axis=0),
                pair_stack(out_grad, first_half),
            )
            write_block(out_ref, group, first, grad_query.astype(BF16))
            write_block(out_ref, group, width + first, grad_key.astype(BF16))
            write_block(out_ref, group, 2 * width + first, grad_value.astype(BF16))
        return carry

    lax.fori_loop(0, NODES_PER_TILE // GROUP, group_step, 0)
    grad_triple = out_ref[...].reshape(TOKENS, 3 * width)
    grad_attend_ref[...] += dot_lead(normed_ref[...], grad_triple)


def embed_back_tile(
    tile,
    hidden_ref,
    stacked_ref,
    grad_second_ref,
    grad_triple_ref,
    attend,
    embed,
    gain,
    rows_keep,
    grad_embed_ref,
    grad_stacked_ref,
):
    grad_triple = grad_triple_ref[tile].reshape(TOKENS, grad_triple_ref.shape[-1])
    grad_normed = dot_last(grad_triple, attend)
    normal, inv = norm_stats(hidden_ref[...])
    rows_keep[0:1] += jnp.sum(grad_normed * normal, axis=0, keepdims=True)
    rows_keep[1:2] += jnp.sum(grad_normed, axis=0, keepdims=True)
    grad_normal = grad_normed * gain
    grad_hidden = grad_second_ref[...] + inv * (
        grad_normal
        - jnp.mean(grad_normal, axis=-1, keepdims=True)
        - normal * jnp.mean(grad_normal * normal, axis=-1, keepdims=True)
    )
    grad_hidden = grad_hidden.astype(BF16)
    stacked = stacked_ref[...].reshape(TOKENS, stacked_ref.shape[-1])
    grad_embed_ref[...] += dot_lead(stacked, grad_hidden)
    grad_stacked_ref[tile] = dot_last(grad_hidden, embed).reshape(grad_stacked_ref.shape[1:])


def hop_back(counts_ref, adjacency_ref, grad_stacked_ref, grad_features_ref, between):
    clusters, slots = adjacency_ref.shape[:2]
    per_cluster = slots // NODES_PER_TILE
    links = []
    states = []

    def hop_grad(cluster, index):
        return jnp.concatenate(
            [grad_stacked_ref[cluster * per_cluster + p, index] for p in range(per_cluster)],
            axis=0,
        )

    for cluster in range(clusters):
        links.append(link_of(adjacency_ref[cluster], counts_ref[cluster]))
        states.append(hop_grad(cluster, HOPS))
    for index in range(HOPS - 1, -1, -1):
        for cluster in range(clusters):
            states[cluster] = hop_grad(cluster, index) + hop(*links[cluster], states[cluster])
        if index in between:
            between[index]()
    for cluster in range(clusters):
        grad_features_ref[cluster * slots : (cluster + 1) * slots] = states[cluster] * live_rows(
            counts_ref[cluster], 0, slots
        )


def backward_kernel(
    lines,
    counts_ref,
    adjacency_ref,
    triple_ref,
    normed_ref,
    grad_second_ref,
    hidden_ref,
    stacked_ref,
    embed_ref,
    rows_ref,
    attend_ref,
    merge_ref,
    terms_ref,
    rows_grad_ref,
    grad_features_ref,
    middle_share_ref,
    attend_share_ref,
    tail_share_ref,
    grad_mixed_ref,
    grad_triple_ref,
    grad_stacked_ref,
    grad_attend_ref,
    grad_embed_ref,
    rows_keep,
    middle_got,
    middle_chip,
    middle_plane,
    middle_line_out,
    middle_line,
    middle_result,
    attend_terms,
    attend_got,
    attend_chip,
    attend_plane,
    attend_line_out,
    attend_line,
    attend_result,
    tail_own,
    tail_plane,
    tail_line_out,
    tail_line,
    tail_mine,
    tail_other,
    middle_sems,
    attend_sems,
    tail_sems,
):
    step = pl.program_id(0)
    tiles = grad_triple_ref.shape[0]
    width = hidden_ref.shape[-1]
    place = Place(lines)
    middle = Scatter(
        place,
        terms_ref,
        middle_got,
        middle_chip,
        middle_plane,
        middle_line_out,
        middle_line,
        middle_result,
        middle_sems,
    )
    attend = Scatter(
        place,
        attend_terms,
        attend_got,
        attend_chip,
        attend_plane,
        attend_line_out,
        attend_line,
        attend_result,
        attend_sems,
    )
    tail = TailScatter(
        place, tail_own, tail_plane, tail_line_out, tail_line, tail_mine, tail_other, tail_sems
    )

    @pl.when(step == 0)
    def _():
        place.greet()
        rows_keep[...] = rows_grad_ref[...]
        grad_attend_ref[...] = jnp.zeros_like(grad_attend_ref)
        grad_embed_ref[...] = jnp.zeros_like(grad_embed_ref)

    @pl.when(step < tiles)
    def _():
        attend_back_tile(
            step,
            triple_ref,
            normed_ref,
            grad_second_ref,
            merge_ref[...].reshape(width, width),
            grad_mixed_ref,
            grad_triple_ref,
            grad_attend_ref,
        )

    @pl.when(step >= tiles)
    def _():
        embed_back_tile(
            step - tiles,
            hidden_ref,
            stacked_ref,
            grad_second_ref,
            grad_triple_ref,
            attend_ref[...].reshape(width, 3 * width),
            embed_ref[...],
            rows_ref[0:1],
            rows_keep,
            grad_embed_ref,
            grad_stacked_ref,
        )

    @pl.when(step == 0)
    def _():
        place.greeted()
        middle.begin()

    @pl.when(step == 1)
    def _():
        middle.to_plane()

    @pl.when(step == 3)
    def _():
        middle.to_line()

    @pl.when(step == 4)
    def _():
        middle.to_sibling()

    @pl.when(step == tiles - 1)
    def _():
        middle.end()
        attend_terms[...] = grad_attend_ref[...].astype(BF16).reshape(attend_terms.shape)
        attend.begin()

    @pl.when(step == tiles)
    def _():
        attend.to_plane()

    @pl.when(step == tiles + 2)
    def _():
        attend.to_line()

    @pl.when(step == tiles + 4)
    def _():
        attend.to_sibling()

    @pl.when(step == 2 * tiles - 1)
    def _():
        attend.end()
        own = grad_embed_ref[...].reshape(lines, PLANE, 8, width)
        for spot in range(PLANE):
            tail_own[spot, 0:lines] = own[:, spot]
            tail_own[spot, lines] = rows_keep[...]
        tail.begin()
        hop_back(
            counts_ref,
            adjacency_ref,
            grad_stacked_ref,
            grad_features_ref,
            {4: tail.to_line, 1: tail.to_sibling},
        )
        middle_share_ref[...] = middle_result[...]
        attend_share_ref[...] = attend_result[...]
        tail_share_ref[...] = tail.end()


def backward_alone_kernel(
    counts_ref,
    adjacency_ref,
    triple_ref,
    normed_ref,
    grad_second_ref,
    hidden_ref,
    stacked_ref,
    embed_ref,
    rows_ref,
    attend_ref,
    merge_ref,
    rows_grad_ref,
    grad_features_ref,
    grad_attend_ref,
    grad_embed_ref,
    rows_keep,
    grad_mixed_ref,
    grad_triple_ref,
    grad_stacked_ref,
):
    step = pl.program_id(0)
    tiles = grad_triple_ref.shape[0]
    width = hidden_ref.shape[-1]

    @pl.when(step == 0)
    def _():
        rows_keep[...] = rows_grad_ref[...]
        grad_attend_ref[...] = jnp.zeros_like(grad_attend_ref)
        grad_embed_ref[...] = jnp.zeros_like(grad_embed_ref)

    @pl.when(step < tiles)
    def _():
        attend_back_tile(
            step,
            triple_ref,
            normed_ref,
            grad_second_ref,
            merge_ref[...].reshape(width, width),
            grad_mixed_ref,
            grad_triple_ref,
            grad_attend_ref,
        )

    @pl.when(step >= tiles)
    def _():
        embed_back_tile(
            step - tiles,
            hidden_ref,
            stacked_ref,
            grad_second_ref,
            grad_triple_ref,
            attend_ref[...].reshape(width, 3 * width),
            embed_ref[...],
            rows_ref[0:1],
            rows_keep,
            grad_embed_ref,
            grad_stacked_ref,
        )

    @pl.when(step == 2 * tiles - 1)
    def _():
        hop_back(counts_ref, adjacency_ref, grad_stacked_ref, grad_features_ref, {})


def unpack_kernel(
    middle_ref,
    attend_ref,
    tail_ref,
    features_ref,
    grad_features_ref,
    grad_embed_ref,
    grad_gain_one,
    grad_shift_one,
    grad_attend,
    grad_merge,
    grad_gain_two,
    grad_shift_two,
    grad_expand,
    grad_reduce,
    grad_readout,
):
    owner = lax.axis_index("fsdp")
    width = middle_ref.shape[-1]
    grad_features_ref[...] = features_ref[...]
    for half in range(2):
        grad_attend[half * 16 : half * 16 + 16] = attend_ref[half]
        grad_expand[half * 16 : half * 16 + 16, 0:width] = middle_ref[half, 0:16]
        grad_expand[half * 16 : half * 16 + 16, width : 2 * width] = middle_ref[half, 16:32]
        grad_reduce[half * 32 : half * 32 + 32] = middle_ref[half, 32:64]
        grad_merge[half * 16 : half * 16 + 16] = middle_ref[half, 64:80]
    grad_embed_ref[...] = tail_ref[0]
    rows = tail_ref[1]
    length = grad_gain_one.shape[0]
    turned = pltpu.roll(rows, lax.rem(width - owner * length, width), 1)
    for index, ref in enumerate((grad_gain_one, grad_shift_one, grad_gain_two, grad_shift_two)):
        ref[...] = turned[index : index + 1, 0:length].reshape(length)
    length = grad_readout.shape[0]
    first = owner * length
    turned = pltpu.roll(rows, lax.rem(2 * width - first, width), 1)
    row = jnp.where(first < width, turned[4:5, 0:length], turned[5:6, 0:length])
    grad_readout[...] = row.reshape(length)


def whole(shape):
    return pl.BlockSpec(shape, lambda t: (0,) * len(shape), pipeline_mode=pl.Buffered(1))


def kept(shape):
    return pl.BlockSpec(shape, lambda t: (0,) * len(shape))


def tiled(*shape, at=lambda t: t):
    return pl.BlockSpec((None,) + shape, lambda t: (at(t),) + (0,) * len(shape))


def rows_of(*shape, at=lambda t: t):
    return pl.BlockSpec(shape, lambda t: (at(t),) + (0,) * (len(shape) - 1))


def sds(shape, dtype):
    return jax.ShapeDtypeStruct(shape, dtype)


SMEM_SPEC = pl.BlockSpec(memory_space=pltpu.SMEM)


VMEM_SPEC = pl.BlockSpec(memory_space=pltpu.VMEM)
ANY_SPEC = pl.BlockSpec(memory_space=pl.ANY)


def params(collective=None):
    more = {} if collective is None else {"collective_id": collective, "has_side_effects": True}
    return pltpu.CompilerParams(
        vmem_limit_bytes=56 * MIB, dimension_semantics=("arbitrary",), **more
    )


def forward_outs(tiles, feat, width):
    hops, per = HOP_TOKENS, NODES_PER_TILE
    early = lambda t: jnp.minimum(t, tiles - 1)
    late = lambda t: jnp.maximum(t - tiles, 0)
    out_specs = [
        kept((tiles, hops, per, feat)),
        tiled(TOKENS, width, at=early),
        tiled(TOKENS, width, at=early),
        rows_of(hops, per, 3 * width, at=late),
        rows_of(hops, per, width, at=late),
        tiled(TOKENS, width, at=late),
    ]
    out_shape = [
        sds((tiles, hops, per, feat), BF16),
        sds((tiles, TOKENS, width), F32),
        sds((tiles, TOKENS, width), BF16),
        sds((tiles * hops, per, 3 * width), BF16),
        sds((tiles * hops, per, width), BF16),
        sds((tiles, TOKENS, width), F32),
    ]
    keep = [pltpu.VMEM((tiles, TOKENS, width), F32), pltpu.VMEM((tiles, TOKENS, width), BF16)]
    return out_specs, out_shape, keep


def forward_part(
    lines, counts, adjacency, features, embed, vectors, attend, merge, expand, reducer
):
    nodes, feat = features.shape
    owners = lines * PLANE
    width = merge.shape[1]
    tiles = nodes // NODES_PER_TILE
    out_specs, out_shape, keep = forward_outs(tiles, feat, width)
    half = lambda shard: (owners, 2, shard.shape[0] // 2, shard.shape[1])
    copies = lines + PLANE - 2 + (lines - 1) * (PLANE - 1)
    return pl.pallas_call(
        functools.partial(forward_kernel, lines),
        grid=(2 * tiles,),
        in_specs=[SMEM_SPEC, whole(adjacency.shape), whole(features.shape)]
        + [VMEM_SPEC] * 6
        + [whole(attend.shape), whole(merge.shape), ANY_SPEC, ANY_SPEC],
        out_specs=out_specs + [kept((8, width)), kept((feat, width))] + [ANY_SPEC] * 4,
        out_shape=out_shape
        + [sds((8, width), F32), sds((feat, width), BF16)]
        + [sds(half(shard), BF16) for shard in (attend, merge, expand, reducer)],
        scratch_shapes=[
            pltpu.VMEM((8, 128), F32),
            pltpu.VMEM((owners, 16, width // 2 + 128), BF16),
            pltpu.VMEM(half(attend), BF16),
            pltpu.VMEM(half(merge), BF16),
        ]
        + keep
        + [
            pltpu.SemaphoreType.DMA((5, copies)),
            pltpu.SemaphoreType.DMA((5, owners)),
            pltpu.SemaphoreType.DMA((5, 2)),
            pltpu.SemaphoreType.DMA((4,)),
        ],
        compiler_params=params(0),
        name="hops_attention",
    )(counts, adjacency, features, embed, *vectors, attend, merge, expand, reducer)


def forward_alone_part(counts, adjacency, features, rows, embed, attend, merge):
    nodes, feat = features.shape
    width = merge.shape[-1]
    tiles = nodes // NODES_PER_TILE
    out_specs, out_shape, keep = forward_outs(tiles, feat, width)
    return pl.pallas_call(
        forward_alone_kernel,
        grid=(2 * tiles,),
        in_specs=[SMEM_SPEC]
        + [whole(a.shape) for a in (adjacency, features, rows, embed, attend, merge)],
        out_specs=out_specs,
        out_shape=out_shape,
        scratch_shapes=keep,
        compiler_params=params(),
        name="hops_attention_alone",
    )(counts, adjacency, features, rows, embed, attend, merge)


def middle_part(counts, second, mixed, cotangent, rows, expand, reducer):
    tiles, _, width = second.shape
    hops, per = HOP_TOKENS, NODES_PER_TILE
    spread = expand.shape[-1]
    terms = (PACK, 2, 80, width)
    return pl.pallas_call(
        middle_kernel,
        grid=(tiles,),
        in_specs=[
            SMEM_SPEC,
            tiled(TOKENS, width),
            rows_of(hops, per, width),
            rows_of(per, width),
            whole(rows.shape),
            whole(expand.shape),
            whole(reducer.shape),
        ],
        out_specs=[
            rows_of(per, width),
            tiled(TOKENS, width),
            kept(terms),
            kept(rows.shape),
        ],
        out_shape=[
            sds(cotangent.shape, F32),
            sds(second.shape, F32),
            sds(terms, BF16),
            sds(rows.shape, F32),
        ],
        scratch_shapes=[
            pltpu.VMEM((width, width), F32),
            pltpu.VMEM((width, spread), F32),
            pltpu.VMEM((spread, width), F32),
        ],
        compiler_params=params(),
        name="feed_forward",
    )(counts, second, mixed, cotangent, rows, expand, reducer)


def backward_ins(tiles, feat, width, arrays):
    hops, per = HOP_TOKENS, NODES_PER_TILE
    early = lambda t: jnp.minimum(t, tiles - 1)
    late = lambda t: jnp.maximum(t - tiles, 0)
    both = lambda t: lax.rem(t, tiles)
    return [
        SMEM_SPEC,
        whole(arrays[1].shape),
        rows_of(hops, per, 3 * width, at=early),
        tiled(TOKENS, width, at=early),
        tiled(TOKENS, width, at=both),
        tiled(TOKENS, width, at=late),
        tiled(hops, per, feat, at=late),
    ] + [whole(a.shape) for a in arrays[7:]]


def backward_part(lines, *arrays):
    tiles, _, width = arrays[3].shape
    hops, per, feat = arrays[6].shape[1:]
    owners = lines * PLANE
    rest = (80, width)
    wide = (width // owners // 2, 3 * width)

    def buffers(shape):
        return [
            pltpu.VMEM((owners,) + shape, BF16),
            pltpu.VMEM((lines, PLANE) + shape, BF16),
            pltpu.VMEM((PLANE - 1, lines) + shape, BF16),
            pltpu.VMEM((lines,) + shape, BF16),
            pltpu.VMEM((lines - 1,) + shape, BF16),
            pltpu.VMEM((2,) + shape, F32),
        ]

    sems = pltpu.SemaphoreType.DMA((2, PLANE + lines))
    outs = [(tiles * per, feat), (2,) + rest, (2,) + wide, (2, 8, width)]
    return pl.pallas_call(
        functools.partial(backward_kernel, lines),
        grid=(2 * tiles,),
        in_specs=backward_ins(tiles, feat, width, arrays),
        out_specs=[kept(shape) for shape in outs],
        out_shape=[sds(shape, F32) for shape in outs],
        scratch_shapes=[
            pltpu.VMEM((hops, per, width), BF16),
            pltpu.VMEM((tiles, hops, per, 3 * width), BF16),
            pltpu.VMEM((tiles, hops, per, feat), F32),
            pltpu.VMEM((width, 3 * width), F32),
            pltpu.VMEM((feat, width), F32),
            pltpu.VMEM((8, width), F32),
        ]
        + buffers(rest)
        + [pltpu.VMEM((owners, 2) + wide, BF16)]
        + buffers(wide)
        + [
            pltpu.VMEM((PLANE, lines + 1, 8, width), F32),
            pltpu.VMEM((PLANE - 1, lines + 1, 8, width), F32),
            pltpu.VMEM((lines, 2, 8, width), F32),
            pltpu.VMEM((lines - 1, 2, 8, width), F32),
            pltpu.VMEM((2, 8, width), F32),
            pltpu.VMEM((2, 8, width), F32),
        ]
        + [sems] * 3,
        compiler_params=params(1),
        name="attention_backward",
    )(*arrays)


def backward_alone_part(*arrays):
    tiles, _, width = arrays[3].shape
    hops, per, feat = arrays[6].shape[1:]
    outs = [(tiles * per, feat), (width, 3 * width), (feat, width), (8, width)]
    return pl.pallas_call(
        backward_alone_kernel,
        grid=(2 * tiles,),
        in_specs=backward_ins(tiles, feat, width, arrays),
        out_specs=[kept(shape) for shape in outs],
        out_shape=[sds(shape, F32) for shape in outs],
        scratch_shapes=[
            pltpu.VMEM((hops, per, width), BF16),
            pltpu.VMEM((tiles, hops, per, 3 * width), BF16),
            pltpu.VMEM((tiles, hops, per, feat), F32),
        ],
        compiler_params=params(),
        name="attention_backward_alone",
    )(*arrays)


def unpack_part(middle, attend, tail, features, shapes):
    return pl.pallas_call(
        unpack_kernel,
        in_specs=[VMEM_SPEC] * 4,
        out_specs=[VMEM_SPEC] * 11,
        out_shape=[sds(features.shape, F32)] + [sds(shape, F32) for shape in shapes],
        compiler_params=pltpu.CompilerParams(vmem_limit_bytes=24 * MIB),
        name="unpack_shares",
    )(middle, attend, tail, features)


def gather(block):
    return lax.all_gather(block, "fsdp", axis=0, tiled=True)


def share(term):
    part = lax.psum_scatter(term.astype(BF16), "fsdp", scatter_dimension=0, tiled=True)
    return lax.psum(part.astype(F32), "grp")


def body(
    features,
    adjacency,
    counts,
    input_weight,
    first_gain,
    first_shift,
    attend_weight,
    merge_weight,
    second_gain,
    second_shift,
    expand_weight,
    reduce_weight,
    readout_weight,
    cotangent,
):
    vectors = (first_gain, first_shift, second_gain, second_shift, readout_weight)
    owners = lax.axis_size("fsdp")
    if owners % PLANE == 0 and input_weight.shape[0] == 8 and attend_weight.shape[0] == 32:
        lines = owners // PLANE
        (
            stacked,
            hidden,
            normed,
            triple,
            mixed,
            second,
            rows,
            embed,
            attend,
            merge,
            expand,
            reducer,
        ) = forward_part(
            lines,
            counts,
            adjacency,
            features,
            input_weight,
            vectors,
            attend_weight,
            merge_weight,
            expand_weight,
            reduce_weight,
        )
        output, grad_second, terms, rows_grad = middle_part(
            counts, second, mixed, cotangent, rows, expand, reducer
        )
        grad_features, *shares = backward_part(
            lines,
            counts,
            adjacency,
            triple,
            normed,
            grad_second,
            hidden,
            stacked,
            embed,
            rows,
            attend,
            merge,
            terms,
            rows_grad,
        )
        shapes = [
            weight.shape
            for weight in (
                input_weight,
                first_gain,
                first_shift,
                attend_weight,
                merge_weight,
                second_gain,
                second_shift,
                expand_weight,
                reduce_weight,
                readout_weight,
            )
        ]
        return (output, *unpack_part(*shares, grad_features, shapes))
    return body_apart(
        features,
        adjacency,
        counts,
        input_weight,
        vectors,
        attend_weight,
        merge_weight,
        expand_weight,
        reduce_weight,
        cotangent,
    )


def body_apart(
    features,
    adjacency,
    counts,
    input_weight,
    vectors,
    attend_weight,
    merge_weight,
    expand_weight,
    reduce_weight,
    cotangent,
):
    lengths = [v.shape[0] for v in vectors]
    places = [sum(lengths[:i]) for i in range(len(lengths) + 1)]
    packed = lax.all_gather(jnp.concatenate(vectors), "fsdp", axis=0, tiled=False)
    width = merge_weight.shape[1]
    full = [
        packed[:, places[i] : places[i + 1]].astype(F32).reshape(-1, width)
        for i in range(len(lengths))
    ]
    rows = jnp.concatenate(full + [jnp.zeros((2, width), F32)], axis=0)
    embed, attend, merge, expand, reducer = map(
        gather, (input_weight, attend_weight, merge_weight, expand_weight, reduce_weight)
    )
    stacked, hidden, normed, triple, mixed, second = forward_alone_part(
        counts, adjacency, features, rows, embed, attend, merge
    )
    output, grad_second, terms, rows_grad = middle_part(
        counts, second, mixed, cotangent, rows, expand, reducer
    )
    grad_features, grad_attend, grad_embed, rows_grad = backward_alone_part(
        counts,
        adjacency,
        triple,
        normed,
        grad_second,
        hidden,
        stacked,
        embed,
        rows,
        attend,
        merge,
        rows_grad,
    )
    spread = expand.shape[1]
    grad_expand = jnp.concatenate([terms[:, :, 0:16], terms[:, :, 16:32]], axis=-1)
    parts = lax.axis_size("fsdp")
    pieces = [rows_grad[i] for i in range(4)] + [rows_grad[4:6]]
    packed_grad = jnp.concatenate([piece.reshape(parts, -1) for piece in pieces], axis=1)
    packed_grad = lax.psum(
        lax.psum_scatter(packed_grad, "fsdp", scatter_dimension=0, tiled=True), "grp"
    ).reshape(-1)
    small = [packed_grad[places[i] : places[i + 1]] for i in range(len(lengths))]
    return (
        output,
        grad_features,
        share(grad_embed),
        small[0],
        small[1],
        share(grad_attend),
        share(terms[:, :, 64:80].reshape(width, width)),
        small[2],
        small[3],
        share(grad_expand.reshape(width, spread)),
        share(terms[:, :, 32:64].reshape(spread, width)),
        small[4],
    )


def solution(mesh):
    nodes = ("grp", "fsdp")
    rows = P("fsdp", None)
    vector = P("fsdp")
    in_specs = (
        P(nodes, None),
        P(nodes, None, None),
        P(nodes),
        rows,
        vector,
        vector,
        rows,
        rows,
        vector,
        vector,
        rows,
        rows,
        vector,
        P(nodes, None),
    )
    out_specs = (
        P(nodes, None),
        P(nodes, None),
        rows,
        vector,
        vector,
        rows,
        rows,
        vector,
        vector,
        rows,
        rows,
        vector,
    )
    return jax.shard_map(body, mesh=mesh, in_specs=in_specs, out_specs=out_specs, check_vma=False)
```

time: 744 us -> 199 us (0.27)
  waiting for transfers between devices: 348 us -> 0 us
  blocking collectives: 208 us -> 0 us
  Pallas kernels: 149 us -> 194 us
  between operations: 14.9 us -> 0.68 us
  other arithmetic: 10.8 us -> 0 us
  local copies, waits for them, and re-layouts: 11.1 us -> 3.58 us
    reduce_scatter x5 -> x0, waiting for transfers between devices: 343 us -> none  [share(): lax.psum_scatter(term.astype(BF16), 'fsdp', scatter_dimension=0, tiled=True)]
    unnamed x2 -> x0, blocking collectives: 119 us -> none
    all_gather x2 -> x0, blocking collectives: 82.9 us -> none  [gather(): return lax.all_gather(block, 'fsdp', axis=0, tiled=True)]
    pallas_call x2 -> x3, Pallas kernels: 114 us -> 157 us  [the longest x1 96.9 us: backward_part(): pl.pallas_call(functools.partial(backward_kernel, lines), grid=(2 * tiles...]
    convert_element_type x7 -> x0, other arithmetic: 8.11 us -> none  [the longest x5 8.03 us: share(): term.astype(BF16)]
  transfers between devices with their start and end apart: 8 -> 0, of which waited for: 5 -> 0; matrix products, arithmetic and copies ran while one was open for 3% -> 0% of each run, Pallas kernels for 5% -> 0%
where the time goes in v2:
time: 199 us; the launch traced here: 198 us
  Pallas kernels  194 us (97%)
  local copies, waits for them, and re-layouts  3.58 us (2%)
    pallas_call x1, Pallas kernels, backward_part(): pl.pallas_call(functools.partial(backward_kernel, lines), grid=(2 * tiles...  96.9 us
    pallas_call x1, Pallas kernels, forward_part(): pl.pallas_call(functools.partial(forward_kernel, lines), grid=(2 * tiles,...  59.5 us
    pallas_call x1, Pallas kernels, middle_part(): pl.pallas_call(middle_kernel, grid=(tiles,), in_specs=[SMEM_SPEC, tiled(T...  36.8 us

profile of v2, /device:TPU:0, one launch (start us, length us, event | category | flops | bytes accessed | tf_op | source)
XLA Modules:
  0.0 198.4 jit_solution(3586726982382320533)
XLA Ops:
  0.6 59.5 %hops_attention.1 = (bf16[6,8,64,128]{3,2,1,0:T(8,128)(2,1)}, f32[6,512,512]{2,1,0:T(8,128)}, bf16[6,512,512]{2,1,0:T(8,128)(2,1)}, bf16[48,64,1536]{2,1,0:T(8,1...) custom-call(s32[3]{0:T(128)} %counts_ref.5, ...), custom_call_target="tpu_custom_call" | custom-call | tf_op jit(solution)/shard_map/hops_attention/pallas_call | solution.py:1239
  60.1 36.8 %feed_forward.1 = (f32[384,512]{1,0:T(8,128)}, f32[6,512,512]{2,1,0:T(8,128)}, bf16[16,2,80,512]{3,2,1,0:T(8,128)(2,1)}, f32[8,512]{1,0:T(8,128)}) custom-call(s32[3]{0:T(128)} %counts_ref.5, f32[6,512,512]{2,1,0:T(8,128)} %get-tuple-element.43.second_ref, bf16[48,64,512]{2,1,0:T(8,128)(2,1)} %get-tuple-element.44.mixed_ref, f32[384,512]{1,0:T(8,128)} %cotangent_ref.1, ...), custom_call_target="tpu_custom_call" | custom-call | tf_op jit(solution)/shard_map/feed_forward/pallas_call | solution.py:1290
  96.9 96.9 %attention_backward.1 = (f32[384,128]{1,0:T(8,128)}, f32[2,80,512]{2,1,0:T(8,128)}, f32[2,16,1536]{2,1,0:T(8,128)}, f32[2,8,512]{2,1,0:T(8,128)}) custom-call(s32[3]{0:T(128)} %counts_ref.5, s32[3,128,128]{2,1,0:T(8,128)} %adjacency_ref.3, bf16[48,64,1536]{2,1,0:T(8,128)(2,1)} %get-tuple-element.49.triple_ref, ...), custom_call_target="tpu_custom_call" | custom-call | tf_op jit(solution)/shard_map/attention_backward/pallas_call | solution.py:1359
  193.9 0.0 copy-start
  193.9 1.0 copy-done
  194.9 0.0 copy-start.1
  194.9 0.9 copy-done.1
  195.8 0.0 copy-start.2
  195.8 0.9 copy-done.2
  196.7 0.0 copy-start.3
  196.7 0.8 copy-done.3
  197.5 0.9 unpack_shares.1
Async XLA Ops:
  193.9 1.0 copy-start
  194.9 0.9 copy-start.1
  195.8 0.9 copy-start.2
  196.7 0.8 copy-start.3

commit v3 on v2

--- a/solution.py
+++ b/solution.py
@@ -13,7 +13,10 @@
 HOP_TOKENS = HOPS + 1
 NODES_PER_TILE = 64
 TOKENS = NODES_PER_TILE * HOP_TOKENS
-GROUP = 16
+GROUP = 8
+GROUPS = NODES_PER_TILE // GROUP
+HOP_PAIRS = HOP_TOKENS // 2
+QUAD = 4 * HEAD
 MIB = 1 << 20
 F32 = jnp.float32
 BF16 = jnp.bfloat16
@@ -71,45 +74,73 @@
     return centred * inv, inv
 
 
-def head_masks():
-    lane = lax.broadcasted_iota(jnp.int32, (GROUP * HOP_TOKENS, 2 * HEAD), 1)
-    return lane < HEAD
-
-
-def pair_stack(block, first_half):
-    zero = jnp.zeros_like(block)
+def quad_stack(block):
+    head = lax.broadcasted_iota(jnp.int32, block.shape, 1) // HEAD
     return jnp.concatenate(
-        [jnp.where(first_half, block, zero), jnp.where(first_half, zero, block)], axis=0
-    )
-
-
-def same_node():
-    span = GROUP * HOP_TOKENS
-    row = lax.broadcasted_iota(jnp.int32, (span, span), 0) % GROUP
-    col = lax.broadcasted_iota(jnp.int32, (span, span), 1) % GROUP
-    return row == col
-
-
-def pair_probs(queries, key_stack, keep):
-    span = GROUP * HOP_TOKENS
-    scores = dot_last(queries, key_stack)
-    halves = []
-    for half in range(2):
-        part = jnp.where(keep, scores[:, half * span : (half + 1) * span], -jnp.inf)
-        top = jnp.max(part, axis=-1, keepdims=True)
-        power = jnp.exp((part - top) * HEAD ** (-0.5))
-        halves.append(power * (1.0 / jnp.sum(power, axis=-1, keepdims=True)))
-    return halves
+        [jnp.where(head == h, block, jnp.zeros_like(block)) for h in range(4)], axis=0
+    )
+
+
+def grad_softmax(probs, grad_probs):
+    tokens, columns = probs.shape
+    weighted = (probs * grad_probs).reshape(HOP_TOKENS, GROUP, columns)
+    total = jnp.sum(weighted, axis=0)
+    shaped = probs.reshape(HOP_TOKENS, GROUP, columns)
+    return (weighted - shaped * total[None]).reshape(tokens, columns).astype(BF16)
+
+
+def quad_probs(scores):
+    tokens, columns = scores.shape
+    scores = scores.reshape(HOP_TOKENS, GROUP, columns)
+    top = jnp.max(scores, axis=0)
+    power = jnp.exp((scores - top[None]) * HEAD ** (-0.5))
+    row = lax.broadcasted_iota(jnp.int32, (GROUP, columns), 0)
+    col = lax.broadcasted_iota(jnp.int32, (GROUP, columns), 1) % GROUP
+    share = jnp.where(row == col, 1.0 / jnp.sum(power, axis=0), 0.0)
+    return (power * share[None]).reshape(tokens, columns)
+
+
+VARIANT = "A"
+BATCH_A = 8
+BATCH_B = 8
+
+
+def queries_from(weights, block, stack):
+    if VARIANT == "A":
+        tokens = block.shape[0]
+        out = []
+        lane = lax.broadcasted_iota(jnp.int32, (tokens, 2 * HEAD), 1)
+        for first in (0, 2 * HEAD):
+            both = dot_lead(weights[:, first : first + 2 * HEAD], block[:, first : first + 2 * HEAD])
+            out.append(jnp.where(lane < HEAD, both[:tokens], both[tokens:]))
+        return jnp.concatenate(out, axis=1)
+    turned = []
+    for first in (0, 2 * HEAD):
+        part = weights[:, first : first + 2 * HEAD].T
+        turned += [part[:HEAD], part[HEAD:]]
+    return dot(jnp.concatenate(turned, axis=1), stack())
 
 
 def read_block(ref, group, first):
-    rows = pl.ds(pl.multiple_of(group * GROUP, GROUP), GROUP)
-    return ref[:, rows, first : first + 2 * HEAD].reshape(GROUP * HOP_TOKENS, 2 * HEAD)
+    return ref[:, group, :, first : first + QUAD].reshape(GROUP * HOP_TOKENS, QUAD)
 
 
 def write_block(ref, group, first, block):
-    rows = pl.ds(pl.multiple_of(group * GROUP, GROUP), GROUP)
-    ref[:, rows, first : first + 2 * HEAD] = block.reshape(HOP_TOKENS, GROUP, 2 * HEAD)
+    ref[:, group, :, first : first + QUAD] = block.reshape(HOP_PAIRS, 2 * GROUP, QUAD)
+
+
+def hop_rows(values, index):
+    shaped = values.reshape(HOP_PAIRS, GROUPS, 2, GROUP, values.shape[-1])
+    return shaped[index // 2, :, index % 2].reshape(NODES_PER_TILE, values.shape[-1])
+
+
+def hop_join(parts):
+    width = parts[0].shape[-1]
+    blocks = []
+    for pair in range(HOP_PAIRS):
+        both = [parts[2 * pair + k].reshape(GROUPS, 1, GROUP, width) for k in range(2)]
+        blocks.append(jnp.concatenate(both, axis=1))
+    return jnp.concatenate(blocks, axis=0).reshape(TOKENS, width)
 
 
 class Place:
@@ -406,15 +437,23 @@
             features_ref[cluster * slots : (cluster + 1) * slots].astype(F32)
             * live_rows(count, 0, slots)
         )
+    earlier = [None] * clusters
     for index in range(HOP_TOKENS):
         for cluster in range(clusters):
             if index > 0:
                 states[cluster] = hop(*links[cluster], states[cluster])
-            rounded = states[cluster].astype(BF16)
+            if index % 2 == 0:
+                earlier[cluster] = states[cluster]
+                continue
             for part in range(per_cluster):
-                stacked_ref[cluster * per_cluster + part, index] = rounded[
-                    part * NODES_PER_TILE : (part + 1) * NODES_PER_TILE
+                rows = slice(part * NODES_PER_TILE, (part + 1) * NODES_PER_TILE)
+                both = [
+                    state[rows].reshape(GROUPS, GROUP, state.shape[-1])
+                    for state in (earlier[cluster], states[cluster])
                 ]
+                stacked_ref[cluster * per_cluster + part, index // 2] = jnp.concatenate(
+                    both, axis=1
+                ).astype(BF16)
 
 
 def embed_tile(step, stacked_ref, embed, gain, shift, hidden_keep, normed_keep, hidden_ref, normed_ref):
@@ -431,20 +470,22 @@
 def attend_tile(tile, hidden_keep, normed_keep, attend, merge_of, triple_ref, mixed_ref, second_ref):
     width = hidden_keep.shape[-1]
     triple_ref[...] = dot(normed_keep[tile], attend).astype(BF16).reshape(triple_ref.shape)
-    first_half = head_masks()
-    keep = same_node()
-
-    def group_step(group, carry):
-        for first in range(0, width, 2 * HEAD):
-            queries = read_block(triple_ref, group, first)
-            keys = pair_stack(read_block(triple_ref, group, width + first), first_half)
-            values = pair_stack(read_block(triple_ref, group, 2 * width + first), first_half)
-            probs = pair_probs(queries, keys, keep)
-            rounded = jnp.concatenate([half.astype(BF16) for half in probs], axis=1)
-            write_block(mixed_ref, group, first, dot(rounded, values).astype(BF16))
+
+    def group_step(index, carry):
+        places = [
+            (index * BATCH_A + g, first) for g in range(BATCH_A) for first in range(0, width, QUAD)
+        ]
+        keys = [read_block(triple_ref, g, width + first) for g, first in places]
+        queries = [quad_stack(read_block(triple_ref, g, first)) for g, first in places]
+        scores = [dot_last(k, q) for k, q in zip(keys, queries)]
+        probs = [quad_probs(score).astype(BF16) for score in scores]
+        values = [read_block(triple_ref, g, 2 * width + first) for g, first in places]
+        mixed = [queries_from(p, v, lambda v=v: quad_stack(v)) for p, v in zip(probs, values)]
+        for (g, first), block in zip(places, mixed):
+            write_block(mixed_ref, g, first, block.astype(BF16))
         return carry
 
-    lax.fori_loop(0, NODES_PER_TILE // GROUP, group_step, 0)
+    lax.fori_loop(0, GROUPS // BATCH_A, group_step, 0)
     mixed = mixed_ref[...].reshape(TOKENS, width)
     second_ref[...] = hidden_keep[tile] + dot(mixed, merge_of())
 
@@ -730,7 +771,7 @@
         1.0 + (3.0 * GELU_B) * square
     )
     third = second + dot(after, reducer)
-    shaped = third.reshape(HOP_TOKENS, NODES_PER_TILE, width)
+    shaped = [hop_rows(third, k) for k in range(HOP_TOKENS)]
     keep = live_rows(
         counts_ref[step // per_cluster], (step % per_cluster) * NODES_PER_TILE, NODES_PER_TILE
     )
@@ -763,7 +804,7 @@
         read_hop = read_hop + grad_logits[k - 1] * shaped[k]
     rows_grad_ref[4:5] += jnp.sum(grad_base * centre, axis=0, keepdims=True)
     rows_grad_ref[5:6] += jnp.sum(read_hop, axis=0, keepdims=True)
-    grad_third = jnp.concatenate(parts, axis=0)
+    grad_third = hop_join(parts)
     grad_branch = grad_third.astype(BF16)
     grad_reduce_ref[...] += dot_lead(after, grad_branch)
     grad_before = (slope * dot_last(grad_branch, reducer)).astype(BF16)
@@ -798,43 +839,33 @@
     width = normed_ref.shape[-1]
     grad_mixed = dot_last(grad_second_ref[...].astype(BF16), merge).astype(BF16)
     grad_mixed_ref[...] = grad_mixed.reshape(grad_mixed_ref.shape)
-    first_half = head_masks()
-    keep = same_node()
-    span = GROUP * HOP_TOKENS
     out_ref = grad_triple_ref.at[tile]
 
-    def group_step(group, carry):
-        for first in range(0, width, 2 * HEAD):
-            queries = read_block(triple_ref, group, first)
-            keys = pair_stack(read_block(triple_ref, group, width + first), first_half)
-            values = pair_stack(read_block(triple_ref, group, 2 * width + first), first_half)
-            out_grad = read_block(grad_mixed_ref, group, first)
-            probs = pair_probs(queries, keys, keep)
-            grad_probs = dot_last(out_grad, values)
-            grad_halves = []
-            for half in range(2):
-                part = grad_probs[:, half * span : (half + 1) * span]
-                weighted = probs[half] * part
-                grad_halves.append(
-                    (weighted - probs[half] * jnp.sum(weighted, axis=-1, keepdims=True)).astype(
-                        BF16
-                    )
-                )
-            grad_scores = jnp.concatenate(grad_halves, axis=1)
-            grad_query = dot(grad_scores, keys) * HEAD ** (-0.5)
-            grad_key = dot_lead(
-                jnp.concatenate(grad_halves, axis=0), pair_stack(queries, first_half)
-            ) * HEAD ** (-0.5)
-            grad_value = dot_lead(
-                jnp.concatenate([half.astype(BF16) for half in probs], axis=0),
-                pair_stack(out_grad, first_half),
-            )
-            write_block(out_ref, group, first, grad_query.astype(BF16))
-            write_block(out_ref, group, width + first, grad_key.astype(BF16))
-            write_block(out_ref, group, 2 * width + first, grad_value.astype(BF16))
+    def group_step(index, carry):
+        places = [
+            (index * BATCH_B + g, first) for g in range(BATCH_B) for first in range(0, width, QUAD)
+        ]
+        scale = HEAD ** (-0.5)
+        keys = [read_block(triple_ref, g, width + first) for g, first in places]
+        queries = [quad_stack(read_block(triple_ref, g, first)) for g, first in places]
+        scores = [dot_last(k, q) for k, q in zip(keys, queries)]
+        values = [read_block(triple_ref, g, 2 * width + first) for g, first in places]
+        out_grads = [quad_stack(read_block(grad_mixed_ref, g, first)) for g, first in places]
+        grad_probs = [dot_last(v, o) for v, o in zip(values, out_grads)]
+        probs = [quad_probs(score) for score in scores]
+        grad_scores = [grad_softmax(p, g) for p, g in zip(probs, grad_probs)]
+        grad_values = [dot(p.astype(BF16), o) for p, o in zip(probs, out_grads)]
+        grad_keys = [dot(s, q) for s, q in zip(grad_scores, queries)]
+        grad_queries = [
+            queries_from(s, k, lambda k=k: quad_stack(k)) for s, k in zip(grad_scores, keys)
+        ]
+        for (g, first), a, b, c in zip(places, grad_queries, grad_keys, grad_values):
+            write_block(out_ref, g, first, (a * scale).astype(BF16))
+            write_block(out_ref, g, width + first, (b * scale).astype(BF16))
+            write_block(out_ref, g, 2 * width + first, c.astype(BF16))
         return carry
 
-    lax.fori_loop(0, NODES_PER_TILE // GROUP, group_step, 0)
+    lax.fori_loop(0, GROUPS // BATCH_B, group_step, 0)
     grad_triple = out_ref[...].reshape(TOKENS, 3 * width)
     grad_attend_ref[...] += dot_lead(normed_ref[...], grad_triple)
 
@@ -877,7 +908,12 @@
 
     def hop_grad(cluster, index):
         return jnp.concatenate(
-            [grad_stacked_ref[cluster * per_cluster + p, index] for p in range(per_cluster)],
+            [
+                grad_stacked_ref[cluster * per_cluster + p, index // 2, :, index % 2].reshape(
+                    NODES_PER_TILE, grad_stacked_ref.shape[-1]
+                )
+                for p in range(per_cluster)
+            ],
             axis=0,
         )
 
@@ -1203,23 +1239,23 @@
 
 
 def forward_outs(tiles, feat, width):
-    hops, per = HOP_TOKENS, NODES_PER_TILE
+    hops, per = HOP_PAIRS, (GROUPS, 2 * GROUP)
     early = lambda t: jnp.minimum(t, tiles - 1)
     late = lambda t: jnp.maximum(t - tiles, 0)
     out_specs = [
-        kept((tiles, hops, per, feat)),
+        kept((tiles, hops, *per, feat)),
         tiled(TOKENS, width, at=early),
         tiled(TOKENS, width, at=early),
-        rows_of(hops, per, 3 * width, at=late),
-        rows_of(hops, per, width, at=late),
+        rows_of(hops, *per, 3 * width, at=late),
+        rows_of(hops, *per, width, at=late),
         tiled(TOKENS, width, at=late),
     ]
     out_shape = [
-        sds((tiles, hops, per, feat), BF16),
+        sds((tiles, hops, *per, feat), BF16),
         sds((tiles, TOKENS, width), F32),
         sds((tiles, TOKENS, width), BF16),
-        sds((tiles * hops, per, 3 * width), BF16),
-        sds((tiles * hops, per, width), BF16),
+        sds((tiles * hops, *per, 3 * width), BF16),
+        sds((tiles * hops, *per, width), BF16),
         sds((tiles, TOKENS, width), F32),
     ]
     keep = [pltpu.VMEM((tiles, TOKENS, width), F32), pltpu.VMEM((tiles, TOKENS, width), BF16)]
@@ -1284,7 +1320,7 @@
 
 def middle_part(counts, second, mixed, cotangent, rows, expand, reducer):
     tiles, _, width = second.shape
-    hops, per = HOP_TOKENS, NODES_PER_TILE
+    hops, per = HOP_PAIRS, (GROUPS, 2 * GROUP)
     spread = expand.shape[-1]
     terms = (PACK, 2, 80, width)
     return pl.pallas_call(
@@ -1293,14 +1329,14 @@
         in_specs=[
             SMEM_SPEC,
             tiled(TOKENS, width),
-            rows_of(hops, per, width),
-            rows_of(per, width),
+            rows_of(hops, *per, width),
+            rows_of(NODES_PER_TILE, width),
             whole(rows.shape),
             whole(expand.shape),
             whole(reducer.shape),
         ],
         out_specs=[
-            rows_of(per, width),
+            rows_of(NODES_PER_TILE, width),
             tiled(TOKENS, width),
             kept(terms),
             kept(rows.shape),
@@ -1322,24 +1358,24 @@
 
 
 def backward_ins(tiles, feat, width, arrays):
-    hops, per = HOP_TOKENS, NODES_PER_TILE
+    hops, per = HOP_PAIRS, (GROUPS, 2 * GROUP)
     early = lambda t: jnp.minimum(t, tiles - 1)
     late = lambda t: jnp.maximum(t - tiles, 0)
     both = lambda t: lax.rem(t, tiles)
     return [
         SMEM_SPEC,
         whole(arrays[1].shape),
-        rows_of(hops, per, 3 * width, at=early),
+        rows_of(hops, *per, 3 * width, at=early),
         tiled(TOKENS, width, at=early),
         tiled(TOKENS, width, at=both),
         tiled(TOKENS, width, at=late),
-        tiled(hops, per, feat, at=late),
+        tiled(hops, *per, feat, at=late),
     ] + [whole(a.shape) for a in arrays[7:]]
 
 
 def backward_part(lines, *arrays):
     tiles, _, width = arrays[3].shape
-    hops, per, feat = arrays[6].shape[1:]
+    hops, per, feat = HOP_PAIRS, (GROUPS, 2 * GROUP), arrays[6].shape[-1]
     owners = lines * PLANE
     rest = (80, width)
     wide = (width // owners // 2, 3 * width)
@@ -1355,7 +1391,7 @@
         ]
 
     sems = pltpu.SemaphoreType.DMA((2, PLANE + lines))
-    outs = [(tiles * per, feat), (2,) + rest, (2,) + wide, (2, 8, width)]
+    outs = [(tiles * NODES_PER_TILE, feat), (2,) + rest, (2,) + wide, (2, 8, width)]
     return pl.pallas_call(
         functools.partial(backward_kernel, lines),
         grid=(2 * tiles,),
@@ -1363,9 +1399,9 @@
         out_specs=[kept(shape) for shape in outs],
         out_shape=[sds(shape, F32) for shape in outs],
         scratch_shapes=[
-            pltpu.VMEM((hops, per, width), BF16),
-            pltpu.VMEM((tiles, hops, per, 3 * width), BF16),
-            pltpu.VMEM((tiles, hops, per, feat), F32),
+            pltpu.VMEM((hops, *per, width), BF16),
+            pltpu.VMEM((tiles, hops, *per, 3 * width), BF16),
+            pltpu.VMEM((tiles, hops, GROUPS, 2, GROUP, feat), F32),
             pltpu.VMEM((width, 3 * width), F32),
             pltpu.VMEM((feat, width), F32),
             pltpu.VMEM((8, width), F32),
@@ -1389,8 +1425,8 @@
 
 def backward_alone_part(*arrays):
     tiles, _, width = arrays[3].shape
-    hops, per, feat = arrays[6].shape[1:]
-    outs = [(tiles * per, feat), (width, 3 * width), (feat, width), (8, width)]
+    hops, per, feat = HOP_PAIRS, (GROUPS, 2 * GROUP), arrays[6].shape[-1]
+    outs = [(tiles * NODES_PER_TILE, feat), (width, 3 * width), (feat, width), (8, width)]
     return pl.pallas_call(
         backward_alone_kernel,
         grid=(2 * tiles,),
@@ -1398,9 +1434,9 @@
         out_specs=[kept(shape) for shape in outs],
         out_shape=[sds(shape, F32) for shape in outs],
         scratch_shapes=[
-            pltpu.VMEM((hops, per, width), BF16),
-            pltpu.VMEM((tiles, hops, per, 3 * width), BF16),
-            pltpu.VMEM((tiles, hops, per, feat), F32),
+            pltpu.VMEM((hops, *per, width), BF16),
+            pltpu.VMEM((tiles, hops, *per, 3 * width), BF16),
+            pltpu.VMEM((tiles, hops, GROUPS, 2, GROUP, feat), F32),
         ],
         compiler_params=params(),
         name="attention_backward_alone",

time: 199 us -> 162 us (0.81)
  Pallas kernels: 194 us -> 158 us
    pallas_call x1, Pallas kernels: 96.9 us -> 72 us  [backward_part(): pl.pallas_call(functools.partial(backward_kernel, lines), grid=(2 * tiles...]
    pallas_call x1, Pallas kernels: 59.5 us -> 47.9 us  [forward_part(): pl.pallas_call(functools.partial(forward_kernel, lines), grid=(2 * tiles,...]
where the time goes in v3:
time: 162 us
  Pallas kernels  158 us (98%)
  local copies, waits for them, and re-layouts  3.58 us (2%)
    pallas_call x1, Pallas kernels, backward_part(): pl.pallas_call(functools.partial(backward_kernel, lines), grid=(2 * tiles...  72 us
    pallas_call x1, Pallas kernels, forward_part(): pl.pallas_call(functools.partial(forward_kernel, lines), grid=(2 * tiles,...  47.9 us
    pallas_call x1, Pallas kernels, middle_part(): pl.pallas_call(middle_kernel, grid=(tiles,), in_specs=[SMEM_SPEC, tiled(T...  37.1 us
    unnamed x8, local copies, waits for them, and re-layouts  3.58 us

profile of v3, /device:TPU:0, one launch (start us, length us, event | category | flops | bytes accessed | tf_op | source)
XLA Modules:
  0.0 162.1 jit_solution(12992579539901669384)
XLA Ops:
  0.6 47.9 %hops_attention.1 = (bf16[6,4,8,16,128]{4,3,2,1,0:T(8,128)(2,1)}, f32[6,512,512]{2,1,0:T(8,128)}, bf16[6,512,512]{2,1,0:T(8,128)(2,1)}, bf16[24,8,16,1536]{3,2,1...) custom-call(s32[3]{0:T(128)} %counts_ref.5, ...), custom_call_target="tpu_custom_call" | custom-call | tf_op jit(solution)/shard_map/hops_attention/pallas_call | solution.py:1275
  48.5 37.1 %feed_forward.1 = (f32[384,512]{1,0:T(8,128)}, f32[6,512,512]{2,1,0:T(8,128)}, bf16[16,2,80,512]{3,2,1,0:T(8,128)(2,1)}, f32[8,512]{1,0:T(8,128)}) custom-call(s32[3]{0:T(128)} %counts_ref.5, f32[6,512,512]{2,1,0:T(8,128)} %get-tuple-element.43.second_ref, bf16[24,8,16,512]{3,2,1,0:T(8,128)(2,1)} %get-tuple-element.44.mixed_ref, f32[384,512]{1,0:T(8,128)} %cotangent_ref.1, ...), custom_call_target="tpu_custom_call" | custom-call | tf_op jit(solution)/shard_map/feed_forward/pallas_call | solution.py:1326
  85.6 72.0 %attention_backward.1 = (f32[384,128]{1,0:T(8,128)}, f32[2,80,512]{2,1,0:T(8,128)}, f32[2,16,1536]{2,1,0:T(8,128)}, f32[2,8,512]{2,1,0:T(8,128)}) custom-call(s32[3]{0:T(128)} %counts_ref.5, s32[3,128,128]{2,1,0:T(8,128)} %adjacency_ref.3, bf16[24,8,16,1536]{3,2,1,0:T(8,128)(2,1)} %get-tuple-element.49.triple_ref, ...), custom_call_target="tpu_custom_call" | custom-call | tf_op jit(solution)/shard_map/attention_backward/pallas_call | solution.py:1395
  157.6 0.0 copy-start
  157.6 1.0 copy-done
  158.6 0.0 copy-start.1
  158.6 0.9 copy-done.1
  159.5 0.0 copy-start.2
  159.5 0.9 copy-done.2
  160.4 0.0 copy-start.3
  160.4 0.8 copy-done.3
  161.2 0.9 unpack_shares.1
Async XLA Ops:
  157.6 1.0 copy-start
  158.6 0.9 copy-start.1
  159.5 0.9 copy-start.2
  160.4 0.8 copy-start.3

commit v4 on v3

v4 whole, which is shorter than its diff:
```python
import functools

import jax
import jax.numpy as jnp
from jax import lax
from jax.experimental import pallas as pl
from jax.experimental.pallas import tpu as pltpu
from jax.sharding import PartitionSpec as P

HEADS = 8
HEAD = 64
HOPS = 7
HOP_TOKENS = HOPS + 1
NODES_PER_TILE = 64
TOKENS = NODES_PER_TILE * HOP_TOKENS
GROUP = 8
STREAMS = 2
FEEDS = 1
SKEW = 1
GROUPS = NODES_PER_TILE // GROUP
HOP_PAIRS = HOP_TOKENS // 2
QUAD = 4 * HEAD
MIB = 1 << 20
VMEM_GRANT = 62 * MIB
F32 = jnp.float32
BF16 = jnp.bfloat16
GELU_A = 0.7978845608028654
GELU_B = 0.044715
PLANE = 4
PACK = 16
MESH = pl.DeviceIdType.MESH


def dot(left, right):
    return jnp.dot(left, right, preferred_element_type=F32)


def dot_lead(left, right):
    return lax.dot_general(left, right, (((0,), (0,)), ((), ())), preferred_element_type=F32)


def dot_last(left, right):
    return lax.dot_general(left, right, (((1,), (1,)), ((), ())), preferred_element_type=F32)


def link_of(adjacency, count):
    slots = adjacency.shape[0]
    rows = lax.broadcasted_iota(jnp.int32, (slots, slots), 0)
    cols = lax.broadcasted_iota(jnp.int32, (slots, slots), 1)
    live = jnp.logical_and(rows < count, cols < count)
    link = jnp.where(live, adjacency, 0) + jnp.where(rows == cols, 1, 0)
    link = link.astype(F32)
    root = lax.rsqrt(jnp.sum(link, axis=-1, keepdims=True))
    return link.astype(BF16), root


def hop(link, root, state):
    width = state.shape[1]
    scaled = state * root
    high = scaled.astype(BF16)
    rest = scaled - high.astype(F32)
    middle = rest.astype(BF16)
    low = (rest - middle.astype(F32)).astype(BF16)
    spread = dot(link, jnp.concatenate([high, middle, low], axis=1))
    return (spread[:, :width] + (spread[:, width : 2 * width] + spread[:, 2 * width :])) * root


def live_rows(count, first, rows):
    index = lax.broadcasted_iota(jnp.int32, (rows, 1), 0) + first
    return jnp.where(index < count, 1.0, 0.0).astype(F32)


def norm_stats(values):
    mean = jnp.mean(values, axis=-1, keepdims=True)
    centred = values - mean
    var = jnp.mean(centred * centred, axis=-1, keepdims=True)
    inv = lax.rsqrt(var + 1e-05)
    return centred * inv, inv


def quad_stack(block):
    head = lax.broadcasted_iota(jnp.int32, block.shape, 1) // HEAD
    return jnp.concatenate(
        [jnp.where(head == h, block, jnp.zeros_like(block)) for h in range(4)], axis=0
    )


def grad_softmax(probs, grad_probs):
    tokens, columns = probs.shape
    weighted = (probs * grad_probs).reshape(HOP_TOKENS, GROUP, columns)
    total = jnp.sum(weighted, axis=0)
    shaped = probs.reshape(HOP_TOKENS, GROUP, columns)
    return (weighted - shaped * total[None]).reshape(tokens, columns).astype(BF16)


def quad_probs(scores):
    tokens, columns = scores.shape
    scores = scores.reshape(HOP_TOKENS, GROUP, columns)
    top = jnp.max(scores, axis=0)
    power = jnp.exp((scores - top[None]) * HEAD ** (-0.5))
    row = lax.broadcasted_iota(jnp.int32, (GROUP, columns), 0)
    col = lax.broadcasted_iota(jnp.int32, (GROUP, columns), 1) % GROUP
    share = jnp.where(row == col, 1.0 / jnp.sum(power, axis=0), 0.0)
    return (power * share[None]).reshape(tokens, columns)


def queries_from(weights, block):
    tokens = block.shape[0]
    out = []
    lane = lax.broadcasted_iota(jnp.int32, (tokens, 2 * HEAD), 1)
    for first in (0, 2 * HEAD):
        both = dot_lead(weights[:, first : first + 2 * HEAD], block[:, first : first + 2 * HEAD])
        out.append(jnp.where(lane < HEAD, both[:tokens], both[tokens:]))
    return jnp.concatenate(out, axis=1)


def hop_rows(values, index):
    shaped = values.reshape(HOP_PAIRS, GROUPS, 2, GROUP, values.shape[-1])
    return shaped[index // 2, :, index % 2].reshape(NODES_PER_TILE, values.shape[-1])


def hop_join(parts):
    width = parts[0].shape[-1]
    blocks = []
    for pair in range(HOP_PAIRS):
        both = [parts[2 * pair + k].reshape(GROUPS, 1, GROUP, width) for k in range(2)]
        blocks.append(jnp.concatenate(both, axis=1))
    return jnp.concatenate(blocks, axis=0).reshape(TOKENS, width)


def interleave(streams):
    live = list(enumerate(streams))
    turn = 0
    while live:
        live = [
            (place, stream)
            for place, stream in live
            if turn < place * SKEW or next(stream, live) is not live
        ]
        turn += 1


class Place:
    def __init__(self, lines):
        self.lines = lines
        self.core = lax.axis_index("grp")
        self.owner = lax.axis_index("fsdp")
        self.line = lax.div(self.owner, PLANE)
        self.spot = lax.rem(self.owner, PLANE)

    def line_turn(self, ahead):
        return lax.rem(self.line + ahead + self.lines, self.lines)

    def spot_turn(self, ahead):
        return lax.rem(self.spot + ahead + PLANE, PLANE)

    def line_peer(self, ahead):
        return (self.core, self.line_turn(ahead) * PLANE + self.spot)

    def plane_peer(self, ahead):
        return (self.core, self.line * PLANE + self.spot_turn(ahead))

    def sibling(self):
        return (1 - self.core, self.owner)

    def peers(self):
        return (
            [self.line_peer(d) for d in range(1, self.lines)]
            + [self.plane_peer(e) for e in range(1, PLANE)]
            + [self.sibling()]
        )

    def greet(self):
        barrier = pltpu.get_barrier_semaphore()
        for peer in self.peers():
            pl.semaphore_signal(barrier, inc=1, device_id=peer, device_id_type=MESH)

    def greeted(self):
        pl.semaphore_wait(pltpu.get_barrier_semaphore(), self.lines + PLANE - 1)


def remote(source, target, send, recv, device):
    return pltpu.make_async_remote_copy(
        src_ref=source,
        dst_ref=target,
        send_sem=send,
        recv_sem=recv,
        device_id=device,
        device_id_type=MESH,
    )


class Gather:
    def __init__(self, place, slots, source, send, recv, pair, halves=True):
        self.place, self.slots, self.source = place, slots, source
        self.send, self.recv, self.pair_sems, self.halves = send, recv, pair, halves

    def slot(self, owner):
        return self.slots.at[owner, self.place.core] if self.halves else self.slots.at[owner]

    def own_copies(self):
        place = self.place
        peers = [place.line_peer(d) for d in range(1, place.lines)]
        peers += [place.plane_peer(e) for e in range(1, PLANE)]
        return [
            remote(
                self.source, self.slot(place.owner), self.send.at[i], self.recv.at[place.owner], peer
            )
            for i, peer in enumerate(peers)
        ]

    def onward(self, d):
        place = self.place
        owner = place.line_turn(-d) * PLANE + place.spot
        first = place.lines + PLANE - 2 + (d - 1) * (PLANE - 1)
        return [
            remote(
                self.slot(owner),
                self.slot(owner),
                self.send.at[first + e - 1],
                self.recv.at[owner],
                place.plane_peer(e),
            )
            for e in range(1, PLANE)
        ]

    def start_line(self):
        for copy in self.own_copies()[: self.place.lines - 1]:
            copy.start()

    def start_plane(self):
        for copy in self.own_copies()[self.place.lines - 1 :]:
            copy.start()

    def start(self):
        self.start_line()
        self.start_plane()

    def forward(self):
        for d in range(1, self.place.lines):
            copies = self.onward(d)
            copies[0].wait_recv()
            for copy in copies:
                copy.start()

    def finish(self):
        place = self.place
        for d in range(place.lines):
            for e in range(1, PLANE):
                owner = place.line_turn(d) * PLANE + place.spot_turn(-e)
                remote(
                    self.slot(owner),
                    self.slot(owner),
                    self.send.at[0],
                    self.recv.at[owner],
                    place.plane_peer(e),
                ).wait_recv()
        for copy in self.own_copies():
            copy.wait_send()
        for d in range(1, place.lines):
            for copy in self.onward(d):
                copy.wait_send()

    def pair(self):
        half = self.slots.at[:, self.place.core]
        return remote(half, half, self.pair_sems.at[0], self.pair_sems.at[1], self.place.sibling())


class Scatter:
    def __init__(self, place, terms, got, chip, plane_got, line_out, line_got, result, sems):
        self.place, self.terms, self.got, self.chip = place, terms, got, chip
        self.plane_got, self.line_out, self.line_got = plane_got, line_out, line_got
        self.result, self.sems = result, sems

    def pair(self):
        place = self.place
        return remote(
            self.terms.at[:, 1 - place.core],
            self.got,
            self.sems.at[0, 0],
            self.sems.at[1, 0],
            place.sibling(),
        )

    def plane(self):
        place = self.place
        return [
            remote(
                self.chip.at[:, place.spot_turn(e)],
                self.plane_got.at[e - 1],
                self.sems.at[0, e],
                self.sems.at[1, e],
                place.plane_peer(e),
            )
            for e in range(1, PLANE)
        ]

    def line(self):
        place = self.place
        return [
            remote(
                self.line_out.at[place.line_turn(d)],
                self.line_got.at[d - 1],
                self.sems.at[0, PLANE + d - 1],
                self.sems.at[1, PLANE + d - 1],
                place.line_peer(d),
            )
            for d in range(1, place.lines)
        ]

    def last(self):
        place = self.place
        half = self.result.at[place.core]
        k = PLANE + place.lines - 1
        return remote(half, half, self.sems.at[0, k], self.sems.at[1, k], place.sibling())

    def begin(self):
        self.pair().start()

    def to_plane(self):
        place = self.place
        self.pair().wait()

        def add(line, carry):
            for spot in range(PLANE):
                owner = line * PLANE + spot
                both = self.terms[owner, place.core].astype(F32) + self.got[owner].astype(F32)
                self.chip[line, spot] = both.astype(BF16)
            return carry

        lax.fori_loop(0, place.lines, add, 0)
        for copy in self.plane():
            copy.start()

    def to_line(self):
        place = self.place
        for copy in self.plane():
            copy.wait()

        def add(line, carry):
            total = self.chip[line, place.spot].astype(F32)
            for e in range(PLANE - 1):
                total = total + self.plane_got[e, line].astype(F32)
            self.line_out[line] = total.astype(BF16)
            return carry

        lax.fori_loop(0, place.lines, add, 0)
        for copy in self.line():
            copy.start()

    def to_sibling(self):
        place = self.place
        for copy in self.line():
            copy.wait()
        total = self.line_out[place.line].astype(F32)
        for d in range(place.lines - 1):
            total = total + self.line_got[d].astype(F32)
        self.result[place.core] = total
        self.last().start()

    def end(self):
        self.last().wait()


class TailScatter:
    def __init__(self, place, own, plane_got, line_out, line_got, mine, other, sems):
        self.place, self.own, self.plane_got, self.line_out = place, own, plane_got, line_out
        self.line_got, self.mine, self.other, self.sems = line_got, mine, other, sems

    def plane(self):
        place = self.place
        return [
            remote(
                self.own.at[place.spot_turn(e)],
                self.plane_got.at[e - 1],
                self.sems.at[0, e],
                self.sems.at[1, e],
                place.plane_peer(e),
            )
            for e in range(1, PLANE)
        ]

    def line(self):
        place = self.place
        return [
            remote(
                self.line_out.at[place.line_turn(d)],
                self.line_got.at[d - 1],
                self.sems.at[0, PLANE + d - 1],
                self.sems.at[1, PLANE + d - 1],
                place.line_peer(d),
            )
            for d in range(1, place.lines)
        ]

    def last(self):
        return remote(
            self.mine, self.other, self.sems.at[0, 0], self.sems.at[1, 0], self.place.sibling()
        )

    def begin(self):
        for copy in self.plane():
            copy.start()

    def to_line(self):
        place = self.place
        for copy in self.plane():
            copy.wait()
        total = self.own[place.spot]
        for e in range(PLANE - 1):
            total = total + self.plane_got[e]
        for line in range(place.lines):
            self.line_out[line, 0] = total[line]
            self.line_out[line, 1] = total[place.lines]
        for copy in self.line():
            copy.start()

    def to_sibling(self):
        place = self.place
        for copy in self.line():
            copy.wait()
        total = self.line_out[place.line]
        for d in range(place.lines - 1):
            total = total + self.line_got[d]
        self.mine[...] = total
        self.last().start()

    def end(self):
        self.last().wait()
        return self.mine[...] + self.other[...]


def hop_states(counts_ref, adjacency_ref, features_ref, stacked_ref):
    clusters, slots = adjacency_ref.shape[:2]
    per_cluster = slots // NODES_PER_TILE
    links = []
    states = []
    for cluster in range(clusters):
        count = counts_ref[cluster]
        links.append(link_of(adjacency_ref[cluster], count))
        states.append(
            features_ref[cluster * slots : (cluster + 1) * slots].astype(F32)
            * live_rows(count, 0, slots)
        )
    earlier = [None] * clusters
    for index in range(HOP_TOKENS):
        for cluster in range(clusters):
            if index > 0:
                states[cluster] = hop(*links[cluster], states[cluster])
            if index % 2 == 0:
                earlier[cluster] = states[cluster]
                continue
            for part in range(per_cluster):
                rows = slice(part * NODES_PER_TILE, (part + 1) * NODES_PER_TILE)
                both = [
                    state[rows].reshape(GROUPS, GROUP, state.shape[-1])
                    for state in (earlier[cluster], states[cluster])
                ]
                stacked_ref[cluster * per_cluster + part, index // 2] = jnp.concatenate(
                    both, axis=1
                ).astype(BF16)


def spread_vectors(small, owners, width):
    rows = small.shape[0]
    lane = lax.broadcasted_iota(jnp.int32, (128, width), 0)
    column = lax.broadcasted_iota(jnp.int32, (128, width), 1)
    row = lax.broadcasted_iota(jnp.int32, (rows, width), 0)
    place = lax.broadcasted_iota(jnp.int32, (rows, width), 1)
    piece = width // owners
    pieces = dot(small, jnp.where(lane == column % piece, 1.0, 0.0).astype(BF16))
    out = []
    for vector in range(4):
        mine = jnp.logical_and(row % 8 == vector, lax.div(row, 8) == lax.div(place, piece))
        out.append(jnp.sum(jnp.where(mine, pieces, 0.0), axis=0, keepdims=True))
    pieces = dot(small, jnp.where(lane == column % (2 * piece), 1.0, 0.0).astype(BF16))
    for first in (0, owners // 2):
        owner = lax.div(place, 2 * piece) + first
        mine = jnp.logical_and(row % 8 == 4, lax.div(row, 8) == owner)
        out.append(jnp.sum(jnp.where(mine, pieces, 0.0), axis=0, keepdims=True))
    return jnp.concatenate(out + [jnp.zeros((2, width), F32)], axis=0)


def hop_back(counts_ref, adjacency_ref, grad_stacked_ref, grad_features_ref, between):
    clusters, slots = adjacency_ref.shape[:2]
    per_cluster = slots // NODES_PER_TILE
    links = []
    states = []

    def hop_grad(cluster, index):
        return jnp.concatenate(
            [
                grad_stacked_ref[cluster * per_cluster + p, index // 2, :, index % 2].reshape(
                    NODES_PER_TILE, grad_stacked_ref.shape[-1]
                )
                for p in range(per_cluster)
            ],
            axis=0,
        )

    for cluster in range(clusters):
        links.append(link_of(adjacency_ref[cluster], counts_ref[cluster]))
        states.append(hop_grad(cluster, HOPS))
    for index in range(HOPS - 1, -1, -1):
        for cluster in range(clusters):
            states[cluster] = hop_grad(cluster, index) + hop(*links[cluster], states[cluster])
        if index in between:
            between[index]()
    for cluster in range(clusters):
        grad_features_ref[cluster * slots : (cluster + 1) * slots] = states[cluster] * live_rows(
            counts_ref[cluster], 0, slots
        )


def block_of(ref, tile, group, first):
    return ref[tile, :, group, :, first : first + QUAD].reshape(GROUP * HOP_TOKENS, QUAD)


def put_block(ref, tile, group, first, block):
    ref[tile, :, group, :, first : first + QUAD] = block.astype(BF16).reshape(
        HOP_PAIRS, 2 * GROUP, QUAD
    )


def tokens_of(ref, tile):
    return ref[tile].reshape(TOKENS, ref.shape[-1])


def embed_tile(tile, stacked_ref, embed, gain, shift, second_ref, normed_ref):
    hidden = dot(tokens_of(stacked_ref, tile), embed)
    second_ref[tile] = hidden
    normal, _ = norm_stats(hidden)
    normed_ref[tile] = (normal * gain + shift).astype(BF16)


def attend_tile(tile, normed_ref, attend, merge_of, triple_ref, mixed_ref, second_ref):
    width = normed_ref.shape[-1]
    triple = dot(normed_ref[tile], attend).astype(BF16)
    triple_ref[tile] = triple.reshape(triple_ref.shape[1:])
    places = [(tile, g, first) for g in range(GROUPS) for first in range(0, width, QUAD)]
    keys = [block_of(triple_ref, t, g, width + first) for t, g, first in places]
    queries = [quad_stack(block_of(triple_ref, *place)) for place in places]
    scores = [dot_last(k, q) for k, q in zip(keys, queries)]
    probs = [quad_probs(score).astype(BF16) for score in scores]
    values = [block_of(triple_ref, t, g, 2 * width + first) for t, g, first in places]
    blocks = [queries_from(p, v) for p, v in zip(probs, values)]
    for place, block in zip(places, blocks):
        put_block(mixed_ref, *place, block)
    second_ref[tile] += dot(tokens_of(mixed_ref, tile), merge_of())


def middle_step(
    first_tile,
    counts_ref,
    second_ref,
    mixed_ref,
    cotangent_ref,
    rows_ref,
    expand,
    reducer,
    output_ref,
    rows_grad_ref,
    grad_merge_ref,
    grad_expand_ref,
    grad_reduce_ref,
):
    width = second_ref.shape[-1]
    gain, shift = rows_ref[2:3], rows_ref[3:4]
    row_node, row_hop = rows_ref[4:5], rows_ref[5:6]

    def stream(part):
        tile = first_tile + part
        second = second_ref[tile]
        normal, inv = norm_stats(second)
        inner = (normal * gain + shift).astype(BF16)
        yield
        before = dot(inner, expand)
        yield
        square = before * before
        curve = jnp.tanh(GELU_A * before * (1.0 + GELU_B * square))
        after = (0.5 * before * (1.0 + curve)).astype(BF16)
        slope = 0.5 * (1.0 + curve) + (0.5 * GELU_A) * before * (1.0 - curve * curve) * (
            1.0 + (3.0 * GELU_B) * square
        )
        yield
        third = second + dot(after, reducer)
        yield
        shaped = [hop_rows(third, k) for k in range(HOP_TOKENS)]
        node = tile * NODES_PER_TILE
        keep = live_rows(counts_ref[lax.div(node, 128)], lax.rem(node, 128), NODES_PER_TILE)
        centre = shaped[0]
        base = jnp.sum(centre * row_node, axis=-1, keepdims=True)
        logits = [
            base + jnp.sum(shaped[k] * row_hop, axis=-1, keepdims=True)
            for k in range(1, HOP_TOKENS)
        ]
        top = functools.reduce(jnp.maximum, logits)
        powers = [jnp.exp(logit - top) for logit in logits]
        scale = 1.0 / functools.reduce(jnp.add, powers)
        shares = [power * scale for power in powers]
        total = centre
        for k in range(1, HOP_TOKENS):
            total = total + shares[k - 1] * shaped[k]
        output_ref[tile] = total * keep
        cotangent = cotangent_ref[tile] * keep
        grad_shares = [
            jnp.sum(cotangent * shaped[k], axis=-1, keepdims=True) for k in range(1, HOP_TOKENS)
        ]
        mean_share = functools.reduce(jnp.add, [s * g for s, g in zip(shares, grad_shares)])
        grad_logits = [s * (g - mean_share) for s, g in zip(shares, grad_shares)]
        grad_base = functools.reduce(jnp.add, grad_logits)
        parts = [cotangent + grad_base * row_node]
        read_hop = jnp.zeros((NODES_PER_TILE, width), F32)
        for k in range(1, HOP_TOKENS):
            parts.append(shares[k - 1] * cotangent + grad_logits[k - 1] * row_hop)
            read_hop = read_hop + grad_logits[k - 1] * shaped[k]
        rows_grad_ref[4:5] += jnp.sum(grad_base * centre, axis=0, keepdims=True)
        rows_grad_ref[5:6] += jnp.sum(read_hop, axis=0, keepdims=True)
        grad_third = hop_join(parts)
        grad_branch = grad_third.astype(BF16)
        yield
        grad_after = dot_last(grad_branch, reducer)
        grad_reduce_ref[...] += dot_lead(after, grad_branch)
        yield
        grad_before = (slope * grad_after).astype(BF16)
        yield
        grad_inner = dot_last(grad_before, expand)
        grad_expand_ref[...] += dot_lead(inner, grad_before)
        yield
        rows_grad_ref[2:3] += jnp.sum(grad_inner * normal, axis=0, keepdims=True)
        rows_grad_ref[3:4] += jnp.sum(grad_inner, axis=0, keepdims=True)
        grad_normal = grad_inner * gain
        grad_second = grad_third + inv * (
            grad_normal
            - jnp.mean(grad_normal, axis=-1, keepdims=True)
            - normal * jnp.mean(grad_normal * normal, axis=-1, keepdims=True)
        )
        second_ref[tile] = grad_second
        yield
        grad_merge_ref[...] += dot_lead(tokens_of(mixed_ref, tile), grad_second.astype(BF16))

    interleave([stream(part) for part in range(FEEDS)])


def pack_terms(terms_ref, grad_merge_ref, grad_expand_ref, grad_reduce_ref):
    width, spread = grad_expand_ref.shape
    wide = grad_expand_ref[...].astype(BF16).reshape(PACK, 2, width // PACK // 2, spread)
    deep = grad_reduce_ref[...].astype(BF16).reshape(PACK, 2, spread // PACK // 2, width)
    square = grad_merge_ref[...].astype(BF16).reshape(PACK, 2, width // PACK // 2, width)
    terms_ref[:, :, 0:16] = wide[..., :width]
    terms_ref[:, :, 16:32] = wide[..., width:]
    terms_ref[:, :, 32:64] = deep
    terms_ref[:, :, 64:80] = square


def attend_back_step(quad, first_tile, triple_ref, second_ref, normed_ref, merge, grad_mixed_ref, grad_attend_ref):
    width = normed_ref.shape[-1]
    for part in range(STREAMS):
        grad_mixed = dot_last(second_ref[first_tile + part].astype(BF16), merge).astype(BF16)
        grad_mixed_ref[part] = grad_mixed.reshape(grad_mixed_ref.shape[1:])
    places = [(part, group) for part in range(STREAMS) for group in range(GROUPS)]
    scale = HEAD ** (-0.5)
    starts = [kind * width + quad * QUAD for kind in range(3)]

    def read(kind):
        return [block_of(triple_ref, first_tile + p, g, starts[kind]) for p, g in places]

    keys = read(1)
    queries = [quad_stack(block) for block in read(0)]
    scores = [dot_last(k, q) for k, q in zip(keys, queries)]
    values = read(2)
    out_grads = [quad_stack(block_of(grad_mixed_ref, p, g, 0)) for p, g in places]
    grad_probs = [dot_last(v, o) for v, o in zip(values, out_grads)]
    probs = [quad_probs(score) for score in scores]
    grad_scores = [grad_softmax(p, g) for p, g in zip(probs, grad_probs)]
    grad_values = [dot(p.astype(BF16), o) for p, o in zip(probs, out_grads)]
    grad_keys = [dot(s, q) for s, q in zip(grad_scores, queries)]
    grad_queries = [queries_from(s, k) for s, k in zip(grad_scores, keys)]
    for (part, group), a, b, c in zip(places, grad_queries, grad_keys, grad_values):
        for start, block in zip(starts, (a * scale, b * scale, c)):
            put_block(triple_ref, first_tile + part, group, start, block)
    tiles = pl.ds(first_tile, STREAMS)
    grads = jnp.concatenate(
        [
            triple_ref[tiles, :, :, :, start : start + QUAD].reshape(STREAMS * TOKENS, QUAD)
            for start in starts
        ],
        axis=1,
    )
    grad_attend_ref[:, 0 : 3 * QUAD] += dot_lead(
        normed_ref[tiles].reshape(STREAMS * TOKENS, width), grads
    )


def embed_back_step(
    first_tile,
    stacked_ref,
    second_ref,
    triple_ref,
    attend,
    embed,
    gain,
    rows_keep,
    grad_embed_ref,
    grad_stacked_ref,
):
    def stream(part):
        tile = first_tile + part
        stacked = tokens_of(stacked_ref, tile)
        grad_normed = dot_last(tokens_of(triple_ref, tile), attend)
        hidden = dot(stacked, embed)
        yield
        normal, inv = norm_stats(hidden)
        rows_keep[0:1] += jnp.sum(grad_normed * normal, axis=0, keepdims=True)
        rows_keep[1:2] += jnp.sum(grad_normed, axis=0, keepdims=True)
        grad_normal = grad_normed * gain
        grad_hidden = second_ref[tile] + inv * (
            grad_normal
            - jnp.mean(grad_normal, axis=-1, keepdims=True)
            - normal * jnp.mean(grad_normal * normal, axis=-1, keepdims=True)
        )
        grad_hidden = grad_hidden.astype(BF16)
        yield
        grad_embed_ref[...] += dot_lead(stacked, grad_hidden)
        grad_stacked_ref[tile] = dot_last(grad_hidden, embed).reshape(grad_stacked_ref.shape[1:])

    interleave([stream(part) for part in range(STREAMS)])


class Silent:
    def __getattr__(self, name):
        return lambda *arguments: None


def loop(count, step):
    def body(index, carry):
        step(index)
        return carry

    lax.fori_loop(0, count, body, 0)


def layer_phases(
    counts_ref,
    adjacency_ref,
    features_ref,
    cotangent_ref,
    rows_ref,
    embed_ref,
    attend_ref,
    merge_ref,
    expand_ref,
    reduce_ref,
    output_ref,
    grad_features_ref,
    terms_ref,
    early_terms,
    late_terms,
    grad_embed_ref,
    rows_keep,
    keep,
    transfers,
):
    (
        stacked_ref,
        second_ref,
        normed_ref,
        triple_ref,
        mixed_ref,
        grad_mixed_ref,
        grad_merge_ref,
        grad_expand_ref,
        grad_reduce_ref,
        grad_stacked_ref,
    ) = keep
    tiles, _, width = second_ref.shape
    pairs = tiles // STREAMS
    hop_states(counts_ref, adjacency_ref, features_ref, stacked_ref)
    transfers.head()

    def embed_step(tile):
        embed_tile(
            tile, stacked_ref, embed_ref[...], rows_ref[0:1], rows_ref[1:2], second_ref, normed_ref
        )
        transfers.beside_embed(tile, tiles)

    loop(tiles, embed_step)
    transfers.before_attention()

    def attend_step(tile):
        def merge_of():
            transfers.before_merge(tile)
            return merge_ref[...].reshape(width, width)

        attend_tile(
            tile,
            normed_ref,
            attend_ref[...].reshape(width, 3 * width),
            merge_of,
            triple_ref,
            mixed_ref,
            second_ref,
        )
        transfers.beside_attention(tile, tiles)

    loop(tiles, attend_step)
    transfers.before_middle()
    for ref in (rows_keep, grad_merge_ref, grad_expand_ref, grad_reduce_ref, grad_embed_ref):
        ref[...] = jnp.zeros_like(ref)
    spread = grad_expand_ref.shape[1]

    def feed_step(pair):
        middle_step(
            pair * FEEDS,
            counts_ref,
            second_ref,
            mixed_ref,
            cotangent_ref,
            rows_ref,
            expand_ref[...].reshape(width, spread),
            reduce_ref[...].reshape(spread, width),
            output_ref,
            rows_keep,
            grad_merge_ref,
            grad_expand_ref,
            grad_reduce_ref,
        )

    loop(tiles // FEEDS, feed_step)
    pack_terms(terms_ref, grad_merge_ref, grad_expand_ref, grad_reduce_ref)
    transfers.after_middle()
    grad_attend_ref = grad_expand_ref
    for quad, terms in enumerate((early_terms, late_terms)):
        grad_attend_ref[...] = jnp.zeros_like(grad_attend_ref)

        def back_step(pair, quad=quad):
            attend_back_step(
                quad,
                pair * STREAMS,
                triple_ref,
                second_ref,
                normed_ref,
                merge_ref[...].reshape(width, width)[quad * QUAD : (quad + 1) * QUAD],
                grad_mixed_ref,
                grad_attend_ref,
            )
            transfers.beside_backward(quad, pair, pairs)

        loop(pairs, back_step)
        terms[...] = grad_attend_ref[:, 0 : 3 * QUAD].astype(BF16).reshape(terms.shape)
        transfers.after_backward(quad)

    def embed_back(pair):
        embed_back_step(
            pair * STREAMS,
            stacked_ref,
            second_ref,
            triple_ref,
            attend_ref[...].reshape(width, 3 * width),
            embed_ref[...],
            rows_ref[0:1],
            rows_keep,
            grad_embed_ref,
            grad_stacked_ref,
        )
        transfers.beside_embed_back(pair, pairs)

    loop(pairs, embed_back)
    transfers.after_embed_back()
    hop_back(
        counts_ref,
        adjacency_ref,
        grad_stacked_ref,
        grad_features_ref,
        {1: transfers.beside_hops},
    )
    transfers.end()


class Transfers:
    def __init__(self, place, gathers, scatters, unpack_head, pack_tail, publish):
        self.place = place
        self.lead, self.attend, self.merge, self.expand, self.reducer = gathers
        self.middle, self.early, self.late, self.tail = scatters
        self.unpack_head, self.pack_tail, self.publish = unpack_head, pack_tail, publish

    def head(self):
        self.place.greeted()
        self.lead.start()
        self.attend.start_line()
        self.lead.forward()
        self.attend.start_plane()
        self.attend.forward()
        self.lead.finish()
        self.unpack_head()

    def beside_embed(self, tile, tiles):
        @pl.when(tile == 0)
        def _():
            self.merge.start()

        @pl.when(tile == tiles - 3)
        def _():
            self.merge.forward()

        @pl.when(tile == tiles - 2)
        def _():
            self.attend.finish()
            self.attend.pair().start()
            self.expand.start()
            self.reducer.start()

    def before_attention(self):
        self.merge.finish()
        self.merge.pair().start()
        self.attend.pair().wait()

    def before_merge(self, tile):
        @pl.when(tile == 0)
        def _():
            self.merge.pair().wait()
            self.expand.forward()
            self.reducer.forward()

    def beside_attention(self, tile, tiles):
        @pl.when(tile == tiles - 2)
        def _():
            self.expand.finish()
            self.expand.pair().start()
            self.reducer.finish()
            self.reducer.pair().start()

    def before_middle(self):
        self.expand.pair().wait()
        self.reducer.pair().wait()

    def after_middle(self):
        self.middle.begin()

    def beside_backward(self, quad, pair, pairs):
        if quad == 0:

            @pl.when(pair == 0)
            def _():
                self.middle.to_plane()

        else:

            @pl.when(pair == 0)
            def _():
                self.early.to_plane()

            @pl.when(pair == pairs - 2)
            def _():
                self.middle.to_line()

    def after_backward(self, quad):
        if quad == 0:
            self.early.begin()
        else:
            self.late.begin()
            self.early.to_line()

    def beside_embed_back(self, pair, pairs):
        @pl.when(pair == 0)
        def _():
            self.late.to_plane()

        @pl.when(pair == 1)
        def _():
            self.middle.to_sibling()

    def after_embed_back(self):
        self.pack_tail()
        self.tail.begin()
        self.early.to_sibling()

    def beside_hops(self):
        self.late.to_line()
        self.tail.to_line()

    def end(self):
        self.tail.to_sibling()
        self.middle.end()
        self.early.end()
        self.late.to_sibling()
        tail = self.tail.end()
        self.late.end()
        self.publish(tail)


def layer_kernel(
    lines,
    counts_ref,
    adjacency_ref,
    features_ref,
    cotangent_ref,
    embed_shard,
    vector_a,
    vector_b,
    vector_c,
    vector_d,
    vector_e,
    attend_shard,
    merge_shard,
    expand_shard,
    reduce_shard,
    output_ref,
    grad_features_ref,
    middle_share_ref,
    attend_share_ref,
    tail_share_ref,
    *scratch,
):
    keep = scratch[0:10]
    embed_ref, rows_ref, small_keep, head_slots = scratch[10:14]
    attend_slots, merge_slots, expand_slots, reduce_slots = scratch[14:18]
    grad_embed_ref, rows_keep = scratch[18:20]
    middle_refs, early_refs, late_refs = scratch[20:27], scratch[27:34], scratch[34:41]
    tail_refs = scratch[41:47]
    send, recv, pair, scatter_sems = scratch[47:51]
    owners = head_slots.shape[0]
    width = embed_ref.shape[-1]
    half_width = width // 2
    place = Place(lines)
    core, owner = place.core, place.owner
    place.greet()

    def half_of(shard):
        rows = shard.shape[0] // 2
        return shard.at[pl.ds(pl.multiple_of(core * rows, rows), rows)]

    def gather(index, slots, source, halves=True):
        return Gather(
            place, slots, source, send.at[index], recv.at[index], pair.at[index], halves
        )

    small_keep[...] = jnp.zeros_like(small_keep)
    for index, vector in enumerate((vector_a, vector_b, vector_c, vector_d, vector_e)):
        length = vector.shape[0]
        small_keep[index : index + 1, 0:length] = vector[...].astype(F32).reshape(1, length)
    mine = embed_shard[...].astype(F32)
    packed = jnp.concatenate(
        [
            jnp.concatenate([mine[:, :half_width], small_keep[...]], axis=1),
            jnp.concatenate([mine[:, half_width:], jnp.zeros((8, 128), F32)], axis=1),
        ],
        axis=0,
    )
    head_slots[owner] = packed.astype(BF16)
    matrices = (
        (attend_slots, attend_shard),
        (merge_slots, merge_shard),
        (expand_slots, expand_shard),
        (reduce_slots, reduce_shard),
    )
    for slots, shard in matrices:
        slots[owner, core] = half_of(shard)[...]
    gathers = [gather(0, head_slots, head_slots.at[owner], False)]
    gathers += [
        gather(1 + index, slots, half_of(shard)) for index, (slots, shard) in enumerate(matrices)
    ]
    middle = Scatter(place, *middle_refs, scatter_sems.at[0])
    early = Scatter(place, *early_refs, scatter_sems.at[1])
    late = Scatter(place, *late_refs, scatter_sems.at[2])
    tail = TailScatter(place, *tail_refs, scatter_sems.at[3])

    def unpack_head():
        whole_head = head_slots[...].astype(F32)
        top = whole_head[:, 0:8].reshape(owners * 8, half_width + 128)
        bottom = whole_head[:, 8:16].reshape(owners * 8, half_width + 128)
        embed_ref[:, :half_width] = top[:, :half_width].astype(BF16)
        embed_ref[:, half_width:] = bottom[:, :half_width].astype(BF16)
        rows_ref[...] = spread_vectors(top[:, half_width:].astype(BF16), owners, width)

    def pack_tail():
        own = grad_embed_ref[...].reshape(lines, PLANE, 8, width)
        for spot in range(PLANE):
            tail.own[spot, 0:lines] = own[:, spot]
            tail.own[spot, lines] = rows_keep[...]

    def publish(tail_total):
        middle_share_ref[...] = middle.result[...]
        attend_share_ref[0] = early.result[...]
        attend_share_ref[1] = late.result[...]
        tail_share_ref[...] = tail_total

    transfers = Transfers(
        place, gathers, (middle, early, late, tail), unpack_head, pack_tail, publish
    )
    layer_phases(
        counts_ref,
        adjacency_ref,
        features_ref,
        cotangent_ref,
        rows_ref,
        embed_ref,
        attend_slots,
        merge_slots,
        expand_slots,
        reduce_slots,
        output_ref,
        grad_features_ref,
        middle.terms,
        early.terms,
        late.terms,
        grad_embed_ref,
        rows_keep,
        keep,
        transfers,
    )


def layer_alone_kernel(*refs):
    layer_phases(*refs[:17], refs[17:], Silent())


def unpack_kernel(
    middle_ref,
    attend_ref,
    tail_ref,
    features_ref,
    nodes_ref,
    output_ref,
    grad_features_ref,
    grad_embed_ref,
    grad_gain_one,
    grad_shift_one,
    grad_attend,
    grad_merge,
    grad_gain_two,
    grad_shift_two,
    grad_expand,
    grad_reduce,
    grad_readout,
):
    owner = lax.axis_index("fsdp")
    width = middle_ref.shape[-1]
    output_ref[...] = nodes_ref[...]
    grad_features_ref[...] = features_ref[...]
    for half in range(2):
        for quad in range(width // QUAD):
            for kind in range(3):
                first = kind * width + quad * QUAD
                grad_attend[half * 16 : half * 16 + 16, first : first + QUAD] = attend_ref[
                    quad, half, :, kind * QUAD : (kind + 1) * QUAD
                ]
        grad_expand[half * 16 : half * 16 + 16, 0:width] = middle_ref[half, 0:16]
        grad_expand[half * 16 : half * 16 + 16, width : 2 * width] = middle_ref[half, 16:32]
        grad_reduce[half * 32 : half * 32 + 32] = middle_ref[half, 32:64]
        grad_merge[half * 16 : half * 16 + 16] = middle_ref[half, 64:80]
    grad_embed_ref[...] = tail_ref[0]
    rows = tail_ref[1]
    length = grad_gain_one.shape[0]
    turned = pltpu.roll(rows, lax.rem(width - owner * length, width), 1)
    for index, ref in enumerate((grad_gain_one, grad_shift_one, grad_gain_two, grad_shift_two)):
        ref[...] = turned[index : index + 1, 0:length].reshape(length)
    length = grad_readout.shape[0]
    first = owner * length
    turned = pltpu.roll(rows, lax.rem(2 * width - first, width), 1)
    row = jnp.where(first < width, turned[4:5, 0:length], turned[5:6, 0:length])
    grad_readout[...] = row.reshape(length)


def sds(shape, dtype):
    return jax.ShapeDtypeStruct(shape, dtype)


SMEM_SPEC = pl.BlockSpec(memory_space=pltpu.SMEM)
VMEM_SPEC = pl.BlockSpec(memory_space=pltpu.VMEM)
ANY_SPEC = pl.BlockSpec(memory_space=pl.ANY)


def layer_keep(tiles, feat, width, spread):
    rows = (HOP_PAIRS, GROUPS, 2 * GROUP)
    return [
        pltpu.VMEM((tiles, *rows, feat), BF16),
        pltpu.VMEM((tiles, TOKENS, width), F32),
        pltpu.VMEM((tiles, TOKENS, width), BF16),
        pltpu.VMEM((tiles, *rows, 3 * width), BF16),
        pltpu.VMEM((tiles, *rows, width), BF16),
        pltpu.VMEM((STREAMS, *rows, QUAD), BF16),
        pltpu.VMEM((width, width), F32),
        pltpu.VMEM((width, spread), F32),
        pltpu.VMEM((spread, width), F32),
        pltpu.VMEM((tiles, HOP_PAIRS, GROUPS, 2, GROUP, feat), F32),
    ]


def layer_part(
    lines, counts, adjacency, features, cotangent, embed, vectors, attend, merge, expand, reducer
):
    nodes, feat = features.shape
    owners = lines * PLANE
    width, spread = expand.shape[0] * owners, expand.shape[1]
    tiles = nodes // NODES_PER_TILE
    rest = (80, width)
    wide = (width // owners // 2, 3 * QUAD)
    copies = lines + PLANE - 2 + (lines - 1) * (PLANE - 1)

    def slots(shard):
        return pltpu.VMEM((owners, 2, shard.shape[0] // 2, shard.shape[1]), BF16)

    def buffers(shape):
        return [
            pltpu.VMEM((owners, 2) + shape, BF16),
            pltpu.VMEM((owners,) + shape, BF16),
            pltpu.VMEM((lines, PLANE) + shape, BF16),
            pltpu.VMEM((PLANE - 1, lines) + shape, BF16),
            pltpu.VMEM((lines,) + shape, BF16),
            pltpu.VMEM((lines - 1,) + shape, BF16),
            pltpu.VMEM((2,) + shape, F32),
        ]

    outs = [
        cotangent.shape,
        features.shape,
        (2,) + rest,
        (width // QUAD, 2) + wide,
        (2, 8, width),
    ]
    return pl.pallas_call(
        functools.partial(layer_kernel, lines),
        in_specs=[SMEM_SPEC] + [VMEM_SPEC] * 13,
        out_specs=[VMEM_SPEC] * 5,
        out_shape=[sds(shape, F32) for shape in outs],
        scratch_shapes=layer_keep(tiles, feat, width, spread)
        + [
            pltpu.VMEM((feat, width), BF16),
            pltpu.VMEM((8, width), F32),
            pltpu.VMEM((8, 128), F32),
            pltpu.VMEM((owners, 16, width // 2 + 128), BF16),
        ]
        + [slots(shard) for shard in (attend, merge, expand, reducer)]
        + [pltpu.VMEM((feat, width), F32), pltpu.VMEM((8, width), F32)]
        + buffers(rest)
        + buffers(wide) * 2
        + [
            pltpu.VMEM((PLANE, lines + 1, 8, width), F32),
            pltpu.VMEM((PLANE - 1, lines + 1, 8, width), F32),
            pltpu.VMEM((lines, 2, 8, width), F32),
            pltpu.VMEM((lines - 1, 2, 8, width), F32),
            pltpu.VMEM((2, 8, width), F32),
            pltpu.VMEM((2, 8, width), F32),
        ]
        + [
            pltpu.SemaphoreType.DMA((5, copies)),
            pltpu.SemaphoreType.DMA((5, owners)),
            pltpu.SemaphoreType.DMA((5, 2)),
            pltpu.SemaphoreType.DMA((4, 2, PLANE + lines)),
        ],
        compiler_params=pltpu.CompilerParams(
            vmem_limit_bytes=VMEM_GRANT, collective_id=0, has_side_effects=True
        ),
        name="layer",
    )(counts, adjacency, features, cotangent, embed, *vectors, attend, merge, expand, reducer)


def layer_alone_part(
    counts, adjacency, features, cotangent, rows, embed, attend, merge, expand, reducer
):
    nodes, feat = features.shape
    width, spread = expand.shape
    tiles = nodes // NODES_PER_TILE
    wide = (PACK, 2, width // PACK // 2, 3 * QUAD)
    return pl.pallas_call(
        layer_alone_kernel,
        in_specs=[SMEM_SPEC] + [VMEM_SPEC] * 9,
        out_specs=[VMEM_SPEC] * 7,
        out_shape=[
            sds(cotangent.shape, F32),
            sds(features.shape, F32),
            sds((PACK, 2, 80, width), BF16),
            sds(wide, BF16),
            sds(wide, BF16),
            sds((feat, width), F32),
            sds((8, width), F32),
        ],
        scratch_shapes=layer_keep(tiles, feat, width, spread),
        compiler_params=pltpu.CompilerParams(vmem_limit_bytes=VMEM_GRANT),
        name="layer_alone",
    )(counts, adjacency, features, cotangent, rows, embed, attend, merge, expand, reducer)


def unpack_part(middle, attend, tail, features, nodes, shapes):
    return pl.pallas_call(
        unpack_kernel,
        out_shape=[sds(shape, F32) for shape in [nodes.shape, features.shape] + shapes],
        compiler_params=pltpu.CompilerParams(vmem_limit_bytes=VMEM_GRANT),
        name="unpack_shares",
    )(middle, attend, tail, features, nodes)


def gather(block):
    return lax.all_gather(block, "fsdp", axis=0, tiled=True)


def share(term):
    part = lax.psum_scatter(term.astype(BF16), "fsdp", scatter_dimension=0, tiled=True)
    return lax.psum(part.astype(F32), "grp")


def body(
    features,
    adjacency,
    counts,
    input_weight,
    first_gain,
    first_shift,
    attend_weight,
    merge_weight,
    second_gain,
    second_shift,
    expand_weight,
    reduce_weight,
    readout_weight,
    cotangent,
):
    vectors = (first_gain, first_shift, second_gain, second_shift, readout_weight)
    owners = lax.axis_size("fsdp")
    if owners % PLANE == 0 and input_weight.shape[0] == 8 and attend_weight.shape[0] == 32:
        lines = owners // PLANE
        tiles = cotangent.shape[0] // NODES_PER_TILE
        output, grad_features, *shares = layer_part(
            lines,
            counts,
            adjacency,
            features,
            cotangent.reshape(tiles, NODES_PER_TILE, cotangent.shape[1]),
            input_weight,
            vectors,
            attend_weight,
            merge_weight,
            expand_weight,
            reduce_weight,
        )
        shapes = [
            weight.shape
            for weight in (
                input_weight,
                first_gain,
                first_shift,
                attend_weight,
                merge_weight,
                second_gain,
                second_shift,
                expand_weight,
                reduce_weight,
                readout_weight,
            )
        ]
        return tuple(
            unpack_part(*shares, grad_features, output.reshape(cotangent.shape), shapes)
        )
    return body_apart(
        features,
        adjacency,
        counts,
        input_weight,
        vectors,
        attend_weight,
        merge_weight,
        expand_weight,
        reduce_weight,
        cotangent,
    )


def body_apart(
    features,
    adjacency,
    counts,
    input_weight,
    vectors,
    attend_weight,
    merge_weight,
    expand_weight,
    reduce_weight,
    cotangent,
):
    lengths = [v.shape[0] for v in vectors]
    places = [sum(lengths[:i]) for i in range(len(lengths) + 1)]
    packed = lax.all_gather(jnp.concatenate(vectors), "fsdp", axis=0, tiled=False)
    width = merge_weight.shape[1]
    full = [
        packed[:, places[i] : places[i + 1]].astype(F32).reshape(-1, width)
        for i in range(len(lengths))
    ]
    rows = jnp.concatenate(full + [jnp.zeros((2, width), F32)], axis=0)
    embed, attend, merge, expand, reducer = map(
        gather, (input_weight, attend_weight, merge_weight, expand_weight, reduce_weight)
    )
    tiles = cotangent.shape[0] // NODES_PER_TILE
    output, grad_features, terms, early, late, grad_embed, rows_grad = layer_alone_part(
        counts,
        adjacency,
        features,
        cotangent.reshape(tiles, NODES_PER_TILE, width),
        rows,
        embed,
        attend,
        merge,
        expand,
        reducer,
    )
    grad_attend = jnp.stack([early.reshape(width, 3, QUAD), late.reshape(width, 3, QUAD)], axis=2)
    grad_attend = grad_attend.reshape(width, 3 * width)
    spread = expand.shape[1]
    grad_expand = jnp.concatenate([terms[:, :, 0:16], terms[:, :, 16:32]], axis=-1)
    parts = lax.axis_size("fsdp")
    pieces = [rows_grad[i] for i in range(4)] + [rows_grad[4:6]]
    packed_grad = jnp.concatenate([piece.reshape(parts, -1) for piece in pieces], axis=1)
    packed_grad = lax.psum(
        lax.psum_scatter(packed_grad, "fsdp", scatter_dimension=0, tiled=True), "grp"
    ).reshape(-1)
    small = [packed_grad[places[i] : places[i + 1]] for i in range(len(lengths))]
    return (
        output.reshape(cotangent.shape),
        grad_features,
        share(grad_embed),
        small[0],
        small[1],
        share(grad_attend),
        share(terms[:, :, 64:80].reshape(width, width)),
        small[2],
        small[3],
        share(grad_expand.reshape(width, spread)),
        share(terms[:, :, 32:64].reshape(spread, width)),
        small[4],
    )


def solution(mesh):
    nodes = ("grp", "fsdp")
    rows = P("fsdp", None)
    vector = P("fsdp")
    in_specs = (
        P(nodes, None),
        P(nodes, None, None),
        P(nodes),
        rows,
        vector,
        vector,
        rows,
        rows,
        vector,
        vector,
        rows,
        rows,
        vector,
        P(nodes, None),
    )
    out_specs = (
        P(nodes, None),
        P(nodes, None),
        rows,
        vector,
        vector,
        rows,
        rows,
        vector,
        vector,
        rows,
        rows,
        vector,
    )
    return jax.shard_map(body, mesh=mesh, in_specs=in_specs, out_specs=out_specs, check_vma=False)
```

time: 162 us -> 125 us (0.77)
  Pallas kernels: 158 us -> 124 us
  local copies, waits for them, and re-layouts: 3.58 us -> 0 us
    pallas_call x4 -> x2, Pallas kernels: 158 us -> 124 us  [the longest x1 122 us: layer_part(): pl.pallas_call(functools.partial(layer_kernel, lines), in_specs=[SMEM_SPE...]
    unnamed x8 -> x0, local copies, waits for them, and re-layouts: 3.58 us -> none
where the time goes in v4:
time: 125 us
  Pallas kernels  124 us (99%)
    pallas_call x1, Pallas kernels, layer_part(): pl.pallas_call(functools.partial(layer_kernel, lines), in_specs=[SMEM_SPE...  122 us
    pallas_call x1, Pallas kernels, unpack_part(): pl.pallas_call(unpack_kernel, out_shape=[sds(shape, F32) for shape in [no...  2.57 us

profile of v4, /device:TPU:0, one launch (start us, length us, event | category | flops | bytes accessed | tf_op | source)
XLA Modules:
  0.0 124.9 jit_solution(7750900230459895426)
XLA Ops:
  0.6 121.5 %layer.1 = (f32[6,64,512]{2,1,0:T(8,128)}, f32[384,128]{1,0:T(8,128)}, f32[2,80,512]{2,1,0:T(8,128)}, f32[2,2,16,768]{3,2,1,0:T(8,128)}, f32[2,8,512]{2,1,0:T(8,128)}) custom-call(s32[3]{0:T(128)} %counts_ref.1, s32[3,128,128]{2,1,0:T(8,128)} %adjacency_ref.1, bf16[384,128]{1,0:T(8,128)(2,1)} %features_ref.1, f32[6,64,512]{2,1,0:T(8,128)} %bitcast.2, ...), custom_call_target="tpu_custom_call" | custom-call | tf_op jit(solution)/shard_map/layer/pallas_call | solution.py:1222
  122.2 2.6 %unpack_shares.1 = (f32[384,512]{1,0:T(8,128)}, f32[384,128]{1,0:T(8,128)}, f32[8,512]{1,0:T(8,128)}, f32[32]{0:T(128)}, f32[32]{0:T(128)}, /*index=5*/f32[32,15...) custom-call(f32[2,80,512]{2,1,0:T(8,128)} %get-tuple-element.17.midd, ...), custom_call_target="tpu_custom_call" | custom-call | tf_op jit(solution)/shard_map/unpack_shares/pallas_call | solution.py:1286

commit v5 on v4

--- a/solution.py
+++ b/solution.py
@@ -191,8 +191,8 @@
 
 
 class Gather:
-    def __init__(self, place, slots, source, send, recv, pair, halves=True):
-        self.place, self.slots, self.source = place, slots, source
+    def __init__(self, place, slots, send, recv, pair, halves):
+        self.place, self.slots = place, slots
         self.send, self.recv, self.pair_sems, self.halves = send, recv, pair, halves
 
     def slot(self, owner):
@@ -202,10 +202,9 @@
         place = self.place
         peers = [place.line_peer(d) for d in range(1, place.lines)]
         peers += [place.plane_peer(e) for e in range(1, PLANE)]
+        own = self.slot(place.owner)
         return [
-            remote(
-                self.source, self.slot(place.owner), self.send.at[i], self.recv.at[place.owner], peer
-            )
+            remote(own, own, self.send.at[i], self.recv.at[place.owner], peer)
             for i, peer in enumerate(peers)
         ]
 
@@ -324,8 +323,7 @@
         def add(line, carry):
             for spot in range(PLANE):
                 owner = line * PLANE + spot
-                both = self.terms[owner, place.core].astype(F32) + self.got[owner].astype(F32)
-                self.chip[line, spot] = both.astype(BF16)
+                self.chip[line, spot] = self.terms[owner, place.core] + self.got[owner]
             return carry
 
         lax.fori_loop(0, place.lines, add, 0)
@@ -533,10 +531,20 @@
     normed_ref[tile] = (normal * gain + shift).astype(BF16)
 
 
-def attend_tile(tile, normed_ref, attend, merge_of, triple_ref, mixed_ref, second_ref):
+def project_step(first_tile, kind, normed_ref, weight, triple_ref):
     width = normed_ref.shape[-1]
-    triple = dot(normed_ref[tile], attend).astype(BF16)
-    triple_ref[tile] = triple.reshape(triple_ref.shape[1:])
+    tiles = pl.ds(first_tile, STREAMS)
+    normed = normed_ref[tiles].reshape(STREAMS * TOKENS, width)
+    triple_ref[tiles, :, :, :, kind * width : (kind + 1) * width] = (
+        dot(normed, weight).astype(BF16).reshape(STREAMS, *triple_ref.shape[1:-1], width)
+    )
+
+
+def attend_tile(tile, normed_ref, value_weight, triple_ref, mixed_ref):
+    width = normed_ref.shape[-1]
+    triple_ref[tile, :, :, :, 2 * width :] = (
+        dot(normed_ref[tile], value_weight).astype(BF16).reshape(*triple_ref.shape[1:-1], width)
+    )
     places = [(tile, g, first) for g in range(GROUPS) for first in range(0, width, QUAD)]
     keys = [block_of(triple_ref, t, g, width + first) for t, g, first in places]
     queries = [quad_stack(block_of(triple_ref, *place)) for place in places]
@@ -546,7 +554,6 @@
     blocks = [queries_from(p, v) for p, v in zip(probs, values)]
     for place, block in zip(places, blocks):
         put_block(mixed_ref, *place, block)
-    second_ref[tile] += dot(tokens_of(mixed_ref, tile), merge_of())
 
 
 def middle_step(
@@ -577,10 +584,11 @@
         before = dot(inner, expand)
         yield
         square = before * before
-        curve = jnp.tanh(GELU_A * before * (1.0 + GELU_B * square))
-        after = (0.5 * before * (1.0 + curve)).astype(BF16)
-        slope = 0.5 * (1.0 + curve) + (0.5 * GELU_A) * before * (1.0 - curve * curve) * (
-            1.0 + (3.0 * GELU_B) * square
+        gate = 1.0 / (1.0 + jnp.exp(before * (square * (-2.0 * GELU_A * GELU_B) - 2.0 * GELU_A)))
+        gated = before * gate
+        after = gated.astype(BF16)
+        slope = gate + (gated - gated * gate) * (
+            square * (6.0 * GELU_A * GELU_B) + 2.0 * GELU_A
         )
         yield
         third = second + dot(after, reducer)
@@ -702,7 +710,7 @@
     gain,
     rows_keep,
     grad_embed_ref,
-    grad_stacked_ref,
+    normed_ref,
 ):
     def stream(part):
         tile = first_tile + part
@@ -722,7 +730,7 @@
         grad_hidden = grad_hidden.astype(BF16)
         yield
         grad_embed_ref[...] += dot_lead(stacked, grad_hidden)
-        grad_stacked_ref[tile] = dot_last(grad_hidden, embed).reshape(grad_stacked_ref.shape[1:])
+        normed_ref[tile] = grad_hidden
 
     interleave([stream(part) for part in range(STREAMS)])
 
@@ -747,7 +755,9 @@
     cotangent_ref,
     rows_ref,
     embed_ref,
-    attend_ref,
+    query_ref,
+    key_ref,
+    value_ref,
     merge_ref,
     expand_ref,
     reduce_ref,
@@ -785,25 +795,31 @@
         transfers.beside_embed(tile, tiles)
 
     loop(tiles, embed_step)
-    transfers.before_attention()
+    for kind, weight_ref in enumerate((query_ref, key_ref)):
+        transfers.before_projection(kind)
+
+        def project(pair, kind=kind, weight_ref=weight_ref):
+            weight = weight_ref[...].reshape(width, width)
+            project_step(pair * STREAMS, kind, normed_ref, weight, triple_ref)
+            transfers.beside_projection(kind, pair)
+
+        loop(pairs, project)
+    transfers.before_projection(2)
 
     def attend_step(tile):
-        def merge_of():
-            transfers.before_merge(tile)
-            return merge_ref[...].reshape(width, width)
-
-        attend_tile(
-            tile,
-            normed_ref,
-            attend_ref[...].reshape(width, 3 * width),
-            merge_of,
-            triple_ref,
-            mixed_ref,
-            second_ref,
-        )
+        attend_tile(tile, normed_ref, value_ref[...].reshape(width, width), triple_ref, mixed_ref)
         transfers.beside_attention(tile, tiles)
 
     loop(tiles, attend_step)
+    transfers.before_merge()
+
+    def merge_step(pair):
+        mixed = mixed_ref[pl.ds(pair * STREAMS, STREAMS)].reshape(STREAMS * TOKENS, width)
+        second_ref[pl.ds(pair * STREAMS, STREAMS)] += dot(
+            mixed, merge_ref[...].reshape(width, width)
+        ).reshape(STREAMS, TOKENS, width)
+
+    loop(pairs, merge_step)
     transfers.before_middle()
     for ref in (rows_keep, grad_merge_ref, grad_expand_ref, grad_reduce_ref, grad_embed_ref):
         ref[...] = jnp.zeros_like(ref)
@@ -856,17 +872,27 @@
             stacked_ref,
             second_ref,
             triple_ref,
-            attend_ref[...].reshape(width, 3 * width),
+            jnp.concatenate(
+                [ref[...].reshape(width, width) for ref in (query_ref, key_ref, value_ref)], axis=1
+            ),
             embed_ref[...],
             rows_ref[0:1],
             rows_keep,
             grad_embed_ref,
-            grad_stacked_ref,
+            normed_ref,
         )
         transfers.beside_embed_back(pair, pairs)
 
     loop(pairs, embed_back)
     transfers.after_embed_back()
+
+    def stacked_back(pair):
+        grad_hidden = normed_ref[pl.ds(pair * STREAMS, STREAMS)].reshape(STREAMS * TOKENS, width)
+        grad_stacked_ref[pl.ds(pair * STREAMS, STREAMS)] = dot_last(
+            grad_hidden, embed_ref[...]
+        ).reshape(STREAMS, *grad_stacked_ref.shape[1:])
+
+    loop(pairs, stacked_back)
     hop_back(
         counts_ref,
         adjacency_ref,
@@ -880,55 +906,69 @@
 class Transfers:
     def __init__(self, place, gathers, scatters, unpack_head, pack_tail, publish):
         self.place = place
-        self.lead, self.attend, self.merge, self.expand, self.reducer = gathers
+        self.lead, *self.attend = gathers[:4]
+        self.merge, self.expand, self.reducer = gathers[4:]
         self.middle, self.early, self.late, self.tail = scatters
         self.unpack_head, self.pack_tail, self.publish = unpack_head, pack_tail, publish
 
     def head(self):
+        queries, keys, values = self.attend
         self.place.greeted()
         self.lead.start()
-        self.attend.start_line()
+        for part in self.attend:
+            part.start_line()
         self.lead.forward()
-        self.attend.start_plane()
-        self.attend.forward()
+        queries.start_plane()
+        queries.forward()
+        keys.start_plane()
         self.lead.finish()
+        keys.forward()
         self.unpack_head()
+        values.start_plane()
+        values.forward()
+        self.merge.start()
+        self.expand.start()
 
     def beside_embed(self, tile, tiles):
-        @pl.when(tile == 0)
+        @pl.when(tile == 2)
         def _():
-            self.merge.start()
-
-        @pl.when(tile == tiles - 3)
+            self.attend[0].finish()
+            self.attend[0].pair().start()
+
+        @pl.when(tile == tiles - 1)
         def _():
             self.merge.forward()
 
-        @pl.when(tile == tiles - 2)
+    def before_projection(self, kind):
+        self.attend[kind].pair().wait()
+
+    def beside_projection(self, kind, pair):
+        @pl.when(pair == 0)
         def _():
-            self.attend.finish()
-            self.attend.pair().start()
-            self.expand.start()
-            self.reducer.start()
-
-    def before_attention(self):
-        self.merge.finish()
-        self.merge.pair().start()
-        self.attend.pair().wait()
-
-    def before_merge(self, tile):
-        @pl.when(tile == 0)
+            self.attend[kind + 1].finish()
+            self.attend[kind + 1].pair().start()
+            if kind == 0:
+                self.reducer.start()
+
+        @pl.when(pair == 1)
         def _():
-            self.merge.pair().wait()
-            self.expand.forward()
-            self.reducer.forward()
+            (self.expand, self.reducer)[kind].forward()
 
     def beside_attention(self, tile, tiles):
+        @pl.when(tile == tiles // 2)
+        def _():
+            self.merge.finish()
+            self.merge.pair().start()
+
         @pl.when(tile == tiles - 2)
         def _():
             self.expand.finish()
             self.expand.pair().start()
-            self.reducer.finish()
-            self.reducer.pair().start()
+
+    def before_merge(self):
+        self.merge.pair().wait()
+        self.reducer.finish()
+        self.reducer.pair().start()
 
     def before_middle(self):
         self.expand.pair().wait()
@@ -1014,26 +1054,18 @@
 ):
     keep = scratch[0:10]
     embed_ref, rows_ref, small_keep, head_slots = scratch[10:14]
-    attend_slots, merge_slots, expand_slots, reduce_slots = scratch[14:18]
-    grad_embed_ref, rows_keep = scratch[18:20]
-    middle_refs, early_refs, late_refs = scratch[20:27], scratch[27:34], scratch[34:41]
-    tail_refs = scratch[41:47]
-    send, recv, pair, scatter_sems = scratch[47:51]
+    attend_slots = scratch[14:17]
+    merge_slots, expand_slots, reduce_slots = scratch[17:20]
+    grad_embed_ref, rows_keep = scratch[20:22]
+    middle_refs, early_refs, late_refs = scratch[22:29], scratch[29:36], scratch[36:43]
+    tail_refs = scratch[43:49]
+    send, recv, pair, scatter_sems = scratch[49:53]
     owners = head_slots.shape[0]
     width = embed_ref.shape[-1]
     half_width = width // 2
     place = Place(lines)
     core, owner = place.core, place.owner
     place.greet()
-
-    def half_of(shard):
-        rows = shard.shape[0] // 2
-        return shard.at[pl.ds(pl.multiple_of(core * rows, rows), rows)]
-
-    def gather(index, slots, source, halves=True):
-        return Gather(
-            place, slots, source, send.at[index], recv.at[index], pair.at[index], halves
-        )
 
     small_keep[...] = jnp.zeros_like(small_keep)
     for index, vector in enumerate((vector_a, vector_b, vector_c, vector_d, vector_e)):
@@ -1048,17 +1080,20 @@
         axis=0,
     )
     head_slots[owner] = packed.astype(BF16)
-    matrices = (
-        (attend_slots, attend_shard),
-        (merge_slots, merge_shard),
-        (expand_slots, expand_shard),
-        (reduce_slots, reduce_shard),
-    )
-    for slots, shard in matrices:
-        slots[owner, core] = half_of(shard)[...]
-    gathers = [gather(0, head_slots, head_slots.at[owner], False)]
-    gathers += [
-        gather(1 + index, slots, half_of(shard)) for index, (slots, shard) in enumerate(matrices)
+
+    def half_of(shard):
+        rows = shard.shape[0] // 2
+        return shard[pl.ds(pl.multiple_of(core * rows, rows), rows)]
+
+    whole_attend = half_of(attend_shard)
+    for kind, slots in enumerate(attend_slots):
+        slots[owner, core] = whole_attend[:, kind * width : (kind + 1) * width]
+    matrices = (merge_slots, expand_slots, reduce_slots)
+    for slots, shard in zip(matrices, (merge_shard, expand_shard, reduce_shard)):
+        slots[owner, core] = half_of(shard)
+    gathers = [
+        Gather(place, slots, send.at[index], recv.at[index], pair.at[index], index > 0)
+        for index, slots in enumerate((head_slots, *attend_slots, *matrices))
     ]
     middle = Scatter(place, *middle_refs, scatter_sems.at[0])
     early = Scatter(place, *early_refs, scatter_sems.at[1])
@@ -1095,7 +1130,7 @@
         cotangent_ref,
         rows_ref,
         embed_ref,
-        attend_slots,
+        *attend_slots,
         merge_slots,
         expand_slots,
         reduce_slots,
@@ -1112,7 +1147,7 @@
 
 
 def layer_alone_kernel(*refs):
-    layer_phases(*refs[:17], refs[17:], Silent())
+    layer_phases(*refs[:19], refs[19:], Silent())
 
 
 def unpack_kernel(
@@ -1198,8 +1233,8 @@
     wide = (width // owners // 2, 3 * QUAD)
     copies = lines + PLANE - 2 + (lines - 1) * (PLANE - 1)
 
-    def slots(shard):
-        return pltpu.VMEM((owners, 2, shard.shape[0] // 2, shard.shape[1]), BF16)
+    def slots(rows, columns):
+        return pltpu.VMEM((owners, 2, rows // 2, columns), BF16)
 
     def buffers(shape):
         return [
@@ -1231,7 +1266,8 @@
             pltpu.VMEM((8, 128), F32),
             pltpu.VMEM((owners, 16, width // 2 + 128), BF16),
         ]
-        + [slots(shard) for shard in (attend, merge, expand, reducer)]
+        + [slots(attend.shape[0], width)] * 3
+        + [slots(*shard.shape) for shard in (merge, expand, reducer)]
         + [pltpu.VMEM((feat, width), F32), pltpu.VMEM((8, width), F32)]
         + buffers(rest)
         + buffers(wide) * 2
@@ -1244,9 +1280,9 @@
             pltpu.VMEM((2, 8, width), F32),
         ]
         + [
-            pltpu.SemaphoreType.DMA((5, copies)),
-            pltpu.SemaphoreType.DMA((5, owners)),
-            pltpu.SemaphoreType.DMA((5, 2)),
+            pltpu.SemaphoreType.DMA((7, copies)),
+            pltpu.SemaphoreType.DMA((7, owners)),
+            pltpu.SemaphoreType.DMA((7, 2)),
             pltpu.SemaphoreType.DMA((4, 2, PLANE + lines)),
         ],
         compiler_params=pltpu.CompilerParams(
@@ -1265,7 +1301,7 @@
     wide = (PACK, 2, width // PACK // 2, 3 * QUAD)
     return pl.pallas_call(
         layer_alone_kernel,
-        in_specs=[SMEM_SPEC] + [VMEM_SPEC] * 9,
+        in_specs=[SMEM_SPEC] + [VMEM_SPEC] * 11,
         out_specs=[VMEM_SPEC] * 7,
         out_shape=[
             sds(cotangent.shape, F32),
@@ -1279,7 +1315,20 @@
         scratch_shapes=layer_keep(tiles, feat, width, spread),
         compiler_params=pltpu.CompilerParams(vmem_limit_bytes=VMEM_GRANT),
         name="layer_alone",
-    )(counts, adjacency, features, cotangent, rows, embed, attend, merge, expand, reducer)
+    )(
+        counts,
+        adjacency,
+        features,
+        cotangent,
+        rows,
+        embed,
+        attend[:, :width],
+        attend[:, width : 2 * width],
+        attend[:, 2 * width :],
+        merge,
+        expand,
+        reducer,
+    )
 
 
 def unpack_part(middle, attend, tail, features, nodes, shapes):

time: 125 us -> 119 us (0.952)
  Pallas kernels: 124 us -> 118 us
    pallas_call x1, Pallas kernels: 122 us -> 116 us  [layer_part(): pl.pallas_call(functools.partial(layer_kernel, lines), in_specs=[SMEM_SPE...]
where the time goes in v5:
time: 119 us
  Pallas kernels  118 us (99%)
    pallas_call x1, Pallas kernels, layer_part(): pl.pallas_call(functools.partial(layer_kernel, lines), in_specs=[SMEM_SPE...  116 us
    pallas_call x1, Pallas kernels, unpack_part(): pl.pallas_call(unpack_kernel, out_shape=[sds(shape, F32) for shape in [no...  2.57 us

profile of v5, /device:TPU:0, one launch (start us, length us, event | category | flops | bytes accessed | tf_op | source)
XLA Modules:
  0.0 119.2 jit_solution(6719222845851380788)
XLA Ops:
  0.6 115.9 %layer.1 = (f32[6,64,512]{2,1,0:T(8,128)}, f32[384,128]{1,0:T(8,128)}, f32[2,80,512]{2,1,0:T(8,128)}, f32[2,2,16,768]{3,2,1,0:T(8,128)}, f32[2,8,512]{2,1,0:T(8,128)}) custom-call(s32[3]{0:T(128)} %counts_ref.1, s32[3,128,128]{2,1,0:T(8,128)} %adjacency_ref.1, bf16[384,128]{1,0:T(8,128)(2,1)} %features_ref.1, f32[6,64,512]{2,1,0:T(8,128)} %bitcast.2, ...), custom_call_target="tpu_custom_call" | custom-call | tf_op jit(solution)/shard_map/layer/pallas_call | solution.py:1257
  116.5 2.6 %unpack_shares.1 = (f32[384,512]{1,0:T(8,128)}, f32[384,128]{1,0:T(8,128)}, f32[8,512]{1,0:T(8,128)}, f32[32]{0:T(128)}, f32[32]{0:T(128)}, /*index=5*/f32[32,15...) custom-call(f32[2,80,512]{2,1,0:T(8,128)} %get-tuple-element.17.midd, ...), custom_call_target="tpu_custom_call" | custom-call | tf_op jit(solution)/shard_map/unpack_shares/pallas_call | solution.py:1335

commit v6 on v5

--- a/solution.py
+++ b/solution.py
@@ -26,6 +26,7 @@
 BF16 = jnp.bfloat16
 GELU_A = 0.7978845608028654
 GELU_B = 0.044715
+LOG2_E = 1.4426950408889634
 PLANE = 4
 PACK = 16
 MESH = pl.DeviceIdType.MESH
@@ -97,7 +98,7 @@
     tokens, columns = scores.shape
     scores = scores.reshape(HOP_TOKENS, GROUP, columns)
     top = jnp.max(scores, axis=0)
-    power = jnp.exp((scores - top[None]) * HEAD ** (-0.5))
+    power = jnp.exp2((scores - top[None]) * (HEAD ** (-0.5) * LOG2_E))
     row = lax.broadcasted_iota(jnp.int32, (GROUP, columns), 0)
     col = lax.broadcasted_iota(jnp.int32, (GROUP, columns), 1) % GROUP
     share = jnp.where(row == col, 1.0 / jnp.sum(power, axis=0), 0.0)
@@ -160,6 +161,12 @@
     def plane_peer(self, ahead):
         return (self.core, self.line * PLANE + self.spot_turn(ahead))
 
+    def side_peer(self):
+        return (self.core, self.owner + 1 - 2 * lax.rem(self.spot, 2))
+
+    def side_spot(self):
+        return self.spot + 1 - 2 * lax.rem(self.spot, 2)
+
     def sibling(self):
         return (1 - self.core, self.owner)
 
@@ -191,78 +198,90 @@
 
 
 class Gather:
-    def __init__(self, place, slots, send, recv, pair, halves):
-        self.place, self.slots = place, slots
-        self.send, self.recv, self.pair_sems, self.halves = send, recv, pair, halves
-
-    def slot(self, owner):
-        return self.slots.at[owner, self.place.core] if self.halves else self.slots.at[owner]
-
-    def own_copies(self):
+    def __init__(self, place, slots, send, recv, halves):
+        self.place, self.slots, self.send, self.recv = place, slots, send, recv
+        self.halves = halves
+
+    def slot(self, line, spot):
+        if self.halves:
+            return self.slots.at[line, spot, self.place.core]
+        return self.slots.at[line, spot]
+
+    def line_copies(self):
         place = self.place
-        peers = [place.line_peer(d) for d in range(1, place.lines)]
-        peers += [place.plane_peer(e) for e in range(1, PLANE)]
-        own = self.slot(place.owner)
+        own = self.slot(place.line, place.spot)
         return [
-            remote(own, own, self.send.at[i], self.recv.at[place.owner], peer)
-            for i, peer in enumerate(peers)
+            remote(own, own, self.send.at[d], self.recv.at[d], place.line_peer(d))
+            for d in range(1, place.lines)
         ]
 
-    def onward(self, d):
+    def plane_copies(self):
         place = self.place
-        owner = place.line_turn(-d) * PLANE + place.spot
-        first = place.lines + PLANE - 2 + (d - 1) * (PLANE - 1)
+        line = self.slot(slice(None), place.spot)
+        first = place.lines - 1
         return [
-            remote(
-                self.slot(owner),
-                self.slot(owner),
-                self.send.at[first + e - 1],
-                self.recv.at[owner],
-                place.plane_peer(e),
-            )
+            remote(line, line, self.send.at[first + e], self.recv.at[first + e], place.plane_peer(e))
             for e in range(1, PLANE)
         ]
 
-    def start_line(self):
-        for copy in self.own_copies()[: self.place.lines - 1]:
+    def start(self):
+        for copy in self.line_copies():
             copy.start()
 
-    def start_plane(self):
-        for copy in self.own_copies()[self.place.lines - 1 :]:
+    def forward(self):
+        for copy in self.line_copies():
+            copy.wait()
+        for copy in self.plane_copies():
             copy.start()
 
-    def start(self):
-        self.start_line()
-        self.start_plane()
+    def finish(self):
+        for copy in self.plane_copies():
+            copy.wait()
+
+    def pair(self):
+        half = self.slots.at[:, :, self.place.core]
+        return remote(half, half, self.send.at[0], self.recv.at[0], self.place.sibling())
+
+
+class CrossGather(Gather):
+    def step_copies(self):
+        place = self.place
+        line = self.slot(slice(None), place.spot)
+        first = place.lines
+        return [
+            remote(line, line, self.send.at[first + k], self.recv.at[first + k], peer)
+            for k, peer in enumerate((place.side_peer(), place.plane_peer(2)))
+        ]
+
+    def cross_copies(self):
+        place = self.place
+        first = place.lines + 2
+        half = self.slots.shape[-1] // 2
+        copies = []
+        for k, (spot, peer) in enumerate(
+            ((place.side_spot(), place.plane_peer(2)), (place.spot_turn(2), place.side_peer()))
+        ):
+            part = self.slots.at[:, spot, place.core, :, k * half : (k + 1) * half]
+            copies.append(
+                remote(part, part, self.send.at[first + k], self.recv.at[first + k], peer)
+            )
+        return copies
 
     def forward(self):
-        for d in range(1, self.place.lines):
-            copies = self.onward(d)
-            copies[0].wait_recv()
-            for copy in copies:
-                copy.start()
+        for copy in self.line_copies():
+            copy.wait()
+        for copy in self.step_copies():
+            copy.start()
+
+    def cross(self):
+        for copy in self.step_copies():
+            copy.wait()
+        for copy in self.cross_copies():
+            copy.start()
 
     def finish(self):
-        place = self.place
-        for d in range(place.lines):
-            for e in range(1, PLANE):
-                owner = place.line_turn(d) * PLANE + place.spot_turn(-e)
-                remote(
-                    self.slot(owner),
-                    self.slot(owner),
-                    self.send.at[0],
-                    self.recv.at[owner],
-                    place.plane_peer(e),
-                ).wait_recv()
-        for copy in self.own_copies():
-            copy.wait_send()
-        for d in range(1, place.lines):
-            for copy in self.onward(d):
-                copy.wait_send()
-
-    def pair(self):
-        half = self.slots.at[:, self.place.core]
-        return remote(half, half, self.pair_sems.at[0], self.pair_sems.at[1], self.place.sibling())
+        for copy in self.cross_copies():
+            copy.wait()
 
 
 class Scatter:
@@ -584,7 +603,7 @@
         before = dot(inner, expand)
         yield
         square = before * before
-        gate = 1.0 / (1.0 + jnp.exp(before * (square * (-2.0 * GELU_A * GELU_B) - 2.0 * GELU_A)))
+        gate = 0.5 + 0.5 * jnp.tanh(before * (square * (GELU_A * GELU_B) + GELU_A))
         gated = before * gate
         after = gated.astype(BF16)
         slope = gate + (gated - gated * gate) * (
@@ -785,8 +804,16 @@
     ) = keep
     tiles, _, width = second_ref.shape
     pairs = tiles // STREAMS
+    sums = (grad_merge_ref, grad_expand_ref, grad_reduce_ref)
+
+    def clear():
+        for ref in (rows_keep, grad_embed_ref, *sums):
+            ref[...] = jnp.zeros_like(ref)
+
+    transfers.lead()
     hop_states(counts_ref, adjacency_ref, features_ref, stacked_ref)
-    transfers.head()
+    if not transfers.head(clear):
+        clear()
 
     def embed_step(tile):
         embed_tile(
@@ -821,8 +848,6 @@
 
     loop(pairs, merge_step)
     transfers.before_middle()
-    for ref in (rows_keep, grad_merge_ref, grad_expand_ref, grad_reduce_ref, grad_embed_ref):
-        ref[...] = jnp.zeros_like(ref)
     spread = grad_expand_ref.shape[1]
 
     def feed_step(pair):
@@ -904,30 +929,39 @@
 
 
 class Transfers:
-    def __init__(self, place, gathers, scatters, unpack_head, pack_tail, publish):
+    def __init__(self, place, gathers, scatters, copies, fill, unpack_head, pack_tail, publish):
         self.place = place
-        self.lead, *self.attend = gathers[:4]
+        self.first, *self.attend = gathers[:4]
         self.merge, self.expand, self.reducer = gathers[4:]
         self.middle, self.early, self.late, self.tail = scatters
+        self.inputs, self.cotangent, self.output = copies[:2], copies[2], copies[3]
+        self.fill = fill
         self.unpack_head, self.pack_tail, self.publish = unpack_head, pack_tail, publish
 
-    def head(self):
+    def lead(self):
+        for copy in (*self.inputs, self.cotangent):
+            copy.start()
+        self.place.greeted()
+        self.first.start()
+        self.fill()
+        for part in self.attend[:2]:
+            part.start()
+        for copy in self.inputs:
+            copy.wait()
+
+    def head(self, clear):
         queries, keys, values = self.attend
-        self.place.greeted()
-        self.lead.start()
-        for part in self.attend:
-            part.start_line()
-        self.lead.forward()
-        queries.start_plane()
+        self.first.forward()
+        values.start()
+        self.merge.start()
         queries.forward()
-        keys.start_plane()
-        self.lead.finish()
+        clear()
+        self.first.finish()
         keys.forward()
         self.unpack_head()
-        values.start_plane()
         values.forward()
-        self.merge.start()
         self.expand.start()
+        return True
 
     def beside_embed(self, tile, tiles):
         @pl.when(tile == 2)
@@ -935,6 +969,10 @@
             self.attend[0].finish()
             self.attend[0].pair().start()
 
+        @pl.when(tile == tiles - 2)
+        def _():
+            self.attend[1].cross()
+
         @pl.when(tile == tiles - 1)
         def _():
             self.merge.forward()
@@ -945,20 +983,30 @@
     def beside_projection(self, kind, pair):
         @pl.when(pair == 0)
         def _():
+            if kind == 0:
+                self.attend[2].cross()
+                self.reducer.start()
             self.attend[kind + 1].finish()
             self.attend[kind + 1].pair().start()
-            if kind == 0:
-                self.reducer.start()
 
         @pl.when(pair == 1)
         def _():
-            (self.expand, self.reducer)[kind].forward()
+            if kind == 0:
+                self.expand.forward()
+            else:
+                self.merge.cross()
+                self.reducer.forward()
 
     def beside_attention(self, tile, tiles):
-        @pl.when(tile == tiles // 2)
+        @pl.when(tile == 1)
         def _():
+            self.expand.cross()
             self.merge.finish()
             self.merge.pair().start()
+
+        @pl.when(tile == tiles - 3)
+        def _():
+            self.reducer.cross()
 
         @pl.when(tile == tiles - 2)
         def _():
@@ -973,9 +1021,11 @@
     def before_middle(self):
         self.expand.pair().wait()
         self.reducer.pair().wait()
+        self.cotangent.wait()
 
     def after_middle(self):
         self.middle.begin()
+        self.output.start()
 
     def beside_backward(self, quad, pair, pairs):
         if quad == 0:
@@ -1026,15 +1076,16 @@
         self.late.to_sibling()
         tail = self.tail.end()
         self.late.end()
+        self.output.wait()
         self.publish(tail)
 
 
 def layer_kernel(
     lines,
     counts_ref,
-    adjacency_ref,
-    features_ref,
-    cotangent_ref,
+    adjacency_in,
+    features_in,
+    cotangent_in,
     embed_shard,
     vector_a,
     vector_b,
@@ -1045,11 +1096,16 @@
     merge_shard,
     expand_shard,
     reduce_shard,
-    output_ref,
+    output_out,
     grad_features_ref,
     middle_share_ref,
     attend_share_ref,
     tail_share_ref,
+    adjacency_ref,
+    features_ref,
+    cotangent_ref,
+    output_ref,
+    local,
     *scratch,
 ):
     keep = scratch[0:10]
@@ -1059,12 +1115,12 @@
     grad_embed_ref, rows_keep = scratch[20:22]
     middle_refs, early_refs, late_refs = scratch[22:29], scratch[29:36], scratch[36:43]
     tail_refs = scratch[43:49]
-    send, recv, pair, scatter_sems = scratch[49:53]
-    owners = head_slots.shape[0]
+    send, recv, scatter_sems = scratch[49:52]
+    owners = lines * PLANE
     width = embed_ref.shape[-1]
     half_width = width // 2
     place = Place(lines)
-    core, owner = place.core, place.owner
+    core, line, spot = place.core, place.line, place.spot
     place.greet()
 
     small_keep[...] = jnp.zeros_like(small_keep)
@@ -1079,20 +1135,36 @@
         ],
         axis=0,
     )
-    head_slots[owner] = packed.astype(BF16)
+    head_slots[line, spot] = packed.astype(BF16)
 
     def half_of(shard):
         rows = shard.shape[0] // 2
         return shard[pl.ds(pl.multiple_of(core * rows, rows), rows)]
 
-    whole_attend = half_of(attend_shard)
-    for kind, slots in enumerate(attend_slots):
-        slots[owner, core] = whole_attend[:, kind * width : (kind + 1) * width]
     matrices = (merge_slots, expand_slots, reduce_slots)
-    for slots, shard in zip(matrices, (merge_shard, expand_shard, reduce_shard)):
-        slots[owner, core] = half_of(shard)
+
+    def fill():
+        whole_attend = half_of(attend_shard)
+        for kind, slots in enumerate(attend_slots):
+            slots[line, spot, core] = whole_attend[:, kind * width : (kind + 1) * width]
+        for slots, shard in zip(matrices, (merge_shard, expand_shard, reduce_shard)):
+            slots[line, spot, core] = half_of(shard)
+
+    copies = [
+        pltpu.make_async_copy(source, target, local.at[index])
+        for index, (source, target) in enumerate(
+            (
+                (adjacency_in, adjacency_ref),
+                (features_in, features_ref),
+                (cotangent_in, cotangent_ref),
+                (output_ref, output_out),
+            )
+        )
+    ]
     gathers = [
-        Gather(place, slots, send.at[index], recv.at[index], pair.at[index], index > 0)
+        (CrossGather if index > 1 else Gather)(
+            place, slots, send.at[index], recv.at[index], index > 0
+        )
         for index, slots in enumerate((head_slots, *attend_slots, *matrices))
     ]
     middle = Scatter(place, *middle_refs, scatter_sems.at[0])
@@ -1101,7 +1173,7 @@
     tail = TailScatter(place, *tail_refs, scatter_sems.at[3])
 
     def unpack_head():
-        whole_head = head_slots[...].astype(F32)
+        whole_head = head_slots[...].astype(F32).reshape(owners, 16, half_width + 128)
         top = whole_head[:, 0:8].reshape(owners * 8, half_width + 128)
         bottom = whole_head[:, 8:16].reshape(owners * 8, half_width + 128)
         embed_ref[:, :half_width] = top[:, :half_width].astype(BF16)
@@ -1120,8 +1192,9 @@
         attend_share_ref[1] = late.result[...]
         tail_share_ref[...] = tail_total
 
+    scatters = (middle, early, late, tail)
     transfers = Transfers(
-        place, gathers, (middle, early, late, tail), unpack_head, pack_tail, publish
+        place, gathers, scatters, copies, fill, unpack_head, pack_tail, publish
     )
     layer_phases(
         counts_ref,
@@ -1231,10 +1304,9 @@
     tiles = nodes // NODES_PER_TILE
     rest = (80, width)
     wide = (width // owners // 2, 3 * QUAD)
-    copies = lines + PLANE - 2 + (lines - 1) * (PLANE - 1)
 
     def slots(rows, columns):
-        return pltpu.VMEM((owners, 2, rows // 2, columns), BF16)
+        return pltpu.VMEM((lines, PLANE, 2, rows // 2, columns), BF16)
 
     def buffers(shape):
         return [
@@ -1256,15 +1328,22 @@
     ]
     return pl.pallas_call(
         functools.partial(layer_kernel, lines),
-        in_specs=[SMEM_SPEC] + [VMEM_SPEC] * 13,
-        out_specs=[VMEM_SPEC] * 5,
+        in_specs=[SMEM_SPEC] + [ANY_SPEC] * 3 + [VMEM_SPEC] * 10,
+        out_specs=[ANY_SPEC] + [VMEM_SPEC] * 4,
         out_shape=[sds(shape, F32) for shape in outs],
-        scratch_shapes=layer_keep(tiles, feat, width, spread)
+        scratch_shapes=[
+            pltpu.VMEM(adjacency.shape, jnp.int32),
+            pltpu.VMEM(features.shape, BF16),
+            pltpu.VMEM(cotangent.shape, F32),
+            pltpu.VMEM(cotangent.shape, F32),
+            pltpu.SemaphoreType.DMA((4,)),
+        ]
+        + layer_keep(tiles, feat, width, spread)
         + [
             pltpu.VMEM((feat, width), BF16),
             pltpu.VMEM((8, width), F32),
             pltpu.VMEM((8, 128), F32),
-            pltpu.VMEM((owners, 16, width // 2 + 128), BF16),
+            pltpu.VMEM((lines, PLANE, 16, width // 2 + 128), BF16),
         ]
         + [slots(attend.shape[0], width)] * 3
         + [slots(*shard.shape) for shard in (merge, expand, reducer)]
@@ -1280,9 +1359,8 @@
             pltpu.VMEM((2, 8, width), F32),
         ]
         + [
-            pltpu.SemaphoreType.DMA((7, copies)),
-            pltpu.SemaphoreType.DMA((7, owners)),
-            pltpu.SemaphoreType.DMA((7, 2)),
+            pltpu.SemaphoreType.DMA((7, lines + PLANE)),
+            pltpu.SemaphoreType.DMA((7, lines + PLANE)),
             pltpu.SemaphoreType.DMA((4, 2, PLANE + lines)),
         ],
         compiler_params=pltpu.CompilerParams(

time: 119 us -> 117 us (0.983)
  Pallas kernels: 118 us -> 116 us
    pallas_call x1, Pallas kernels: 116 us -> 113 us  [layer_part(): pl.pallas_call(functools.partial(layer_kernel, lines), in_specs=[SMEM_SPE...]
where the time goes in v6:
time: 117 us
  Pallas kernels  116 us (99%)
    pallas_call x1, Pallas kernels, layer_part(): pl.pallas_call(functools.partial(layer_kernel, lines), in_specs=[SMEM_SPE...  113 us
    pallas_call x1, Pallas kernels, unpack_part(): pl.pallas_call(unpack_kernel, out_shape=[sds(shape, F32) for shape in [no...  2.57 us

profile of v6, /device:TPU:0, one launch (start us, length us, event | category | flops | bytes accessed | tf_op | source)
XLA Modules:
  0.0 116.6 jit_solution(5765582711652170752)
XLA Ops:
  0.6 113.3 %layer.1 = (f32[6,64,512]{2,1,0:T(8,128)}, f32[384,128]{1,0:T(8,128)}, f32[2,80,512]{2,1,0:T(8,128)}, f32[2,2,16,768]{3,2,1,0:T(8,128)}, f32[2,8,512]{2,1,0:T(8,128)}) custom-call(s32[3]{0:T(128)} %counts_ref.1, s32[3,128,128]{2,1,0:T(8,128)} %adjacency_in.1, bf16[384,128]{1,0:T(8,128)(2,1)} %features_in.1, f32[6,64,512]{2,1,0:T(8,128)} %bitcast.2, ...), custom_call_target="tpu_custom_call" | custom-call | tf_op jit(solution)/shard_map/layer/pallas_call | solution.py:1329
  113.9 2.6 %unpack_shares.1 = (f32[384,512]{1,0:T(8,128)}, f32[384,128]{1,0:T(8,128)}, f32[8,512]{1,0:T(8,128)}, f32[32]{0:T(128)}, f32[32]{0:T(128)}, /*index=5*/f32[32,15...) custom-call(f32[2,80,512]{2,1,0:T(8,128)} %get-tuple-element.17.midd, ...), custom_call_target="tpu_custom_call" | custom-call | tf_op jit(solution)/shard_map/unpack_shares/pallas_call | solution.py:1413

commit v7 on v6

--- a/solution.py
+++ b/solution.py
@@ -94,11 +94,11 @@
     return (weighted - shaped * total[None]).reshape(tokens, columns).astype(BF16)
 
 
-def quad_probs(scores):
+def quad_probs(scores, scale):
     tokens, columns = scores.shape
     scores = scores.reshape(HOP_TOKENS, GROUP, columns)
     top = jnp.max(scores, axis=0)
-    power = jnp.exp2((scores - top[None]) * (HEAD ** (-0.5) * LOG2_E))
+    power = jnp.exp2((scores - top[None]) * (scale * LOG2_E))
     row = lax.broadcasted_iota(jnp.int32, (GROUP, columns), 0)
     col = lax.broadcasted_iota(jnp.int32, (GROUP, columns), 1) % GROUP
     share = jnp.where(row == col, 1.0 / jnp.sum(power, axis=0), 0.0)
@@ -423,9 +423,10 @@
         place = self.place
         for copy in self.plane():
             copy.wait()
-        total = self.own[place.spot]
+        total = self.own[place.spot].astype(F32)
         for e in range(PLANE - 1):
-            total = total + self.plane_got[e]
+            total = total + self.plane_got[e].astype(F32)
+        total = total.astype(BF16)
         for line in range(place.lines):
             self.line_out[line, 0] = total[line]
             self.line_out[line, 1] = total[place.lines]
@@ -436,9 +437,9 @@
         place = self.place
         for copy in self.line():
             copy.wait()
-        total = self.line_out[place.line]
+        total = self.line_out[place.line].astype(F32)
         for d in range(place.lines - 1):
-            total = total + self.line_got[d]
+            total = total + self.line_got[d].astype(F32)
         self.mine[...] = total
         self.last().start()
 
@@ -500,6 +501,8 @@
 
 def hop_back(counts_ref, adjacency_ref, grad_stacked_ref, grad_features_ref, between):
     clusters, slots = adjacency_ref.shape[:2]
+    feat = grad_features_ref.shape[1]
+    rows = TOKENS // HOP_PAIRS
     per_cluster = slots // NODES_PER_TILE
     links = []
     states = []
@@ -507,9 +510,11 @@
     def hop_grad(cluster, index):
         return jnp.concatenate(
             [
-                grad_stacked_ref[cluster * per_cluster + p, index // 2, :, index % 2].reshape(
-                    NODES_PER_TILE, grad_stacked_ref.shape[-1]
-                )
+                grad_stacked_ref[
+                    cluster * per_cluster + p, index // 2 * rows : (index // 2 + 1) * rows, 0:feat
+                ]
+                .reshape(GROUPS, 2, GROUP, feat)[:, index % 2]
+                .reshape(NODES_PER_TILE, feat)
                 for p in range(per_cluster)
             ],
             axis=0,
@@ -559,7 +564,7 @@
     )
 
 
-def attend_tile(tile, normed_ref, value_weight, triple_ref, mixed_ref):
+def attend_tile(tile, normed_ref, value_weight, triple_ref, mixed_ref, probs_ref):
     width = normed_ref.shape[-1]
     triple_ref[tile, :, :, :, 2 * width :] = (
         dot(normed_ref[tile], value_weight).astype(BF16).reshape(*triple_ref.shape[1:-1], width)
@@ -568,11 +573,12 @@
     keys = [block_of(triple_ref, t, g, width + first) for t, g, first in places]
     queries = [quad_stack(block_of(triple_ref, *place)) for place in places]
     scores = [dot_last(k, q) for k, q in zip(keys, queries)]
-    probs = [quad_probs(score).astype(BF16) for score in scores]
+    probs = [quad_probs(score, HEAD ** (-0.5)).astype(BF16) for score in scores]
     values = [block_of(triple_ref, t, g, 2 * width + first) for t, g, first in places]
     blocks = [queries_from(p, v) for p, v in zip(probs, values)]
-    for place, block in zip(places, blocks):
+    for place, block, prob in zip(places, blocks, probs):
         put_block(mixed_ref, *place, block)
+        probs_ref[place[2] // QUAD, tile, place[1]] = prob
 
 
 def middle_step(
@@ -680,31 +686,42 @@
     terms_ref[:, :, 64:80] = square
 
 
-def attend_back_step(quad, first_tile, triple_ref, second_ref, normed_ref, merge, grad_mixed_ref, grad_attend_ref):
+def attend_back_step(
+    quad,
+    first_tile,
+    triple_ref,
+    probs_ref,
+    second_ref,
+    normed_ref,
+    merge,
+    grad_mixed_ref,
+    grad_attend_ref,
+):
     width = normed_ref.shape[-1]
     for part in range(STREAMS):
         grad_mixed = dot_last(second_ref[first_tile + part].astype(BF16), merge).astype(BF16)
-        grad_mixed_ref[part] = grad_mixed.reshape(grad_mixed_ref.shape[1:])
+        grad_mixed_ref[part, :, :, :, 0:QUAD] = grad_mixed.reshape(
+            *grad_mixed_ref.shape[1:-1], QUAD
+        )
     places = [(part, group) for part in range(STREAMS) for group in range(GROUPS)]
-    scale = HEAD ** (-0.5)
+    scale = jnp.asarray(HEAD ** (-0.5), BF16)
     starts = [kind * width + quad * QUAD for kind in range(3)]
 
     def read(kind):
         return [block_of(triple_ref, first_tile + p, g, starts[kind]) for p, g in places]
 
     keys = read(1)
-    queries = [quad_stack(block) for block in read(0)]
-    scores = [dot_last(k, q) for k, q in zip(keys, queries)]
+    queries = [quad_stack(block * scale) for block in read(0)]
+    probs = [probs_ref[quad, first_tile + part, group] for part, group in places]
     values = read(2)
     out_grads = [quad_stack(block_of(grad_mixed_ref, p, g, 0)) for p, g in places]
     grad_probs = [dot_last(v, o) for v, o in zip(values, out_grads)]
-    probs = [quad_probs(score) for score in scores]
-    grad_scores = [grad_softmax(p, g) for p, g in zip(probs, grad_probs)]
-    grad_values = [dot(p.astype(BF16), o) for p, o in zip(probs, out_grads)]
+    grad_scores = [grad_softmax(p.astype(F32), g) for p, g in zip(probs, grad_probs)]
+    grad_values = [dot(p, o) for p, o in zip(probs, out_grads)]
     grad_keys = [dot(s, q) for s, q in zip(grad_scores, queries)]
-    grad_queries = [queries_from(s, k) for s, k in zip(grad_scores, keys)]
+    grad_queries = [queries_from(s, k * scale) for s, k in zip(grad_scores, keys)]
     for (part, group), a, b, c in zip(places, grad_queries, grad_keys, grad_values):
-        for start, block in zip(starts, (a * scale, b * scale, c)):
+        for start, block in zip(starts, (a, b, c)):
             put_block(triple_ref, first_tile + part, group, start, block)
     tiles = pl.ds(first_tile, STREAMS)
     grads = jnp.concatenate(
@@ -796,11 +813,10 @@
         normed_ref,
         triple_ref,
         mixed_ref,
-        grad_mixed_ref,
         grad_merge_ref,
         grad_expand_ref,
         grad_reduce_ref,
-        grad_stacked_ref,
+        probs_ref,
     ) = keep
     tiles, _, width = second_ref.shape
     pairs = tiles // STREAMS
@@ -834,7 +850,14 @@
     transfers.before_projection(2)
 
     def attend_step(tile):
-        attend_tile(tile, normed_ref, value_ref[...].reshape(width, width), triple_ref, mixed_ref)
+        attend_tile(
+            tile,
+            normed_ref,
+            value_ref[...].reshape(width, width),
+            triple_ref,
+            mixed_ref,
+            probs_ref,
+        )
         transfers.beside_attention(tile, tiles)
 
     loop(tiles, attend_step)
@@ -879,10 +902,11 @@
                 quad,
                 pair * STREAMS,
                 triple_ref,
+                probs_ref,
                 second_ref,
                 normed_ref,
                 merge_ref[...].reshape(width, width)[quad * QUAD : (quad + 1) * QUAD],
-                grad_mixed_ref,
+                mixed_ref,
                 grad_attend_ref,
             )
             transfers.beside_backward(quad, pair, pairs)
@@ -913,15 +937,15 @@
 
     def stacked_back(pair):
         grad_hidden = normed_ref[pl.ds(pair * STREAMS, STREAMS)].reshape(STREAMS * TOKENS, width)
-        grad_stacked_ref[pl.ds(pair * STREAMS, STREAMS)] = dot_last(
+        second_ref[pl.ds(pair * STREAMS, STREAMS), :, 0 : embed_ref.shape[0]] = dot_last(
             grad_hidden, embed_ref[...]
-        ).reshape(STREAMS, *grad_stacked_ref.shape[1:])
+        ).reshape(STREAMS, TOKENS, embed_ref.shape[0])
 
     loop(pairs, stacked_back)
     hop_back(
         counts_ref,
         adjacency_ref,
-        grad_stacked_ref,
+        second_ref,
         grad_features_ref,
         {1: transfers.beside_hops},
     )
@@ -1078,6 +1102,11 @@
         self.late.end()
         self.output.wait()
         self.publish(tail)
+
+
+def fold(block):
+    half = block.shape[-1] // 2
+    return jnp.concatenate([block[..., :half], block[..., half:]], axis=-2)
 
 
 def layer_kernel(
@@ -1108,14 +1137,15 @@
     local,
     *scratch,
 ):
-    keep = scratch[0:10]
-    embed_ref, rows_ref, small_keep, head_slots = scratch[10:14]
-    attend_slots = scratch[14:17]
-    merge_slots, expand_slots, reduce_slots = scratch[17:20]
-    grad_embed_ref, rows_keep = scratch[20:22]
-    middle_refs, early_refs, late_refs = scratch[22:29], scratch[29:36], scratch[36:43]
-    tail_refs = scratch[43:49]
-    send, recv, scatter_sems = scratch[49:52]
+    keep = scratch[0:9]
+    scratch = scratch[9:]
+    embed_ref, rows_ref, small_keep, head_slots = scratch[0:4]
+    attend_slots = scratch[4:7]
+    merge_slots, expand_slots, reduce_slots = scratch[7:10]
+    grad_embed_ref, rows_keep = scratch[10:12]
+    middle_refs, early_refs, late_refs = scratch[12:19], scratch[19:26], scratch[26:33]
+    tail_refs = scratch[33:39]
+    send, recv, scatter_sems = scratch[39:42]
     owners = lines * PLANE
     width = embed_ref.shape[-1]
     half_width = width // 2
@@ -1181,10 +1211,12 @@
         rows_ref[...] = spread_vectors(top[:, half_width:].astype(BF16), owners, width)
 
     def pack_tail():
-        own = grad_embed_ref[...].reshape(lines, PLANE, 8, width)
-        for spot in range(PLANE):
-            tail.own[spot, 0:lines] = own[:, spot]
-            tail.own[spot, lines] = rows_keep[...]
+        own = fold(grad_embed_ref[...].reshape(owners, 8, width)).astype(BF16)
+        own = own.reshape(lines, PLANE, 16, half_width)
+        rows = fold(rows_keep[...].reshape(1, 8, width))[0].astype(BF16)
+        for peer_spot in range(PLANE):
+            tail.own[peer_spot, 0:lines] = own[:, peer_spot]
+            tail.own[peer_spot, lines] = rows
 
     def publish(tail_total):
         middle_share_ref[...] = middle.result[...]
@@ -1257,8 +1289,8 @@
         grad_expand[half * 16 : half * 16 + 16, width : 2 * width] = middle_ref[half, 16:32]
         grad_reduce[half * 32 : half * 32 + 32] = middle_ref[half, 32:64]
         grad_merge[half * 16 : half * 16 + 16] = middle_ref[half, 64:80]
-    grad_embed_ref[...] = tail_ref[0]
-    rows = tail_ref[1]
+    grad_embed_ref[...] = jnp.concatenate([tail_ref[0, 0:8], tail_ref[0, 8:16]], axis=1)
+    rows = jnp.concatenate([tail_ref[1, 0:8], tail_ref[1, 8:16]], axis=1)
     length = grad_gain_one.shape[0]
     turned = pltpu.roll(rows, lax.rem(width - owner * length, width), 1)
     for index, ref in enumerate((grad_gain_one, grad_shift_one, grad_gain_two, grad_shift_two)):
@@ -1287,11 +1319,10 @@
         pltpu.VMEM((tiles, TOKENS, width), BF16),
         pltpu.VMEM((tiles, *rows, 3 * width), BF16),
         pltpu.VMEM((tiles, *rows, width), BF16),
-        pltpu.VMEM((STREAMS, *rows, QUAD), BF16),
         pltpu.VMEM((width, width), F32),
         pltpu.VMEM((width, spread), F32),
         pltpu.VMEM((spread, width), F32),
-        pltpu.VMEM((tiles, HOP_PAIRS, GROUPS, 2, GROUP, feat), F32),
+        pltpu.VMEM((width // QUAD, tiles, GROUPS, GROUP * HOP_TOKENS, QUAD), BF16),
     ]
 
 
@@ -1324,7 +1355,7 @@
         features.shape,
         (2,) + rest,
         (width // QUAD, 2) + wide,
-        (2, 8, width),
+        (2, 16, width // 2),
     ]
     return pl.pallas_call(
         functools.partial(layer_kernel, lines),
@@ -1351,12 +1382,12 @@
         + buffers(rest)
         + buffers(wide) * 2
         + [
-            pltpu.VMEM((PLANE, lines + 1, 8, width), F32),
-            pltpu.VMEM((PLANE - 1, lines + 1, 8, width), F32),
-            pltpu.VMEM((lines, 2, 8, width), F32),
-            pltpu.VMEM((lines - 1, 2, 8, width), F32),
-            pltpu.VMEM((2, 8, width), F32),
-            pltpu.VMEM((2, 8, width), F32),
+            pltpu.VMEM((PLANE, lines + 1, 16, width // 2), BF16),
+            pltpu.VMEM((PLANE - 1, lines + 1, 16, width // 2), BF16),
+            pltpu.VMEM((lines, 2, 16, width // 2), BF16),
+            pltpu.VMEM((lines - 1, 2, 16, width // 2), BF16),
+            pltpu.VMEM((2, 16, width // 2), F32),
+            pltpu.VMEM((2, 16, width // 2), F32),
         ]
         + [
             pltpu.SemaphoreType.DMA((7, lines + PLANE)),

time: 117 us -> 115 us (0.983)
  Pallas kernels: 116 us -> 114 us
    pallas_call x1, Pallas kernels: 113 us -> 111 us  [layer_part(): pl.pallas_call(functools.partial(layer_kernel, lines), in_specs=[SMEM_SPE...]
where the time goes in v7:
time: 115 us; the launch traced here: 114 us
  Pallas kernels  114 us (99%)
    pallas_call x1, Pallas kernels, layer_part(): pl.pallas_call(functools.partial(layer_kernel, lines), in_specs=[SMEM_SPE...  111 us
    pallas_call x1, Pallas kernels, unpack_part(): pl.pallas_call(unpack_kernel, out_shape=[sds(shape, F32) for shape in [no...  2.57 us

profile of v7, /device:TPU:0, one launch (start us, length us, event | category | flops | bytes accessed | tf_op | source)
XLA Modules:
  0.0 114.3 jit_solution(3539565578763598891)
XLA Ops:
  0.6 111.0 %layer.1 = (f32[6,64,512]{2,1,0:T(8,128)}, f32[384,128]{1,0:T(8,128)}, f32[2,80,512]{2,1,0:T(8,128)}, f32[2,2,16,768]{3,2,1,0:T(8,128)}, f32[2,16,256]{2,1,0:T(8,128)}) custom-call(s32[3]{0:T(128)} %counts_ref.1, s32[3,128,128]{2,1,0:T(8,128)} %adjacency_in.1, bf16[384,128]{1,0:T(8,128)(2,1)} %features_in.1, f32[6,64,512]{2,1,0:T(8,128)} %bitcast.2, ...), custom_call_target="tpu_custom_call" | custom-call | tf_op jit(solution)/shard_map/layer/pallas_call | solution.py:1360
  111.7 2.6 %unpack_shares.1 = (f32[384,512]{1,0:T(8,128)}, f32[384,128]{1,0:T(8,128)}, f32[8,512]{1,0:T(8,128)}, f32[32]{0:T(128)}, f32[32]{0:T(128)}, /*index=5*/f32[32,15...) custom-call(f32[2,80,512]{2,1,0:T(8,128)} %get-tuple-element.17.midd, ...), custom_call_target="tpu_custom_call" | custom-call | tf_op jit(solution)/shard_map/unpack_shares/pallas_call | solution.py:1444

commit v8 on v7

--- a/solution.py
+++ b/solution.py
@@ -16,7 +16,7 @@
 GROUP = 8
 STREAMS = 2
 FEEDS = 1
-SKEW = 1
+SKEW = 0
 GROUPS = NODES_PER_TILE // GROUP
 HOP_PAIRS = HOP_TOKENS // 2
 QUAD = 4 * HEAD
@@ -776,12 +776,12 @@
         return lambda *arguments: None
 
 
-def loop(count, step):
+def loop(count, step, unroll=1):
     def body(index, carry):
         step(index)
         return carry
 
-    lax.fori_loop(0, count, body, 0)
+    lax.fori_loop(0, count, body, 0, unroll=unroll)
 
 
 def layer_phases(
@@ -869,7 +869,7 @@
             mixed, merge_ref[...].reshape(width, width)
         ).reshape(STREAMS, TOKENS, width)
 
-    loop(pairs, merge_step)
+    loop(pairs, merge_step, pairs)
     transfers.before_middle()
     spread = grad_expand_ref.shape[1]
 
@@ -890,7 +890,7 @@
             grad_reduce_ref,
         )
 
-    loop(tiles // FEEDS, feed_step)
+    loop(tiles // FEEDS, feed_step, 2)
     pack_terms(terms_ref, grad_merge_ref, grad_expand_ref, grad_reduce_ref)
     transfers.after_middle()
     grad_attend_ref = grad_expand_ref
@@ -941,7 +941,7 @@
             grad_hidden, embed_ref[...]
         ).reshape(STREAMS, TOKENS, embed_ref.shape[0])
 
-    loop(pairs, stacked_back)
+    loop(pairs, stacked_back, pairs)
     hop_back(
         counts_ref,
         adjacency_ref,
@@ -1037,10 +1037,13 @@
             self.expand.finish()
             self.expand.pair().start()
 
+        @pl.when(tile == tiles - 1)
+        def _():
+            self.reducer.finish()
+            self.reducer.pair().start()
+
     def before_merge(self):
         self.merge.pair().wait()
-        self.reducer.finish()
-        self.reducer.pair().start()
 
     def before_middle(self):
         self.expand.pair().wait()

time: 115 us -> 114 us (level)
  no operation moved by 1% of the time
where the time goes in v8:
time: 114 us; the launch traced here: 113 us
  Pallas kernels  113 us (99%)
    pallas_call x1, Pallas kernels, layer_part(): pl.pallas_call(functools.partial(layer_kernel, lines), in_specs=[SMEM_SPE...  110 us
    pallas_call x1, Pallas kernels, unpack_part(): pl.pallas_call(unpack_kernel, out_shape=[sds(shape, F32) for shape in [no...  2.57 us

profile of v8, /device:TPU:0, one launch (start us, length us, event | category | flops | bytes accessed | tf_op | source)
XLA Modules:
  0.0 113.4 jit_solution(6628884260070978440)
XLA Ops:
  0.6 110.0 %layer.1 = (f32[6,64,512]{2,1,0:T(8,128)}, f32[384,128]{1,0:T(8,128)}, f32[2,80,512]{2,1,0:T(8,128)}, f32[2,2,16,768]{3,2,1,0:T(8,128)}, f32[2,16,256]{2,1,0:T(8,128)}) custom-call(s32[3]{0:T(128)} %counts_ref.1, s32[3,128,128]{2,1,0:T(8,128)} %adjacency_in.1, bf16[384,128]{1,0:T(8,128)(2,1)} %features_in.1, f32[6,64,512]{2,1,0:T(8,128)} %bitcast.2, ...), custom_call_target="tpu_custom_call" | custom-call | tf_op jit(solution)/shard_map/layer/pallas_call | solution.py:1363
  110.7 2.6 %unpack_shares.1 = (f32[384,512]{1,0:T(8,128)}, f32[384,128]{1,0:T(8,128)}, f32[8,512]{1,0:T(8,128)}, f32[32]{0:T(128)}, f32[32]{0:T(128)}, /*index=5*/f32[32,15...) custom-call(f32[2,80,512]{2,1,0:T(8,128)} %get-tuple-element.17.midd, ...), custom_call_target="tpu_custom_call" | custom-call | tf_op jit(solution)/shard_map/unpack_shares/pallas_call | solution.py:1447
